TPU v7x, 32 devices: a whole 2x2x4 slice. The times are simulated.
32 devices in a mesh: dp: 4 (over y, core), mp: 8 (over z, x).
Axes of the slice: x: 2, y: 2, z: 4, core: 2. Of those that a mesh axis runs over, the one named last changes fastest.
Arguments:
- latents: float32 [128, 256, 16], P(('dp', 'mp')), may hold values from -6 to 6
- noise_draw: float32 [128, 256, 16], P(('dp', 'mp')), may hold values from -6 to 6
- alpha_bar: float32 [128], P('dp'), may hold values from 0.05 to 0.95
- timesteps: int32 [128], P('dp'), may hold values from 0 to 999
- labels: int32 [128], P('dp'), may hold values from 0 to 999
- lengths: int32 [128], replicated, may hold values from 1 to 256, as said below
- class_vectors: bfloat16 [1000, 1152], replicated, may hold values from -6 to 6
- embedder: float32 [16, 1152], replicated, may hold values from -1.5 to 1.5
- time_first: float32 [256, 1152], replicated, may hold values from -0.375 to 0.375
- time_second: float32 [1152, 1152], replicated, may hold values from -0.1875 to 0.1875
- modulator: float32 [1152, 6912], P(None, 'mp'), may hold values from -0.1875 to 0.1875
- mixer_input: float32 [1152, 3456], P(None, 'mp'), may hold values from -0.25 to 0.25
- mixer_output: float32 [1152, 1152], P('mp'), may hold values from -0.75 to 0.75
- expander: float32 [1152, 4608], P(None, 'mp'), may hold values from -0.1875 to 0.1875
- contractor: float32 [4608, 1152], P('mp'), may hold values from -0.09375 to 0.09375
- finisher: float32 [1152, 2304], P(None, 'mp'), may hold values from -0.1875 to 0.1875
- readout: float32 [1152, 16], replicated, may hold values from -0.1875 to 0.1875
- row_states: float32 [12944], replicated, may hold values from 8.8649465e-13 to 3.5459786e-12
- column_states: float32 [23056], replicated, may hold values from 8.8649465e-13 to 3.5459786e-12
Outputs:
- loss_sum: float32 [], replicated
- loss_count: float32 [], replicated
- grad_norm: float32 [], replicated
- embedder_next: float32 [16, 1152], replicated
- time_first_next: float32 [256, 1152], replicated
- time_second_next: float32 [1152, 1152], replicated
- modulator_next: float32 [1152, 6912], P(None, 'mp')
- mixer_input_next: float32 [1152, 3456], P(None, 'mp')
- mixer_output_next: float32 [1152, 1152], P('mp')
- expander_next: float32 [1152, 4608], P(None, 'mp')
- contractor_next: float32 [4608, 1152], P('mp')
- finisher_next: float32 [1152, 2304], P(None, 'mp')
- readout_next: float32 [1152, 16], replicated
- embedder_grad: float32 [16, 1152], replicated
- time_first_grad: float32 [256, 1152], replicated
- time_second_grad: float32 [1152, 1152], replicated
- modulator_grad: float32 [1152, 6912], P(None, 'mp')
- mixer_input_grad: float32 [1152, 3456], P(None, 'mp')
- mixer_output_grad: float32 [1152, 1152], P('mp')
- expander_grad: float32 [1152, 4608], P(None, 'mp')
- contractor_grad: float32 [4608, 1152], P('mp')
- finisher_grad: float32 [1152, 2304], P(None, 'mp')
- readout_grad: float32 [1152, 16], replicated
- row_stats: float32 [12944], replicated
- column_stats: float32 [23056], replicated
Inputs may be any that keep to these rules, and one draw needn't show every extreme that they name: Patches 0 to lengths - 1 of an image are valid; at least one image is whole.
All inputs are finite; a program needn't handle non-finite values.
Results may differ from a plain program's by a relative error of at most 0.019.
The roundings to bfloat16 on the way count: a program that leaves them out, or rounds other values in their place, can miss the bound.
Values may be sent and summed in bfloat16 or wider, within the bound.
A program may use at most 576 MiB of HBM per device.

v0:
```python
import math

import jax
import jax.numpy as jnp
from jax import lax
from jax.sharding import PartitionSpec as P

HD = 72
FREQ = 256
PIN = 16
SIDE = 16
MICRO = 4
IMG_DEV = 1


eps_norm = 1e-06
eps_factor = 1e-30
clip_limit = 0.005
state_decay = 0.5
step_rate = 1.5
neg_large = -1e30
highest = lax.Precision.HIGHEST


def product(operand, other_operand):
    return jnp.dot(operand, other_operand, preferred_element_type=jnp.float32)


def product_right(operand, other_operand):
    return lax.dot_general(
        operand, other_operand, (((1,), (1,)), ((), ())), preferred_element_type=jnp.float32
    )


def product_left(operand, other_operand):
    return lax.dot_general(
        operand, other_operand, (((0,), (0,)), ((), ())), preferred_element_type=jnp.float32
    )


def layer_norm(values):
    center = values - jnp.mean(values, axis=-1, keepdims=True)
    return center * lax.rsqrt(jnp.mean(center * center, axis=-1, keepdims=True) + eps_norm)


def norm_back(values, upstream):
    center = values - jnp.mean(values, axis=-1, keepdims=True)
    inverse = lax.rsqrt(jnp.mean(center * center, axis=-1, keepdims=True) + eps_norm)
    normed = center * inverse
    return inverse * (
        upstream
        - jnp.mean(upstream, axis=-1, keepdims=True)
        - normed * jnp.mean(upstream * normed, axis=-1, keepdims=True)
    )


def position_table(side, width):
    quarter = width // 4
    omega = jnp.exp(-math.log(10000.0) * jnp.arange(quarter, dtype=jnp.float32) / quarter)
    place = jnp.arange(side * side)
    column = (place % side).astype(jnp.float32)[:, None] * omega[None, :]
    row_angle = (place // side).astype(jnp.float32)[:, None] * omega[None, :]
    return jnp.concatenate(
        [jnp.sin(column), jnp.cos(column), jnp.sin(row_angle), jnp.cos(row_angle)], axis=1
    )


def time_features(steps, width):
    half = width // 2
    freq = jnp.exp(-math.log(10000.0) * jnp.arange(half, dtype=jnp.float32) / half)
    angle = steps.astype(jnp.float32)[:, None] * freq[None, :]
    return jnp.concatenate([jnp.cos(angle), jnp.sin(angle)], axis=1)


def rows_in(values):
    return lax.all_gather(values, "mp", axis=0, tiled=True)


def rows_out(values):
    return lax.psum_scatter(values, "mp", scatter_dimension=0, tiled=True)


def grads_in(values):
    return lax.all_gather(values, "mp", axis=0, tiled=True)


def grads_out(values):
    return lax.psum_scatter(values, "mp", scatter_dimension=0, tiled=True)


def attention_scores(queries, key_part, live_keys):
    scores = jnp.einsum(
        "gqhe,gkhe->ghqk", queries, key_part, preferred_element_type=jnp.float32
    ) * HD ** (-0.5)
    return jnp.where(live_keys[:, None, None, :], scores, neg_large)


def partial_sums(matrix, layout):
    if layout == "columns":
        return jnp.sum(matrix * matrix, axis=1)
    return jnp.sum(matrix * matrix, axis=0)


def body(
    latents,
    noise_draw,
    alpha_bar,
    timesteps,
    labels,
    lengths,
    class_vectors,
    embedder,
    time_first,
    time_second,
    modulator,
    mixer_input,
    mixer_output,
    expander,
    contractor,
    finisher,
    readout,
    row_states,
    column_states,
):
    groups = lax.axis_size("mp")
    member = lax.axis_index("mp")
    width = embedder.shape[1]
    patches = SIDE * SIDE
    own_images = MICRO * IMG_DEV
    per_group = groups * own_images
    own_rows = IMG_DEV * patches
    valid_total = jnp.sum(lengths).astype(jnp.float32) * PIN
    group_lengths = lax.dynamic_slice_in_dim(
        lengths, lax.axis_index("dp") * per_group, per_group
    ).reshape(groups, MICRO, IMG_DEV)
    own_lengths = lax.dynamic_index_in_dim(group_lengths, member, 0, keepdims=False)
    own_alpha = lax.dynamic_index_in_dim(
        alpha_bar.reshape(groups, MICRO, IMG_DEV), member, 0, keepdims=False
    )
    positions = position_table(SIDE, width)
    place = jnp.arange(patches)
    features = time_features(timesteps, FREQ)
    class_rows = jnp.take(class_vectors, labels, axis=0).astype(jnp.float32)

    def condition(first_weight, second_weight):
        hidden = jax.nn.silu(jnp.dot(features, first_weight, precision=highest))
        return jax.nn.silu(jnp.dot(hidden, second_weight, precision=highest) + class_rows)

    signal_full, condition_pull = jax.vjp(condition, time_first, time_second)
    signal = signal_full.astype(jnp.bfloat16)
    modulator_low = modulator.astype(jnp.bfloat16)
    finisher_low = finisher.astype(jnp.bfloat16)
    steer_part = product(signal, modulator_low).astype(jnp.bfloat16)
    final_part = product(signal, finisher_low).astype(jnp.bfloat16)
    steer_own, final_own = (
        lax.all_to_all(steer_part, "mp", split_axis=0, concat_axis=1, tiled=True),
        lax.all_to_all(final_part, "mp", split_axis=0, concat_axis=1, tiled=True),
    )
    steer_own = steer_own.astype(jnp.float32).reshape(MICRO, IMG_DEV, 6, 1, width)
    final_own = final_own.astype(jnp.float32).reshape(MICRO, IMG_DEV, 2, 1, width)
    embedder_low = embedder.astype(jnp.bfloat16)
    readout_low = readout.astype(jnp.bfloat16)
    inputs_low = mixer_input.astype(jnp.bfloat16)
    outputs_low = mixer_output.astype(jnp.bfloat16)
    expand_low = expander.astype(jnp.bfloat16)
    contract_low = contractor.astype(jnp.bfloat16)
    inputs_use, outputs_use, expand_use, contract_use = (
        inputs_low,
        outputs_low,
        expand_low,
        contract_low,
    )
    heads_here = inputs_use.shape[1] // (3 * HD)

    def layer_backward(grad_residual, steering, kept):
        (
            residual_zero,
            residual_one,
            normed_one,
            normed_two,
            input_one,
            qkv_rows,
            log_mass,
            mixed_out,
            branch_one,
            input_two,
            pre_active,
            active,
            branch_two,
            live_keys,
        ) = kept
        gate_two_grad = jnp.sum(grad_residual * branch_two, axis=1)
        branch_two_grad = grads_in(
            (steering[:, 5] * grad_residual).astype(jnp.bfloat16).reshape(own_rows, width)
        )
        contract_grad = product_left(active, branch_two_grad)
        active_grad = product_right(branch_two_grad, contract_use)
        gelu_pull = jax.vjp(lambda inner: jax.nn.gelu(inner, approximate=True), pre_active)[1]
        pre_grad = gelu_pull(active_grad)[0].astype(jnp.bfloat16)
        expand_grad = product_left(input_two, pre_grad)
        input_two_grad = grads_out(product_right(pre_grad, expand_use)).reshape(
            IMG_DEV, patches, width
        )
        shift_two_grad = jnp.sum(input_two_grad, axis=1)
        scale_two_grad = jnp.sum(input_two_grad * normed_two, axis=1)
        grad_residual = grad_residual + norm_back(
            residual_one, input_two_grad * (1.0 + steering[:, 4])
        )
        gate_one_grad = jnp.sum(grad_residual * branch_one, axis=1)
        branch_one_grad = grads_in(
            (steering[:, 2] * grad_residual).astype(jnp.bfloat16).reshape(own_rows, width)
        )
        outputs_grad = product_left(mixed_out, branch_one_grad)
        images_here = qkv_rows.shape[0]
        mixed_grad = (
            product_right(branch_one_grad, outputs_use)
            .astype(jnp.bfloat16)
            .reshape(images_here, patches, heads_here, HD)
        )
        queries = qkv_rows[:, :, :, 0]
        key_part = qkv_rows[:, :, :, 1]
        value_part = qkv_rows[:, :, :, 2]
        attend = jnp.exp(attention_scores(queries, key_part, live_keys) - log_mass)
        attend_grad = jnp.einsum(
            "gqhe,gkhe->ghqk", mixed_grad, value_part, preferred_element_type=jnp.float32
        )
        score_grad = (
            attend * (attend_grad - jnp.sum(attend * attend_grad, axis=-1, keepdims=True))
        ).astype(jnp.bfloat16)
        query_grad = jnp.einsum(
            "ghqk,gkhe->gqhe", score_grad, key_part, preferred_element_type=jnp.float32
        ) * HD ** (-0.5)
        key_grad = jnp.einsum(
            "ghqk,gqhe->gkhe", score_grad, queries, preferred_element_type=jnp.float32
        ) * HD ** (-0.5)
        value_grad = jnp.einsum(
            "ghqk,gqhe->gkhe",
            attend.astype(jnp.bfloat16),
            mixed_grad,
            preferred_element_type=jnp.float32,
        )
        qkv_grad = (
            jnp.stack([query_grad, key_grad, value_grad], axis=3)
            .astype(jnp.bfloat16)
            .reshape(images_here * patches, heads_here * 3 * HD)
        )
        inputs_grad = product_left(input_one, qkv_grad)
        input_one_grad = grads_out(product_right(qkv_grad, inputs_use)).reshape(
            IMG_DEV, patches, width
        )
        shift_one_grad = jnp.sum(input_one_grad, axis=1)
        scale_one_grad = jnp.sum(input_one_grad * normed_one, axis=1)
        grad_residual = grad_residual + norm_back(
            residual_zero, input_one_grad * (1.0 + steering[:, 1])
        )
        steer_grad = jnp.stack(
            [
                shift_one_grad,
                scale_one_grad,
                gate_one_grad,
                shift_two_grad,
                scale_two_grad,
                gate_two_grad,
            ],
            axis=1,
        )
        return (grad_residual, steer_grad, (inputs_grad, outputs_grad, expand_grad, contract_grad))

    embed_running = jnp.zeros(embedder.shape, jnp.float32)
    readout_running = jnp.zeros(readout.shape, jnp.float32)
    block_running = (
        jnp.zeros(inputs_use.shape, jnp.float32),
        jnp.zeros(outputs_use.shape, jnp.float32),
        jnp.zeros(expand_use.shape, jnp.float32),
        jnp.zeros(contract_use.shape, jnp.float32),
    )
    loss_part = jnp.zeros((), jnp.float32)
    steer_grads = []
    final_grads = []
    for micro_index in range(MICRO):
        first_image = micro_index * IMG_DEV
        root_keep = jnp.sqrt(own_alpha[micro_index])[:, None, None]
        root_noise = jnp.sqrt(1.0 - own_alpha[micro_index])[:, None, None]
        clean_part = latents[first_image : first_image + IMG_DEV]
        noise_part = noise_draw[first_image : first_image + IMG_DEV]
        noisy = (
            (root_keep * clean_part + root_noise * noise_part)
            .astype(jnp.bfloat16)
            .reshape(own_rows, PIN)
        )
        target = (root_keep * noise_part - root_noise * clean_part).reshape(own_rows, PIN)
        live_rows = (place[None, :] < own_lengths[micro_index][:, None]).reshape(own_rows, 1)
        key_lengths = group_lengths[:, micro_index].reshape(-1)
        live_keys = place[None, :] < key_lengths[:, None]
        steering = steer_own[micro_index]
        final_steer = final_own[micro_index]
        residual_zero = (
            product(noisy, embedder_low).reshape(IMG_DEV, patches, width) + positions[None]
        )
        layer_normed_one = layer_norm(residual_zero)
        layer_input_one = rows_in(
            (layer_normed_one * (1.0 + steering[:, 1]) + steering[:, 0])
            .astype(jnp.bfloat16)
            .reshape(own_rows, width)
        )
        layer_images_here = layer_input_one.shape[0] // patches
        layer_qkv_rows = (
            product(layer_input_one, inputs_use)
            .astype(jnp.bfloat16)
            .reshape(layer_images_here, patches, heads_here, 3, HD)
        )
        scores = attention_scores(layer_qkv_rows[:, :, :, 0], layer_qkv_rows[:, :, :, 1], live_keys)
        peak = jnp.max(scores, axis=-1, keepdims=True)
        exponent = jnp.exp(scores - peak)
        mass = jnp.sum(exponent, axis=-1, keepdims=True)
        layer_log_mass = peak + jnp.log(mass)
        layer_mixed_out = jnp.einsum(
            "ghqk,gkhe->gqhe",
            (exponent / mass).astype(jnp.bfloat16),
            layer_qkv_rows[:, :, :, 2],
            preferred_element_type=jnp.float32,
        )
        layer_mixed_out = layer_mixed_out.astype(jnp.bfloat16).reshape(
            layer_images_here * patches, heads_here * HD
        )
        layer_branch_one = rows_out(product(layer_mixed_out, outputs_use)).reshape(
            IMG_DEV, patches, width
        )
        layer_residual_one = residual_zero + steering[:, 2] * layer_branch_one
        layer_normed_two = layer_norm(layer_residual_one)
        layer_input_two = rows_in(
            (layer_normed_two * (1.0 + steering[:, 4]) + steering[:, 3])
            .astype(jnp.bfloat16)
            .reshape(own_rows, width)
        )
        layer_pre_active = product(layer_input_two, expand_use)
        layer_active = jax.nn.gelu(layer_pre_active, approximate=True).astype(jnp.bfloat16)
        layer_branch_two = rows_out(product(layer_active, contract_use)).reshape(
            IMG_DEV, patches, width
        )
        residual_two = layer_residual_one + steering[:, 5] * layer_branch_two
        layer_kept = (
            residual_zero,
            layer_residual_one,
            layer_normed_one,
            layer_normed_two,
            layer_input_one,
            layer_qkv_rows,
            layer_log_mass,
            layer_mixed_out,
            layer_branch_one,
            layer_input_two,
            layer_pre_active,
            layer_active,
            layer_branch_two,
            live_keys,
        )
        residual_two, kept = (residual_two, layer_kept)
        normed_final = layer_norm(residual_two)
        input_final = (
            (normed_final * (1.0 + final_steer[:, 1]) + final_steer[:, 0])
            .astype(jnp.bfloat16)
            .reshape(own_rows, width)
        )
        misfit = product(input_final, readout_low) - target
        loss_part = loss_part + jnp.sum(jnp.where(live_rows, misfit * misfit, 0.0))
        output_grad = jnp.where(live_rows, 2.0 * misfit / valid_total, 0.0).astype(jnp.bfloat16)
        readout_running = readout_running + product_left(input_final, output_grad)
        final_grad = product_right(output_grad, readout_low).reshape(IMG_DEV, patches, width)
        final_shift_grad = jnp.sum(final_grad, axis=1)
        final_scale_grad = jnp.sum(final_grad * normed_final, axis=1)
        grad_residual = norm_back(residual_two, final_grad * (1.0 + final_steer[:, 1]))
        grad_residual, steer_grad, block_grads = layer_backward(grad_residual, steering, kept)
        embed_running = embed_running + product_left(
            noisy, grad_residual.reshape(own_rows, width).astype(jnp.bfloat16)
        )
        block_running = tuple(
            (running + piece for running, piece in zip(block_running, block_grads))
        )
        steer_grads.append(steer_grad)
        final_grads.append(jnp.stack([final_shift_grad, final_scale_grad], axis=1))
    steer_back = jnp.stack(steer_grads).reshape(own_images, 6 * width).astype(jnp.bfloat16)
    final_back = jnp.stack(final_grads).reshape(own_images, 2 * width).astype(jnp.bfloat16)
    steer_cols, final_cols = (
        lax.all_to_all(steer_back, "mp", split_axis=1, concat_axis=0, tiled=True),
        lax.all_to_all(final_back, "mp", split_axis=1, concat_axis=0, tiled=True),
    )
    modulator_grad = product_left(signal, steer_cols)
    finisher_grad = product_left(signal, final_cols)
    signal_grad = product_right(steer_cols, modulator_low) + product_right(final_cols, finisher_low)
    time_first_grad, time_second_grad = condition_pull(signal_grad)
    shared = lax.psum(
        (embed_running, time_first_grad, time_second_grad, readout_running, loss_part), ("dp", "mp")
    )
    split = (
        lax.psum(modulator_grad.astype(jnp.bfloat16), "dp").astype(jnp.float32),
        lax.psum(block_running[0].astype(jnp.bfloat16), "dp").astype(jnp.float32),
        lax.psum(block_running[1].astype(jnp.bfloat16), "dp").astype(jnp.float32),
        lax.psum(block_running[2].astype(jnp.bfloat16), "dp").astype(jnp.float32),
        lax.psum(block_running[3].astype(jnp.bfloat16), "dp").astype(jnp.float32),
        lax.psum(finisher_grad.astype(jnp.bfloat16), "dp").astype(jnp.float32),
    )
    gradients = (
        shared[0],
        shared[1],
        shared[2],
        split[0],
        split[1],
        split[2],
        split[3],
        split[4],
        split[5],
        shared[3],
    )
    loss_sum = shared[4]
    weights = (
        embedder,
        time_first,
        time_second,
        modulator,
        mixer_input,
        mixer_output,
        expander,
        contractor,
        finisher,
        readout,
    )
    layouts = (
        "whole",
        "whole",
        "whole",
        "columns",
        "columns",
        "rows",
        "columns",
        "rows",
        "columns",
        "whole",
    )
    local_square = sum((jnp.sum(gradients[slot] * gradients[slot]) for slot in (0, 1, 2, 9)))
    split_square = sum((jnp.sum(gradients[slot] * gradients[slot]) for slot in range(3, 9)))
    grad_norm = jnp.sqrt(lax.psum(split_square, "mp") + local_square)
    factor = clip_limit / jnp.maximum(grad_norm, clip_limit)
    crossed = list(
        lax.psum(
            (
                partial_sums(gradients[3] * factor, layouts[3]),
                partial_sums(gradients[4] * factor, layouts[4]),
                partial_sums(gradients[5] * factor, layouts[5]),
                partial_sums(gradients[6] * factor, layouts[6]),
                partial_sums(gradients[7] * factor, layouts[7]),
                partial_sums(gradients[8] * factor, layouts[8]),
            ),
            "mp",
        )
    )
    row_pad = jnp.zeros_like(row_states)
    column_pad = jnp.zeros_like(column_states)
    row_at = 0
    column_at = 0
    records = []
    split_energy = []
    for slot in range(10):
        weight = weights[slot]
        layout = layouts[slot]
        local_rows, local_cols = weight.shape
        many_rows = local_rows * (groups if layout == "rows" else 1)
        many_cols = local_cols * (groups if layout == "columns" else 1)
        clipped = gradients[slot] * factor
        square = clipped * clipped
        row_sum = crossed[slot - 3] if layout == "columns" else jnp.sum(square, axis=1)
        column_sum = crossed[slot - 3] if layout == "rows" else jnp.sum(square, axis=0)
        row_mean = row_sum / many_cols + eps_factor
        column_mean = column_sum / many_rows + eps_factor
        if layout == "rows":
            row_old = lax.dynamic_slice_in_dim(row_states, row_at + member * local_rows, local_rows)
        else:
            row_old = row_states[row_at : row_at + many_rows]
        if layout == "columns":
            column_old = lax.dynamic_slice_in_dim(
                column_states, column_at + member * local_cols, local_cols
            )
        else:
            column_old = column_states[column_at : column_at + many_cols]
        row_next = state_decay * row_old + (1.0 - state_decay) * row_mean
        column_next = state_decay * column_old + (1.0 - state_decay) * column_mean
        if layout == "rows":
            row_average = state_decay * jnp.mean(row_states[row_at : row_at + many_rows]) + (
                1.0 - state_decay
            ) * jnp.mean(column_mean)
            row_pad = lax.dynamic_update_slice_in_dim(
                row_pad, row_next, row_at + member * local_rows, 0
            )
        else:
            row_average = jnp.mean(row_next)
        if layout == "columns":
            column_pad = lax.dynamic_update_slice_in_dim(
                column_pad, column_next, column_at + member * local_cols, 0
            )
        update = clipped * lax.rsqrt(row_next[:, None] * column_next[None, :] / row_average)
        energy = jnp.sum(update * update)
        if layout != "whole":
            split_energy.append(energy)
        records.append(
            (
                clipped,
                update,
                energy,
                row_next,
                column_next,
                row_at,
                column_at,
                many_rows,
                many_cols,
            )
        )
        row_at += many_rows
        column_at += many_cols
    energy_sums, row_pad, column_pad = (
        lax.psum(jnp.stack(split_energy).astype(jnp.bfloat16), "mp").astype(jnp.float32),
        lax.psum(row_pad.astype(jnp.bfloat16), "mp").astype(jnp.float32),
        lax.psum(column_pad.astype(jnp.bfloat16), "mp").astype(jnp.float32),
    )
    next_list = []
    clipped_list = []
    row_list = []
    column_list = []
    for slot in range(10):
        (
            clipped,
            update,
            energy,
            row_next,
            column_next,
            row_start,
            column_start,
            many_rows,
            many_cols,
        ) = records[slot]
        layout = layouts[slot]
        if layout != "whole":
            energy = energy_sums[slot - 3]
        scale_down = jnp.maximum(1.0, jnp.sqrt(energy / (many_rows * many_cols)))
        next_list.append(weights[slot] - step_rate / math.sqrt(many_rows) * (update / scale_down))
        clipped_list.append(clipped)
        if layout == "rows":
            row_list.append(row_pad[row_start : row_start + many_rows])
        else:
            row_list.append(row_next)
        if layout == "columns":
            column_list.append(column_pad[column_start : column_start + many_cols])
        else:
            column_list.append(column_next)
    return (
        loss_sum,
        valid_total,
        grad_norm,
        next_list[0],
        next_list[1],
        next_list[2],
        next_list[3],
        next_list[4],
        next_list[5],
        next_list[6],
        next_list[7],
        next_list[8],
        next_list[9],
        clipped_list[0],
        clipped_list[1],
        clipped_list[2],
        clipped_list[3],
        clipped_list[4],
        clipped_list[5],
        clipped_list[6],
        clipped_list[7],
        clipped_list[8],
        clipped_list[9],
        jnp.concatenate(row_list),
        jnp.concatenate(column_list),
    )


def solution(mesh):
    in_specs = (
        P(("dp", "mp"), None, None),
        P(("dp", "mp"), None, None),
        P("dp"),
        P("dp"),
        P("dp"),
        P(),
        P(),
        P(),
        P(),
        P(),
        P(None, "mp"),
        P(None, "mp"),
        P("mp", None),
        P(None, "mp"),
        P("mp", None),
        P(None, "mp"),
        P(),
        P(),
        P(),
    )
    out_specs = (
        P(),
        P(),
        P(),
        P(),
        P(),
        P(),
        P(None, "mp"),
        P(None, "mp"),
        P("mp", None),
        P(None, "mp"),
        P("mp", None),
        P(None, "mp"),
        P(),
        P(),
        P(),
        P(),
        P(None, "mp"),
        P(None, "mp"),
        P("mp", None),
        P(None, "mp"),
        P("mp", None),
        P(None, "mp"),
        P(),
        P(),
        P(),
    )
    return jax.shard_map(body, mesh=mesh, in_specs=in_specs, out_specs=out_specs, check_vma=False)
```

profile of v0, /device:TPU:0, one launch (start us, length us, event | category | flops | bytes accessed | tf_op | source)
XLA Modules:
  0.0 4527.1 jit_solution(2314823475855220711)
XLA Ops:
  12.2 6.1 multiply_convert_fusion.16
  19.7 7.3 all-to-all-start
  60.1 61.2 %all-gather.17.cloned.1.call-done = bf16[2048,1152]{1,0:T(8,128)(2,1)} async-done(((bf16[256,1152]{1,0:T(8,128)(2,1)}), bf16[2048,1152]{1,0:T(8,128)(2,1)}) %all-gather.17.cloned.1.call-update) | async-done | bytes 4718608 | tf_op jit(solution)/shard_map/all_gather | solution.py:76
  137.6 64.6 %all-gather.21.cloned.1.call-done = bf16[2048,1152]{1,0:T(8,128)(2,1)} async-done(((bf16[256,1152]{1,0:T(8,128)(2,1)}), bf16[2048,1152]{1,0:T(8,128)(2,1)}) %all-gather.21.cloned.1.call-update) | async-done | bytes 4718608 | tf_op jit(solution)/shard_map/all_gather | solution.py:76
  218.6 64.5 %all-gather.25.cloned.1.call-done = bf16[2048,1152]{1,0:T(8,128)(2,1)} async-done(((bf16[256,1152]{1,0:T(8,128)(2,1)}), bf16[2048,1152]{1,0:T(8,128)(2,1)}) %all-gather.25.cloned.1.call-update) | async-done | bytes 4718608 | tf_op jit(solution)/shard_map/all_gather | solution.py:76
  299.3 64.5 %all-gather.29.cloned.1.call-done = bf16[2048,1152]{1,0:T(8,128)(2,1)} async-done(((bf16[256,1152]{1,0:T(8,128)(2,1)}), bf16[2048,1152]{1,0:T(8,128)(2,1)}) %all-gather.29.cloned.1.call-update) | async-done | bytes 4718608 | tf_op jit(solution)/shard_map/all_gather | solution.py:76
  379.9 148.8 %reduce-scatter.17.cloned.1.call-done = f32[256,1152]{1,0:T(8,128)} async-done(((f32[2048,1152]{1,0:T(8,128)}), f32[256,1152]{1,0:T(8,128)}) %reduce-scatter.17.cloned.1.call-update) | async-done | bytes 1179664 | tf_op jit(solution)/shard_map/reduce_scatter | solution.py:80
  532.4 162.4 %reduce-scatter.21.cloned.1.call-done = f32[256,1152]{1,0:T(8,128)} async-done(((f32[2048,1152]{1,0:T(8,128)}), f32[256,1152]{1,0:T(8,128)}) %reduce-scatter.21.cloned.1.call-update) | async-done | bytes 1179664 | tf_op jit(solution)/shard_map/reduce_scatter | solution.py:80
  698.5 162.3 %reduce-scatter.25.cloned.1.call-done = f32[256,1152]{1,0:T(8,128)} async-done(((f32[2048,1152]{1,0:T(8,128)}), f32[256,1152]{1,0:T(8,128)}) %reduce-scatter.25.cloned.1.call-update) | async-done | bytes 1179664 | tf_op jit(solution)/shard_map/reduce_scatter | solution.py:80
  864.5 162.3 %reduce-scatter.29.cloned.1.call-done = f32[256,1152]{1,0:T(8,128)} async-done(((f32[2048,1152]{1,0:T(8,128)}), f32[256,1152]{1,0:T(8,128)}) %reduce-scatter.29.cloned.1.call-update) | async-done | bytes 1179664 | tf_op jit(solution)/shard_map/reduce_scatter | solution.py:80
  1033.9 74.7 %all-gather.19.cloned.1.call-done = bf16[2048,1152]{1,0:T(8,128)(2,1)} async-done(((bf16[256,1152]{1,0:T(8,128)(2,1)}), bf16[2048,1152]{1,0:T(8,128)(2,1)}) %all-gather.19.cloned.1.call-update) | async-done | bytes 4718608 | tf_op jit(solution)/shard_map/all_gather | solution.py:76
  1115.9 7.0 fusion.176
  1123.0 66.3 %all-gather.23.cloned.1.call-done = bf16[2048,1152]{1,0:T(8,128)(2,1)} async-done(((bf16[256,1152]{1,0:T(8,128)(2,1)}), bf16[2048,1152]{1,0:T(8,128)(2,1)}) %all-gather.23.cloned.1.call-update) | async-done | bytes 4718608 | tf_op jit(solution)/shard_map/all_gather | solution.py:76
  1196.7 6.9 fusion.177
  1203.7 66.4 %all-gather.27.cloned.1.call-done = bf16[2048,1152]{1,0:T(8,128)(2,1)} async-done(((bf16[256,1152]{1,0:T(8,128)(2,1)}), bf16[2048,1152]{1,0:T(8,128)(2,1)}) %all-gather.27.cloned.1.call-update) | async-done | bytes 4718608 | tf_op jit(solution)/shard_map/all_gather | solution.py:76
  1277.5 6.8 fusion.178
  1284.8 65.9 %all-gather.31.cloned.1.call-done = bf16[2048,1152]{1,0:T(8,128)(2,1)} async-done(((bf16[256,1152]{1,0:T(8,128)(2,1)}), bf16[2048,1152]{1,0:T(8,128)(2,1)}) %all-gather.31.cloned.1.call-update) | async-done | bytes 4718608 | tf_op jit(solution)/shard_map/all_gather | solution.py:76
  1358.2 6.8 fusion.179
  1379.0 138.5 %reduce-scatter.19.cloned.1.call-done = f32[256,1152]{1,0:T(8,128)} async-done(((f32[2048,1152]{1,0:T(8,128)}), f32[256,1152]{1,0:T(8,128)}) %reduce-scatter.19.cloned.1.call-update) | async-done | bytes 1179664 | tf_op jit(solution)/shard_map/reduce_scatter | solution.py:80
  1525.8 157.7 %reduce-scatter.23.cloned.1.call-done = f32[256,1152]{1,0:T(8,128)} async-done(((f32[2048,1152]{1,0:T(8,128)}), f32[256,1152]{1,0:T(8,128)}) %reduce-scatter.23.cloned.1.call-update) | async-done | bytes 1179664 | tf_op jit(solution)/shard_map/reduce_scatter | solution.py:80
  1691.5 158.0 %reduce-scatter.27.cloned.1.call-done = f32[256,1152]{1,0:T(8,128)} async-done(((f32[2048,1152]{1,0:T(8,128)}), f32[256,1152]{1,0:T(8,128)}) %reduce-scatter.27.cloned.1.call-update) | async-done | bytes 1179664 | tf_op jit(solution)/shard_map/reduce_scatter | solution.py:80
  1857.7 157.8 %reduce-scatter.31.cloned.1.call-done = f32[256,1152]{1,0:T(8,128)} async-done(((f32[2048,1152]{1,0:T(8,128)}), f32[256,1152]{1,0:T(8,128)}) %reduce-scatter.31.cloned.1.call-update) | async-done | bytes 1179664 | tf_op jit(solution)/shard_map/reduce_scatter | solution.py:80
  2022.8 74.4 %all-gather.33.cloned.1.call-done = bf16[2048,1152]{1,0:T(8,128)(2,1)} async-done(((bf16[256,1152]{1,0:T(8,128)(2,1)}), bf16[2048,1152]{1,0:T(8,128)(2,1)}) %all-gather.33.cloned.1.call-update) | async-done | bytes 4718608 | tf_op jit(solution)/shard_map/all_gather | solution.py:84
  2097.1 9.7 fusion.6
  2108.3 6.6 fusion.219
  2115.2 62.6 %all-gather.37.cloned.1.call-done = bf16[2048,1152]{1,0:T(8,128)(2,1)} async-done(((bf16[256,1152]{1,0:T(8,128)(2,1)}), bf16[2048,1152]{1,0:T(8,128)(2,1)}) %all-gather.37.cloned.1.call-update) | async-done | bytes 4718608 | tf_op jit(solution)/shard_map/all_gather | solution.py:84
  2177.8 9.7 fusion.13
  2189.0 6.6 fusion.221
  2195.7 63.0 %all-gather.41.cloned.1.call-done = bf16[2048,1152]{1,0:T(8,128)(2,1)} async-done(((bf16[256,1152]{1,0:T(8,128)(2,1)}), bf16[2048,1152]{1,0:T(8,128)(2,1)}) %all-gather.41.cloned.1.call-update) | async-done | bytes 4718608 | tf_op jit(solution)/shard_map/all_gather | solution.py:84
  2258.6 9.8 fusion.20
  2269.8 6.6 fusion.223
  2276.9 62.4 %all-gather.45.cloned.1.call-done = bf16[2048,1152]{1,0:T(8,128)(2,1)} async-done(((bf16[256,1152]{1,0:T(8,128)(2,1)}), bf16[2048,1152]{1,0:T(8,128)(2,1)}) %all-gather.45.cloned.1.call-update) | async-done | bytes 4718608 | tf_op jit(solution)/shard_map/all_gather | solution.py:84
  2339.3 9.7 fusion.27
  2350.4 6.6 fusion.225
  2357.1 147.4 %reduce-scatter.33.cloned.1.call-done = f32[256,1152]{1,0:T(8,128)} async-done(((f32[2048,1152]{1,0:T(8,128)}), f32[256,1152]{1,0:T(8,128)}) %reduce-scatter.33.cloned.1.call-update) | async-done | bytes 1179664 | tf_op jit(solution)/shard_map/reduce_scatter | solution.py:88
  2513.1 157.6 %reduce-scatter.37.cloned.1.call-done = f32[256,1152]{1,0:T(8,128)} async-done(((f32[2048,1152]{1,0:T(8,128)}), f32[256,1152]{1,0:T(8,128)}) %reduce-scatter.37.cloned.1.call-update) | async-done | bytes 1179664 | tf_op jit(solution)/shard_map/reduce_scatter | solution.py:88
  2679.3 157.6 %reduce-scatter.41.cloned.1.call-done = f32[256,1152]{1,0:T(8,128)} async-done(((f32[2048,1152]{1,0:T(8,128)}), f32[256,1152]{1,0:T(8,128)}) %reduce-scatter.41.cloned.1.call-update) | async-done | bytes 1179664 | tf_op jit(solution)/shard_map/reduce_scatter | solution.py:88
  2844.1 158.8 %reduce-scatter.45.cloned.1.call-done = f32[256,1152]{1,0:T(8,128)} async-done(((f32[2048,1152]{1,0:T(8,128)}), f32[256,1152]{1,0:T(8,128)}) %reduce-scatter.45.cloned.1.call-update) | async-done | bytes 1179664 | tf_op jit(solution)/shard_map/reduce_scatter | solution.py:88
  3008.8 75.9 %all-gather.35.cloned.1.call-done = bf16[2048,1152]{1,0:T(8,128)(2,1)} async-done(((bf16[256,1152]{1,0:T(8,128)(2,1)}), bf16[2048,1152]{1,0:T(8,128)(2,1)}) %all-gather.35.cloned.1.call-update) | async-done | bytes 4718608 | tf_op jit(solution)/shard_map/all_gather | solution.py:84
  3101.6 63.7 %all-gather.39.cloned.1.call-done = bf16[2048,1152]{1,0:T(8,128)(2,1)} async-done(((bf16[256,1152]{1,0:T(8,128)(2,1)}), bf16[2048,1152]{1,0:T(8,128)(2,1)}) %all-gather.39.cloned.1.call-update) | async-done | bytes 4718608 | tf_op jit(solution)/shard_map/all_gather | solution.py:84
  3182.3 63.7 %all-gather.43.cloned.1.call-done = bf16[2048,1152]{1,0:T(8,128)(2,1)} async-done(((bf16[256,1152]{1,0:T(8,128)(2,1)}), bf16[2048,1152]{1,0:T(8,128)(2,1)}) %all-gather.43.cloned.1.call-update) | async-done | bytes 4718608 | tf_op jit(solution)/shard_map/all_gather | solution.py:84
  3257.0 5.3 fusion.224
  3263.0 63.8 %all-gather.47.cloned.1.call-done = bf16[2048,1152]{1,0:T(8,128)(2,1)} async-done(((bf16[256,1152]{1,0:T(8,128)(2,1)}), bf16[2048,1152]{1,0:T(8,128)(2,1)}) %all-gather.47.cloned.1.call-update) | async-done | bytes 4718608 | tf_op jit(solution)/shard_map/all_gather | solution.py:84
  3337.7 5.4 fusion.226
  3350.2 5.4 all-to-all-done.3
  3356.9 6.4 fusion.230
  3366.7 7.2 convolution_add_fusion.1
  3374.0 5.9 fusion.38
  3389.3 5.4 convolution_add_fusion.4
  3394.9 7.6 fusion.37
  3420.5 73.0 %reduce-scatter.35.cloned.1.call-done = f32[256,1152]{1,0:T(8,128)} async-done(((f32[2048,1152]{1,0:T(8,128)}), f32[256,1152]{1,0:T(8,128)}) %reduce-scatter.35.cloned.1.call-update) | async-done | bytes 1179664 | tf_op jit(solution)/shard_map/reduce_scatter | solution.py:88
  3493.5 166.0 %reduce-scatter.39.cloned.1.call-done = f32[256,1152]{1,0:T(8,128)} async-done(((f32[2048,1152]{1,0:T(8,128)}), f32[256,1152]{1,0:T(8,128)}) %reduce-scatter.39.cloned.1.call-update) | async-done | bytes 1179664 | tf_op jit(solution)/shard_map/reduce_scatter | solution.py:88
  3662.8 162.9 %reduce-scatter.43.cloned.1.call-done = f32[256,1152]{1,0:T(8,128)} async-done(((f32[2048,1152]{1,0:T(8,128)}), f32[256,1152]{1,0:T(8,128)}) %reduce-scatter.43.cloned.1.call-update) | async-done | bytes 1179664 | tf_op jit(solution)/shard_map/reduce_scatter | solution.py:88
  3825.7 166.2 %reduce-scatter.47.cloned.1.call-done = f32[256,1152]{1,0:T(8,128)} async-done(((f32[2048,1152]{1,0:T(8,128)}), f32[256,1152]{1,0:T(8,128)}) %reduce-scatter.47.cloned.1.call-update) | async-done | bytes 1179664 | tf_op jit(solution)/shard_map/reduce_scatter | solution.py:88
  4000.0 6.8 all-to-all-done.2
  4027.3 6.7 fusion.141
  4038.0 94.8 %all-reduce.12.cloned.1.call-done = (bf16[1152,864]{0,1:T(8,128)(2,1)}, bf16[1152,432]{0,1:T(8,128)(2,1)}, bf16[144,1152]{1,0:T(8,128)(2,1)}, bf16[1152,576]{0,1...) async-done(((bf16[1152,864]{0,1:T(8,128)(2,1)}, bf16[1152,432]{0,1:T(8,128)(2,1)}, bf16[144,1152]{1,0:T(8,128)(2,1)}, bf16[1152,576]{0,1:T(8,128)(2,1)}, ...) | async-done | bytes 6635536 | tf_op jit(solution)/shard_map/psum | solution.py:396
  4148.7 41.3 psum.147
  4190.0 21.6 psum.154
  4211.6 91.5 %all-reduce.8.cloned.1.call-done = (f32[16,1152]{1,0:T(8,128)}, f32[256,1152]{1,0:T(8,128)}, f32[1152,1152]{1,0:T(8,128)}, f32[1152,16]{0,1:T(8,128)}) async-done(((f32[16,1152]{1,0:T(8,128)}, f32[256,1152]{1,0:T(8,128)}, f32[1152,1152]{1,0:T(8,128)}, f32[1152,16]{0,1:T(8,128)}), (f32[16,1152]{1,0:T(8,128)}, f32[256,1152]{1,0:T(8,128)}, f32[1152,1152]{1,0:T(8,128)}, ...) | async-done | bytes 6635536 | tf_op jit(solution)/shard_map/psum | solution.py:392
  4314.6 6.1 multiply_reduce_fusion.2
  4342.1 36.9 all-reduce.1
  4392.0 6.4 multiply_subtract_fusion
  4421.4 65.4 %all-reduce.10.cloned.1.call-done = (bf16[6]{0:T(256)(128)(2,1)}, bf16[12944]{0:T(1024)(128)(2,1)}, bf16[23056]{0:T(1024)(128)(2,1)}) async-done(((bf16[6]{0:T(256)(128)(2,1)}, bf16[12944]{0:T(1024)(128)(2,1)}, bf16[23056]{0:T(1024)(128)(2,1)}), (bf16[6]{0:T(256)(128)(2,1)}, bf16[12944]{0:T(1024)(128)(2,1)}, bf16[23056]{0:T(1024)(128)(2,1)})) %all-reduce.10.cloned.1.call-update) | async-done | bytes 72028 | tf_op jit(solution)/shard_map/psum | solution.py:520
  (1171 shorter events, 447.6 us)
Async XLA Ops:
  19.7 18.0 all-to-all-start
  27.0 94.4 %all-gather.17.cloned.1.call-start = ((), (), s32[]{:S(2)}) async-start(), calls=%async_computation.20 | async-start | bytes 5308416 | tf_op jit(solution)/shard_map/all_gather | solution.py:76
  37.4 491.4 %copy-start.10 = (f32[256,1152]{1,0:T(8,128)}, f32[256,1152]{1,0:T(8,128)S(1)}, u32[]{:S(2)}) copy-start(f32[256,1152]{1,0:T(8,128)S(1)} %get-tuple-element.280) | copy-start | bytes 3538948
  38.8 491.7 %copy-start.182 = (f32[1152]{0:T(1024)}, f32[1152]{0:T(1024)S(1)}, u32[]{:S(2)}) copy-start(f32[1152]{0:T(1024)S(1)} %get-tuple-element.121) | copy-start | bytes 13828
  39.9 162.2 %all-gather.21.cloned.1.call-start = ((), (), s32[]{:S(2)}) async-start(), calls=%async_computation.24 | async-start | bytes 5308416 | tf_op jit(solution)/shard_map/all_gather | solution.py:76
  41.7 653.0 %copy-start.12 = (f32[256,1152]{1,0:T(8,128)}, f32[256,1152]{1,0:T(8,128)S(1)}, u32[]{:S(2)}) copy-start(f32[256,1152]{1,0:T(8,128)S(1)} %get-tuple-element.286) | copy-start | bytes 3538948
  42.8 653.8 %copy-start.180 = (f32[1152]{0:T(1024)}, f32[1152]{0:T(1024)S(1)}, u32[]{:S(2)}) copy-start(f32[1152]{0:T(1024)S(1)} %get-tuple-element.115) | copy-start | bytes 13828
  43.9 239.1 %all-gather.25.cloned.1.call-start = ((), (), s32[]{:S(2)}) async-start(), calls=%async_computation.28 | async-start | bytes 5308416 | tf_op jit(solution)/shard_map/all_gather | solution.py:76
  47.8 813.0 %copy-start.188 = (f32[1152]{0:T(1024)}, f32[1152]{0:T(1024)S(1)}, u32[]{:S(2)}) copy-start(f32[1152]{0:T(1024)S(1)} %get-tuple-element.112) | copy-start | bytes 13828
  47.8 814.8 %copy-start.178 = (f32[1152]{0:T(1024)}, f32[1152]{0:T(1024)S(1)}, u32[]{:S(2)}) copy-start(f32[1152]{0:T(1024)S(1)} %get-tuple-element.109) | copy-start | bytes 13828
  50.3 313.5 %all-gather.29.cloned.1.call-start = ((), (), s32[]{:S(2)}) async-start(), calls=%async_computation.32 | async-start | bytes 5308416 | tf_op jit(solution)/shard_map/all_gather | solution.py:76
  54.1 972.7 %copy-start.186 = (f32[1152]{0:T(1024)}, f32[1152]{0:T(1024)S(1)}, u32[]{:S(2)}) copy-start(f32[1152]{0:T(1024)S(1)} %get-tuple-element.106) | copy-start | bytes 13828
  54.2 974.5 %copy-start.176 = (f32[1152]{0:T(1024)}, f32[1152]{0:T(1024)S(1)}, u32[]{:S(2)}) copy-start(f32[1152]{0:T(1024)S(1)} %get-tuple-element.103) | copy-start | bytes 13828
  56.5 472.2 %reduce-scatter.17.cloned.1.call-start = ((), (), s32[]{:S(2)}) async-start(), calls=%async_computation.21 | async-start | bytes 10616832 | tf_op jit(solution)/shard_map/reduce_scatter | solution.py:80
  57.0 317.6 %copy-start.51 = (bf16[144,1152]{1,0:T(8,128)(2,1)}, bf16[144,1152]{1,0:T(8,128)(2,1)S(1)}, u32[]{:S(2)}) copy-start(bf16[144,1152]{1,0:T(8,128)(2,1)S(1)} %convert_element_type.399) | copy-start | bytes 995332
  137.2 557.6 %reduce-scatter.21.cloned.1.call-start = ((), (), s32[]{:S(2)}) async-start(), calls=%async_computation.25 | async-start | bytes 10616832 | tf_op jit(solution)/shard_map/reduce_scatter | solution.py:80
  218.0 642.8 %reduce-scatter.25.cloned.1.call-start = ((), (), s32[]{:S(2)}) async-start(), calls=%async_computation.29 | async-start | bytes 10616832 | tf_op jit(solution)/shard_map/reduce_scatter | solution.py:80
  299.0 727.9 %reduce-scatter.29.cloned.1.call-start = ((), (), s32[]{:S(2)}) async-start(), calls=%async_computation.33 | async-start | bytes 10616832 | tf_op jit(solution)/shard_map/reduce_scatter | solution.py:80
  379.9 728.7 %all-gather.19.cloned.1.call-start = ((), (), s32[]{:S(2)}) async-start(), calls=%async_computation.22 | async-start | bytes 5308416 | tf_op jit(solution)/shard_map/all_gather | solution.py:76
  532.4 656.9 %all-gather.23.cloned.1.call-start = ((), (), s32[]{:S(2)}) async-start(), calls=%async_computation.26 | async-start | bytes 5308416 | tf_op jit(solution)/shard_map/all_gather | solution.py:76
  698.5 571.6 %all-gather.27.cloned.1.call-start = ((), (), s32[]{:S(2)}) async-start(), calls=%async_computation.30 | async-start | bytes 5308416 | tf_op jit(solution)/shard_map/all_gather | solution.py:76
  864.4 486.3 %all-gather.31.cloned.1.call-start = ((), (), s32[]{:S(2)}) async-start(), calls=%async_computation.34 | async-start | bytes 5308416 | tf_op jit(solution)/shard_map/all_gather | solution.py:76
  1029.8 487.7 %reduce-scatter.19.cloned.1.call-start = ((), (), s32[]{:S(2)}) async-start(), calls=%async_computation.23 | async-start | bytes 10616832 | tf_op jit(solution)/shard_map/reduce_scatter | solution.py:80
  1032.6 318.2 %copy-start.126 = (bf16[1152,576]{0,1:T(8,128)(2,1)}, bf16[1152,576]{0,1:T(8,128)(2,1)S(1)}, u32[]{:S(2)}) copy-start(bf16[1152,576]{0,1:T(8,128)(2,1)S(1)} %convert_element_type.401) | copy-start | bytes 3981316
  1122.9 560.6 %reduce-scatter.23.cloned.1.call-start = ((), (), s32[]{:S(2)}) async-start(), calls=%async_computation.27 | async-start | bytes 10616832 | tf_op jit(solution)/shard_map/reduce_scatter | solution.py:80
  1203.6 645.9 %reduce-scatter.27.cloned.1.call-start = ((), (), s32[]{:S(2)}) async-start(), calls=%async_computation.31 | async-start | bytes 10616832 | tf_op jit(solution)/shard_map/reduce_scatter | solution.py:80
  1284.4 731.2 %reduce-scatter.31.cloned.1.call-start = ((), (), s32[]{:S(2)}) async-start(), calls=%async_computation.35 | async-start | bytes 10616832 | tf_op jit(solution)/shard_map/reduce_scatter | solution.py:80
  1368.3 10.4 all-to-all-start.1
  1371.6 725.5 %all-gather.33.cloned.1.call-start = ((), (), s32[]{:S(2)}) async-start(), calls=%async_computation.36 | async-start | bytes 5308416 | tf_op jit(solution)/shard_map/all_gather | solution.py:84
  1524.9 652.9 %all-gather.37.cloned.1.call-start = ((), (), s32[]{:S(2)}) async-start(), calls=%async_computation.40 | async-start | bytes 5308416 | tf_op jit(solution)/shard_map/all_gather | solution.py:84
  1690.7 567.9 %all-gather.41.cloned.1.call-start = ((), (), s32[]{:S(2)}) async-start(), calls=%async_computation.44 | async-start | bytes 5308416 | tf_op jit(solution)/shard_map/all_gather | solution.py:84
  1856.7 482.6 %all-gather.45.cloned.1.call-start = ((), (), s32[]{:S(2)}) async-start(), calls=%async_computation.48 | async-start | bytes 5308416 | tf_op jit(solution)/shard_map/all_gather | solution.py:84
  2022.7 481.8 %reduce-scatter.33.cloned.1.call-start = ((), (), s32[]{:S(2)}) async-start(), calls=%async_computation.37 | async-start | bytes 10616832 | tf_op jit(solution)/shard_map/reduce_scatter | solution.py:88
  2114.9 555.8 %reduce-scatter.37.cloned.1.call-start = ((), (), s32[]{:S(2)}) async-start(), calls=%async_computation.41 | async-start | bytes 10616832 | tf_op jit(solution)/shard_map/reduce_scatter | solution.py:88
  2195.6 641.3 %reduce-scatter.41.cloned.1.call-start = ((), (), s32[]{:S(2)}) async-start(), calls=%async_computation.45 | async-start | bytes 10616832 | tf_op jit(solution)/shard_map/reduce_scatter | solution.py:88
  2276.4 726.4 %reduce-scatter.45.cloned.1.call-start = ((), (), s32[]{:S(2)}) async-start(), calls=%async_computation.49 | async-start | bytes 10616832 | tf_op jit(solution)/shard_map/reduce_scatter | solution.py:88
  2357.1 727.6 %all-gather.35.cloned.1.call-start = ((), (), s32[]{:S(2)}) async-start(), calls=%async_computation.38 | async-start | bytes 5308416 | tf_op jit(solution)/shard_map/all_gather | solution.py:84
  2513.0 652.3 %all-gather.39.cloned.1.call-start = ((), (), s32[]{:S(2)}) async-start(), calls=%async_computation.42 | async-start | bytes 5308416 | tf_op jit(solution)/shard_map/all_gather | solution.py:84
  2679.2 566.8 %all-gather.43.cloned.1.call-start = ((), (), s32[]{:S(2)}) async-start(), calls=%async_computation.46 | async-start | bytes 5308416 | tf_op jit(solution)/shard_map/all_gather | solution.py:84
  2844.0 482.8 %all-gather.47.cloned.1.call-start = ((), (), s32[]{:S(2)}) async-start(), calls=%async_computation.50 | async-start | bytes 5308416 | tf_op jit(solution)/shard_map/all_gather | solution.py:84
  3008.5 485.0 %reduce-scatter.35.cloned.1.call-start = ((), (), s32[]{:S(2)}) async-start(), calls=%async_computation.39 | async-start | bytes 10616832 | tf_op jit(solution)/shard_map/reduce_scatter | solution.py:88
  3100.9 558.6 %reduce-scatter.39.cloned.1.call-start = ((), (), s32[]{:S(2)}) async-start(), calls=%async_computation.43 | async-start | bytes 10616832 | tf_op jit(solution)/shard_map/reduce_scatter | solution.py:88
  3181.6 644.1 %reduce-scatter.43.cloned.1.call-start = ((), (), s32[]{:S(2)}) async-start(), calls=%async_computation.47 | async-start | bytes 10616832 | tf_op jit(solution)/shard_map/reduce_scatter | solution.py:88
  3262.3 729.6 %reduce-scatter.47.cloned.1.call-start = ((), (), s32[]{:S(2)}) async-start(), calls=%async_computation.51 | async-start | bytes 10616832 | tf_op jit(solution)/shard_map/reduce_scatter | solution.py:88
  3345.0 10.6 all-to-all-start.3
  3417.0 242.5 %copy-start.11 = (f32[256,1152]{1,0:T(8,128)S(1)}, f32[256,1152]{1,0:T(8,128)}, u32[]{:S(2)}) copy-start(f32[256,1152]{1,0:T(8,128)} %copy-done.10) | copy-start | bytes 3538948
  3417.0 242.5 %copy-start.13 = (f32[256,1152]{1,0:T(8,128)S(1)}, f32[256,1152]{1,0:T(8,128)}, u32[]{:S(2)}) copy-start(f32[256,1152]{1,0:T(8,128)} %copy-done.12) | copy-start | bytes 3538948
  3417.0 242.5 %copy-start.169 = (f32[1152]{0:T(1024)S(1)}, f32[1152]{0:T(1024)}, u32[]{:S(2)}) copy-start(f32[1152]{0:T(1024)} %copy-done.168) | copy-start | bytes 13828
  3417.0 242.5 %copy-start.171 = (f32[1152]{0:T(1024)S(1)}, f32[1152]{0:T(1024)}, u32[]{:S(2)}) copy-start(f32[1152]{0:T(1024)} %copy-done.170) | copy-start | bytes 13828
  3417.0 242.5 %copy-start.219 = (f32[256]{0:T(256)S(1)}, f32[256]{0:T(256)}, u32[]{:S(2)}) copy-start(f32[256]{0:T(256)} %copy-done.218) | copy-start | bytes 3076
  3417.0 242.5 %copy-start.221 = (f32[256]{0:T(256)S(1)}, f32[256]{0:T(256)}, u32[]{:S(2)}) copy-start(f32[256]{0:T(256)} %copy-done.220) | copy-start | bytes 3076
  3417.0 242.5 %copy-start.235 = (f32[256]{0:T(256)S(1)}, f32[256]{0:T(256)}, u32[]{:S(2)}) copy-start(f32[256]{0:T(256)} %copy-done.234) | copy-start | bytes 3076
  3417.1 242.5 %copy-start.237 = (f32[256]{0:T(256)S(1)}, f32[256]{0:T(256)}, u32[]{:S(2)}) copy-start(f32[256]{0:T(256)} %copy-done.236) | copy-start | bytes 3076
  3420.5 571.4 %copy-start.173 = (f32[1152]{0:T(1024)S(1)}, f32[1152]{0:T(1024)}, u32[]{:S(2)}) copy-start(f32[1152]{0:T(1024)} %copy-done.172) | copy-start | bytes 13828
  3420.5 571.4 %copy-start.175 = (f32[1152]{0:T(1024)S(1)}, f32[1152]{0:T(1024)}, u32[]{:S(2)}) copy-start(f32[1152]{0:T(1024)} %copy-done.174) | copy-start | bytes 13828
  3420.5 571.4 %copy-start.223 = (f32[256]{0:T(256)S(1)}, f32[256]{0:T(256)}, u32[]{:S(2)}) copy-start(f32[256]{0:T(256)} %copy-done.222) | copy-start | bytes 3076
  3420.5 571.4 %copy-start.225 = (f32[256]{0:T(256)S(1)}, f32[256]{0:T(256)}, u32[]{:S(2)}) copy-start(f32[256]{0:T(256)} %copy-done.224) | copy-start | bytes 3076
  3420.5 571.4 %copy-start.239 = (f32[256]{0:T(256)S(1)}, f32[256]{0:T(256)}, u32[]{:S(2)}) copy-start(f32[256]{0:T(256)} %copy-done.238) | copy-start | bytes 3076
  3420.5 571.4 %copy-start.241 = (f32[256]{0:T(256)S(1)}, f32[256]{0:T(256)}, u32[]{:S(2)}) copy-start(f32[256]{0:T(256)} %copy-done.240) | copy-start | bytes 3076
  3996.2 10.6 all-to-all-start.2
  3999.9 132.8 %all-reduce.12.cloned.1.call-start = ((), (), s32[]{:S(2)}) async-start(), calls=%async_computation.54 | async-start | bytes 13271040 | tf_op jit(solution)/shard_map/psum | solution.py:396
  4008.9 294.2 %all-reduce.8.cloned.1.call-start = ((), (), s32[]{:S(2)}) async-start(), calls=%async_computation.52 | async-start | bytes 13271040 | tf_op jit(solution)/shard_map/psum | solution.py:392
  4034.1 452.7 %all-reduce.10.cloned.1.call-start = ((), (), s32[]{:S(2)}) async-start(), calls=%async_computation.53 | async-start | bytes 148480 | tf_op jit(solution)/shard_map/psum | solution.py:520
  4314.1 182.8 %copy-start.141 = (f32[1152,16]{0,1:T(8,128)}, f32[1152,16]{0,1:T(8,128)S(1)}, u32[]{:S(2)}) copy-start(f32[1152,16]{0,1:T(8,128)S(1)} %get-tuple-element.166) | copy-start | bytes 221188
  (308 other events, 7052.5 us)
Sparse Core Ops, SparseCore 0:
  40.1 81.2 all-gather.16
  124.1 78.0 all-gather.20
  204.9 78.0 all-gather.24
  285.7 78.0 all-gather.28
  367.2 161.5 reduce-scatter.16
  532.2 162.5 reduce-scatter.20
  698.4 162.3 reduce-scatter.24
  864.4 162.3 reduce-scatter.28
  1029.6 78.9 all-gather.18
  1111.2 78.0 all-gather.22
  1192.0 78.0 all-gather.26
  1272.7 78.0 all-gather.30
  1354.3 163.0 reduce-scatter.18
  1520.9 162.5 reduce-scatter.22
  1686.9 162.5 reduce-scatter.26
  1852.9 162.5 reduce-scatter.30
  2018.1 78.9 all-gather.32
  2099.7 78.0 all-gather.36
  2180.6 78.0 all-gather.40
  2261.2 78.0 all-gather.44
  2342.9 161.5 reduce-scatter.32
  2508.1 162.5 reduce-scatter.36
  2674.3 162.5 reduce-scatter.40
  2840.3 162.5 reduce-scatter.44
  3005.6 78.9 all-gather.34
  3087.3 78.0 all-gather.38
  3167.9 78.0 all-gather.42
  3248.7 78.0 all-gather.46
  3330.4 163.0 reduce-scatter.34
  3496.9 162.5 reduce-scatter.38
  3663.1 162.5 reduce-scatter.42
  3829.3 162.5 reduce-scatter.46
  4009.0 123.7 all-reduce.11
  4140.8 162.1 all-reduce.7
  4420.1 66.6 all-reduce.9
where the time goes:
time: 4540 us; the launch traced here: 4530 us
  waiting for transfers between devices  3760 us (83%)
  matrix products  328 us (7%)
  other arithmetic  184 us (4%)
  blocking collectives  99.7 us (2%)
  local copies, waits for them, and re-layouts  77.6 us (2%)
  between operations  52.2 us (1%)
    reduce_scatter x8, waiting for transfers between devices, rows_out(): return lax.psum_scatter(values, 'mp', scatter_dimension=0, tiled=True)  1250 us
    reduce_scatter x8, waiting for transfers between devices, grads_out(): return lax.psum_scatter(values, 'mp', scatter_dimension=0, tiled=True)  1190 us
    all_gather x8, waiting for transfers between devices, grads_in(): return lax.all_gather(values, 'mp', axis=0, tiled=True)  529 us
    all_gather x8, waiting for transfers between devices, rows_in(): return lax.all_gather(values, 'mp', axis=0, tiled=True)  528 us
    dot_general x22, matrix products, product_right(): lax.dot_general(operand, other_operand, (((1,), (1,)), ((), ())), preferr...  109 us
    dot_general x26, matrix products, product(): return jnp.dot(operand, other_operand, preferred_element_type=jnp.float32)  101 us
    psum x1, waiting for transfers between devices, body(): lax.psum(modulator_grad.astype(jnp.bfloat16), 'dp').astype(jnp.float32)  94.8 us
    psum x1, waiting for transfers between devices, body(): lax.psum((embed_running, time_first_grad, time_second_grad, readout_runni...  91.5 us
  transfers between devices with their start and end apart: 39, of which 38 were waited for; matrix products, arithmetic and copies ran while one was open for 9% of the time, Pallas kernels for 0%

commit v1 on v0

v1 whole, which is shorter than its diff:
```python
import math

import jax
import jax.numpy as jnp
from jax import lax
from jax.sharding import PartitionSpec as P

HD = 72
FREQ = 256
PIN = 16
SIDE = 16


eps_norm = 1e-06
eps_factor = 1e-30
clip_limit = 0.005
state_decay = 0.5
step_rate = 1.5
neg_large = -1e30
highest = lax.Precision.HIGHEST


def product(operand, other_operand):
    return jnp.dot(operand, other_operand, preferred_element_type=jnp.float32)


def product_right(operand, other_operand):
    return lax.dot_general(
        operand, other_operand, (((1,), (1,)), ((), ())), preferred_element_type=jnp.float32
    )


def product_left(operand, other_operand):
    return lax.dot_general(
        operand, other_operand, (((0,), (0,)), ((), ())), preferred_element_type=jnp.float32
    )


def layer_norm(values):
    center = values - jnp.mean(values, axis=-1, keepdims=True)
    return center * lax.rsqrt(jnp.mean(center * center, axis=-1, keepdims=True) + eps_norm)


def norm_back(values, upstream):
    center = values - jnp.mean(values, axis=-1, keepdims=True)
    inverse = lax.rsqrt(jnp.mean(center * center, axis=-1, keepdims=True) + eps_norm)
    normed = center * inverse
    return inverse * (
        upstream
        - jnp.mean(upstream, axis=-1, keepdims=True)
        - normed * jnp.mean(upstream * normed, axis=-1, keepdims=True)
    )


def position_table(side, width):
    quarter = width // 4
    omega = jnp.exp(-math.log(10000.0) * jnp.arange(quarter, dtype=jnp.float32) / quarter)
    place = jnp.arange(side * side)
    column = (place % side).astype(jnp.float32)[:, None] * omega[None, :]
    row_angle = (place // side).astype(jnp.float32)[:, None] * omega[None, :]
    return jnp.concatenate(
        [jnp.sin(column), jnp.cos(column), jnp.sin(row_angle), jnp.cos(row_angle)], axis=1
    )


def time_features(steps, width):
    half = width // 2
    freq = jnp.exp(-math.log(10000.0) * jnp.arange(half, dtype=jnp.float32) / half)
    angle = steps.astype(jnp.float32)[:, None] * freq[None, :]
    return jnp.concatenate([jnp.cos(angle), jnp.sin(angle)], axis=1)


def across(values, axes):
    return lax.all_gather(values, axes, axis=0, tiled=True)


def gather_weight(piece):
    return across(piece, ("dp", "mp"))


def reduce_weight(partial):
    piece = lax.psum_scatter(partial, ("dp", "mp"), scatter_dimension=0, tiled=True)
    return across(piece, "dp")


def body(
    latents,
    noise_draw,
    alpha_bar,
    timesteps,
    labels,
    lengths,
    class_vectors,
    embedder,
    time_first,
    time_second,
    modulator,
    mixer_input,
    mixer_output,
    expander,
    contractor,
    finisher,
    readout,
    row_states,
    column_states,
):
    copies = lax.axis_size("dp")
    groups = lax.axis_size("mp")
    copy = lax.axis_index("dp")
    member = lax.axis_index("mp")
    width = embedder.shape[1]
    patches = SIDE * SIDE
    images = latents.shape[0]
    rows = images * patches
    heads = width // HD
    heads_here = mixer_input.shape[1] // (3 * HD)
    hidden_here = expander.shape[1]
    valid_total = jnp.sum(lengths).astype(jnp.float32) * PIN
    own_lengths = lax.dynamic_slice_in_dim(lengths, (copy * groups + member) * images, images)
    own_alpha = lax.dynamic_slice_in_dim(alpha_bar, member * images, images)

    mixer_rows = (
        mixer_input.astype(jnp.bfloat16)
        .T.reshape(heads_here, 3, HD, width)
        .transpose(1, 0, 2, 3)
        .reshape(3 * heads_here * HD, width)
    )
    shards = (
        jnp.concatenate([mixer_rows, mixer_output.astype(jnp.bfloat16)], axis=0),
        expander.astype(jnp.bfloat16).T,
        contractor.astype(jnp.bfloat16),
    )
    gathered = []
    for shard in shards:
        piece_rows = shard.shape[0] // copies
        piece = lax.dynamic_slice_in_dim(shard, copy * piece_rows, piece_rows)
        gathered.append(gather_weight(piece))
    parts = copies // 4
    piece_rows = shards[0].shape[0] // copies
    mixer_all = (
        gathered[0]
        .reshape(4, parts, groups, piece_rows, width)
        .transpose(0, 2, 1, 3, 4)
        .reshape(4 * width, width)
    )
    inputs_use = mixer_all[: 3 * width]
    outputs_use = mixer_all[3 * width :]
    expand_use = gathered[1]
    contract_use = gathered[2]

    features = time_features(timesteps, FREQ)
    class_rows = jnp.take(class_vectors, labels, axis=0).astype(jnp.float32)
    hidden_pre = jnp.dot(features, time_first, precision=highest)
    condition = jnp.dot(jax.nn.silu(hidden_pre), time_second, precision=highest) + class_rows
    signal = jax.nn.silu(condition).astype(jnp.bfloat16)
    modulator_low = modulator.astype(jnp.bfloat16)
    finisher_low = finisher.astype(jnp.bfloat16)
    steer_part = product(signal, modulator_low).astype(jnp.bfloat16)
    final_part = product(signal, finisher_low).astype(jnp.bfloat16)
    steer_own = lax.all_to_all(steer_part, "mp", split_axis=0, concat_axis=1, tiled=True)
    final_own = lax.all_to_all(final_part, "mp", split_axis=0, concat_axis=1, tiled=True)
    steering = steer_own.astype(jnp.float32).reshape(images, 6, 1, width)
    final_steer = final_own.astype(jnp.float32).reshape(images, 2, 1, width)
    features_all = time_features(across(timesteps, "dp"), FREQ)
    hidden_pre_all = across(hidden_pre, "dp")
    condition_all = across(condition, "dp")
    signal_all = across(signal, "dp")

    embedder_low = embedder.astype(jnp.bfloat16)
    readout_low = readout.astype(jnp.bfloat16)
    place = jnp.arange(patches)
    live = place[None, :] < own_lengths[:, None]
    root_keep = jnp.sqrt(own_alpha)[:, None, None]
    root_noise = jnp.sqrt(1.0 - own_alpha)[:, None, None]
    noisy = (root_keep * latents + root_noise * noise_draw).astype(jnp.bfloat16).reshape(rows, PIN)
    target = (root_keep * noise_draw - root_noise * latents).reshape(rows, PIN)
    residual_zero = (
        product(noisy, embedder_low).reshape(images, patches, width)
        + position_table(SIDE, width)[None]
    )
    normed_one = layer_norm(residual_zero)
    input_one = (
        (normed_one * (1.0 + steering[:, 1]) + steering[:, 0])
        .astype(jnp.bfloat16)
        .reshape(rows, width)
    )
    qkv = product_right(input_one, inputs_use).astype(jnp.bfloat16)
    qkv = qkv.reshape(images, patches, 3, heads, HD)
    queries, key_part, value_part = qkv[:, :, 0], qkv[:, :, 1], qkv[:, :, 2]
    scores = (
        jnp.einsum("gqhe,gkhe->ghqk", queries, key_part, preferred_element_type=jnp.float32)
        * HD ** (-0.5)
    )
    scores = jnp.where(live[:, None, None, :], scores, neg_large)
    peak = jnp.max(scores, axis=-1, keepdims=True)
    exponent = jnp.exp(scores - peak)
    attend = exponent / jnp.sum(exponent, axis=-1, keepdims=True)
    mixed = jnp.einsum(
        "ghqk,gkhe->gqhe",
        attend.astype(jnp.bfloat16),
        value_part,
        preferred_element_type=jnp.float32,
    )
    mixed = mixed.astype(jnp.bfloat16).reshape(rows, width)
    branch_one = product(mixed, outputs_use).reshape(images, patches, width)
    residual_one = residual_zero + steering[:, 2] * branch_one
    normed_two = layer_norm(residual_one)
    input_two = (
        (normed_two * (1.0 + steering[:, 4]) + steering[:, 3])
        .astype(jnp.bfloat16)
        .reshape(rows, width)
    )
    pre_active = product_right(input_two, expand_use)
    active = jax.nn.gelu(pre_active, approximate=True).astype(jnp.bfloat16)
    branch_two = product(active, contract_use).reshape(images, patches, width)
    residual_two = residual_one + steering[:, 5] * branch_two
    normed_final = layer_norm(residual_two)
    input_final = (
        (normed_final * (1.0 + final_steer[:, 1]) + final_steer[:, 0])
        .astype(jnp.bfloat16)
        .reshape(rows, width)
    )
    misfit = product(input_final, readout_low) - target
    live_rows = live.reshape(rows, 1)
    loss_part = jnp.sum(jnp.where(live_rows, misfit * misfit, 0.0))

    output_grad = jnp.where(live_rows, 2.0 * misfit / valid_total, 0.0).astype(jnp.bfloat16)
    readout_part = product_left(input_final, output_grad)
    final_grad = product_right(output_grad, readout_low).reshape(images, patches, width)
    final_shift_grad = jnp.sum(final_grad, axis=1)
    final_scale_grad = jnp.sum(final_grad * normed_final, axis=1)
    grad_residual = norm_back(residual_two, final_grad * (1.0 + final_steer[:, 1]))
    gate_two_grad = jnp.sum(grad_residual * branch_two, axis=1)
    branch_two_grad = (steering[:, 5] * grad_residual).astype(jnp.bfloat16).reshape(rows, width)
    contract_part = product_left(active, branch_two_grad).astype(jnp.bfloat16)
    active_grad = product_right(branch_two_grad, contract_use)
    gelu_pull = jax.vjp(lambda inner: jax.nn.gelu(inner, approximate=True), pre_active)[1]
    pre_grad = gelu_pull(active_grad)[0].astype(jnp.bfloat16)
    expand_part = product_left(pre_grad, input_two).astype(jnp.bfloat16)
    input_two_grad = product(pre_grad, expand_use).reshape(images, patches, width)
    shift_two_grad = jnp.sum(input_two_grad, axis=1)
    scale_two_grad = jnp.sum(input_two_grad * normed_two, axis=1)
    grad_residual = grad_residual + norm_back(
        residual_one, input_two_grad * (1.0 + steering[:, 4])
    )
    gate_one_grad = jnp.sum(grad_residual * branch_one, axis=1)
    branch_one_grad = (steering[:, 2] * grad_residual).astype(jnp.bfloat16).reshape(rows, width)
    outputs_part = product_left(mixed, branch_one_grad).astype(jnp.bfloat16)
    mixed_grad = (
        product_right(branch_one_grad, outputs_use)
        .astype(jnp.bfloat16)
        .reshape(images, patches, heads, HD)
    )
    attend_grad = jnp.einsum(
        "gqhe,gkhe->ghqk", mixed_grad, value_part, preferred_element_type=jnp.float32
    )
    score_grad = (
        attend * (attend_grad - jnp.sum(attend * attend_grad, axis=-1, keepdims=True))
    ).astype(jnp.bfloat16)
    query_grad = (
        jnp.einsum("ghqk,gkhe->gqhe", score_grad, key_part, preferred_element_type=jnp.float32)
        * HD ** (-0.5)
    )
    key_grad = (
        jnp.einsum("ghqk,gqhe->gkhe", score_grad, queries, preferred_element_type=jnp.float32)
        * HD ** (-0.5)
    )
    value_grad = jnp.einsum(
        "ghqk,gqhe->gkhe",
        attend.astype(jnp.bfloat16),
        mixed_grad,
        preferred_element_type=jnp.float32,
    )
    qkv_grad = (
        jnp.stack([query_grad, key_grad, value_grad], axis=2)
        .astype(jnp.bfloat16)
        .reshape(rows, 3 * width)
    )
    inputs_part = product_left(qkv_grad, input_one).astype(jnp.bfloat16)
    input_one_grad = product(qkv_grad, inputs_use).reshape(images, patches, width)
    shift_one_grad = jnp.sum(input_one_grad, axis=1)
    scale_one_grad = jnp.sum(input_one_grad * normed_one, axis=1)
    grad_residual = grad_residual + norm_back(
        residual_zero, input_one_grad * (1.0 + steering[:, 1])
    )
    embed_part = product_left(noisy, grad_residual.reshape(rows, width).astype(jnp.bfloat16))

    mixer_part = jnp.concatenate([inputs_part, outputs_part], axis=0)
    mixer_part = (
        mixer_part.reshape(4, groups, parts, piece_rows, width)
        .transpose(0, 2, 1, 3, 4)
        .reshape(4 * width, width)
    )
    contract_sum = reduce_weight(contract_part).astype(jnp.float32)
    expand_sum = reduce_weight(expand_part).astype(jnp.float32).T
    mixer_sum = reduce_weight(mixer_part).astype(jnp.float32)
    held = heads_here * HD
    inputs_sum = (
        mixer_sum[: 3 * held]
        .reshape(3, heads_here, HD, width)
        .transpose(1, 0, 2, 3)
        .reshape(3 * held, width)
        .T
    )
    outputs_sum = mixer_sum[3 * held :]

    steer_back = jnp.stack(
        [
            shift_one_grad,
            scale_one_grad,
            gate_one_grad,
            shift_two_grad,
            scale_two_grad,
            gate_two_grad,
        ],
        axis=1,
    )
    steer_back = steer_back.reshape(images, 6 * width).astype(jnp.bfloat16)
    final_back = jnp.stack([final_shift_grad, final_scale_grad], axis=1)
    final_back = final_back.reshape(images, 2 * width).astype(jnp.bfloat16)
    steer_cols = lax.all_to_all(steer_back, "mp", split_axis=1, concat_axis=0, tiled=True)
    final_cols = lax.all_to_all(final_back, "mp", split_axis=1, concat_axis=0, tiled=True)
    signal_grad = product_right(steer_cols, modulator_low) + product_right(final_cols, finisher_low)
    signal_grad = across(lax.psum(signal_grad, "mp"), "dp")
    modulator_sum = product_left(signal_all, across(steer_cols, "dp"))
    finisher_sum = product_left(signal_all, across(final_cols, "dp"))
    hidden_all, hidden_pull = jax.vjp(jax.nn.silu, hidden_pre_all)
    condition_grad = jax.vjp(jax.nn.silu, condition_all)[1](signal_grad)[0]
    time_second_sum = lax.dot_general(
        hidden_all, condition_grad, (((0,), (0,)), ((), ())), precision=highest
    )
    hidden_grad = hidden_pull(
        lax.dot_general(condition_grad, time_second, (((1,), (1,)), ((), ())), precision=highest)
    )[0]
    time_first_sum = lax.dot_general(
        features_all, hidden_grad, (((0,), (0,)), ((), ())), precision=highest
    )
    embed_sum, readout_sum, loss_sum = lax.psum((embed_part, readout_part, loss_part), ("dp", "mp"))

    gradients = (
        embed_sum,
        time_first_sum,
        time_second_sum,
        modulator_sum,
        inputs_sum,
        outputs_sum,
        expand_sum,
        contract_sum,
        finisher_sum,
        readout_sum,
    )
    weights = (
        embedder,
        time_first,
        time_second,
        modulator,
        mixer_input,
        mixer_output,
        expander,
        contractor,
        finisher,
        readout,
    )
    layouts = (
        "whole",
        "whole",
        "whole",
        "columns",
        "columns",
        "rows",
        "columns",
        "rows",
        "columns",
        "whole",
    )
    row_squares = [jnp.sum(gradient * gradient, axis=1) for gradient in gradients]
    column_squares = [jnp.sum(gradient * gradient, axis=0) for gradient in gradients]
    split_slots = [slot for slot in range(10) if layouts[slot] != "whole"]
    local_square = sum(jnp.sum(row_squares[slot]) for slot in range(10) if slot not in split_slots)
    split_square = sum(jnp.sum(row_squares[slot]) for slot in split_slots)
    crossing = [
        row_squares[slot] if layouts[slot] == "columns" else column_squares[slot]
        for slot in split_slots
    ]
    lengths_out = [part.shape[0] for part in crossing]
    crossed = lax.psum(jnp.concatenate(crossing + [split_square[None]]), "mp")
    grad_norm = jnp.sqrt(crossed[-1] + local_square)
    factor = clip_limit / jnp.maximum(grad_norm, clip_limit)
    factor_square = factor * factor
    start = 0
    for slot, length in zip(split_slots, lengths_out):
        part = crossed[start : start + length]
        start += length
        if layouts[slot] == "columns":
            row_squares[slot] = part
        else:
            column_squares[slot] = part

    row_at = 0
    column_at = 0
    records = []
    for slot in range(10):
        layout = layouts[slot]
        local_rows, local_cols = weights[slot].shape
        many_rows = local_rows * (groups if layout == "rows" else 1)
        many_cols = local_cols * (groups if layout == "columns" else 1)
        row_mean = row_squares[slot] * factor_square / many_cols + eps_factor
        column_mean = column_squares[slot] * factor_square / many_rows + eps_factor
        row_start = row_at + (member * local_rows if layout == "rows" else 0)
        column_start = column_at + (member * local_cols if layout == "columns" else 0)
        row_old = lax.dynamic_slice_in_dim(row_states, row_start, local_rows)
        column_old = lax.dynamic_slice_in_dim(column_states, column_start, local_cols)
        row_next = state_decay * row_old + (1.0 - state_decay) * row_mean
        column_next = state_decay * column_old + (1.0 - state_decay) * column_mean
        if layout == "rows":
            row_average = state_decay * jnp.mean(row_states[row_at : row_at + many_rows]) + (
                1.0 - state_decay
            ) * jnp.mean(column_mean)
        else:
            row_average = jnp.mean(row_next)
        clipped = gradients[slot] * factor
        update = clipped * lax.rsqrt(row_next[:, None] * column_next[None, :] / row_average)
        records.append(
            (clipped, update, jnp.sum(update * update), row_next, column_next, many_rows, many_cols)
        )
        row_at += many_rows
        column_at += many_cols
    shares = [jnp.stack([records[slot][2] for slot in split_slots])]
    for slot in split_slots:
        shares.append(records[slot][4] if layouts[slot] == "columns" else records[slot][3])
    spread = lax.all_gather(jnp.concatenate(shares), "mp", axis=0)
    energies = jnp.sum(spread[:, : len(split_slots)], axis=0)
    start = len(split_slots)
    next_list = []
    row_list = []
    column_list = []
    for slot in range(10):
        clipped, update, energy, row_next, column_next, many_rows, many_cols = records[slot]
        if layouts[slot] != "whole":
            energy = energies[split_slots.index(slot)]
            length = column_next.shape[0] if layouts[slot] == "columns" else row_next.shape[0]
            joined = spread[:, start : start + length].reshape(-1)
            start += length
            if layouts[slot] == "columns":
                column_next = joined
            else:
                row_next = joined
        scale_down = jnp.maximum(1.0, jnp.sqrt(energy / (many_rows * many_cols)))
        next_list.append(weights[slot] - step_rate / math.sqrt(many_rows) * (update / scale_down))
        row_list.append(row_next)
        column_list.append(column_next)
    return (
        loss_sum,
        valid_total,
        grad_norm,
        *next_list,
        *[record[0] for record in records],
        jnp.concatenate(row_list),
        jnp.concatenate(column_list),
    )


def solution(mesh):
    in_specs = (
        P(("dp", "mp"), None, None),
        P(("dp", "mp"), None, None),
        P("dp"),
        P("dp"),
        P("dp"),
        P(),
        P(),
        P(),
        P(),
        P(),
        P(None, "mp"),
        P(None, "mp"),
        P("mp", None),
        P(None, "mp"),
        P("mp", None),
        P(None, "mp"),
        P(),
        P(),
        P(),
    )
    out_specs = (
        P(),
        P(),
        P(),
        P(),
        P(),
        P(),
        P(None, "mp"),
        P(None, "mp"),
        P("mp", None),
        P(None, "mp"),
        P("mp", None),
        P(None, "mp"),
        P(),
        P(),
        P(),
        P(),
        P(None, "mp"),
        P(None, "mp"),
        P("mp", None),
        P(None, "mp"),
        P("mp", None),
        P(None, "mp"),
        P(),
        P(),
        P(),
    )
    return jax.shard_map(body, mesh=mesh, in_specs=in_specs, out_specs=out_specs, check_vma=False)
```

time: 4540 us -> 1420 us (0.31)
  waiting for transfers between devices: 3760 us -> 616 us
  local copies, waits for them, and re-layouts: 77.6 us -> 138 us
    reduce_scatter x16 -> x3, waiting for transfers between devices: 2440 us -> 332 us  [reduce_weight(): lax.psum_scatter(partial, ('dp', 'mp'), scatter_dimension=0, tiled=True)]
    all_gather x16 -> x6, waiting for transfers between devices: 1060 us -> 89.5 us  [across(): return lax.all_gather(values, axes, axis=0, tiled=True)]
    psum x3 -> x2, waiting for transfers between devices: 252 us -> 120 us  [the longest x1 72.6 us: body(): signal_grad = across(lax.psum(signal_grad, 'mp'), 'dp')]
    unnamed x35 -> x13, waiting for transfers between devices: 0.58 us -> 55.1 us
    dot_general x22 -> x7, matrix products: 109 us -> 75.5 us  [product_right(): lax.dot_general(operand, other_operand, (((1,), (1,)), ((), ())), preferr...]
    dot_general x26 -> x8, matrix products: 101 us -> 73 us  [product(): return jnp.dot(operand, other_operand, preferred_element_type=jnp.float32)]
    psum x3 -> x2, blocking collectives: 99.7 us -> 76.5 us  [the longest x1 39.4 us: body(): lax.psum((embed_part, readout_part, loss_part), ('dp', 'mp'))]
  transfers between devices with their start and end apart: 39 -> 16, of which waited for: 38 -> 13; matrix products, arithmetic and copies ran while one was open for 9% -> 21% of each run, Pallas kernels for 0% -> 0%
where the time goes in v1:
time: 1420 us; the launch traced here: 1410 us
  waiting for transfers between devices  616 us (43%)
  matrix products  284 us (20%)
  other arithmetic  187 us (13%)
  local copies, waits for them, and re-layouts  138 us (10%)
  blocking collectives  123 us (9%)
  between operations  42.7 us (3%)
  starting transfers between devices  21.4 us (2%)
    reduce_scatter x3, waiting for transfers between devices, reduce_weight(): lax.psum_scatter(partial, ('dp', 'mp'), scatter_dimension=0, tiled=True)  332 us
    all_gather x6, waiting for transfers between devices, across(): return lax.all_gather(values, axes, axis=0, tiled=True)  89.5 us
    dot_general x7, matrix products, product_right(): lax.dot_general(operand, other_operand, (((1,), (1,)), ((), ())), preferr...  75.5 us
    dot_general x8, matrix products, product(): return jnp.dot(operand, other_operand, preferred_element_type=jnp.float32)  73 us
    psum x1, waiting for transfers between devices, body(): signal_grad = across(lax.psum(signal_grad, 'mp'), 'dp')  72.6 us
    dot_general x8, matrix products, product_left(): lax.dot_general(operand, other_operand, (((0,), (0,)), ((), ())), preferr...  65.1 us
    unnamed x13, waiting for transfers between devices  55.1 us
    unnamed x291, local copies, waits for them, and re-layouts  48.6 us
  transfers between devices with their start and end apart: 16, of which 13 were waited for; matrix products, arithmetic and copies ran while one was open for 21% of the time, Pallas kernels for 0%

profile of v1, /device:TPU:0, one launch (start us, length us, event | category | flops | bytes accessed | tf_op | source)
XLA Modules:
  0.0 1412.2 jit_solution(1503331910649176412)
XLA Ops:
  20.5 6.1 multiply_convert_fusion.4
  27.6 7.3 all-to-all-start.1
  46.4 6.0 all-to-all-start
  54.0 5.5 all-to-all-done
  60.5 5.8 add_convert_fusion.3
  66.3 38.2 %all-gather.8.cloned.1.call-done = bf16[4608,1152]{1,0:T(8,128)(2,1)} async-done(((bf16[144,1152]{1,0:T(8,128)(2,1)}), bf16[4608,1152]{1,0:T(8,128)(2,1)}) %all-gather.8.cloned.1.call-update) | async-done | bytes 10616848 | tf_op jit(solution)/shard_map/all_gather | solution.py:74
  104.5 15.2 %convolution_convert_fusion.4 = bf16[1024,3456]{1,0:T(8,128)(2,1)} fusion(bf16[1024,1152]{1,0:T(8,128)(2,1)} %bitcast.241, bf16[4608,1152]{1,0:T(8,128)(2,1)} %all-gather.8.cloned.1.call-done), kind=kOutput, calls=%fused_computation.29 | convolution fusion | flops 8157265920 | bytes 17399808 | tf_op jit(solution)/shard_map/dot_general | solution.py:28
  119.7 25.5 %reshape.478 = bf16[4,256,3,16,72]{4,3,2,1,0:T(8,128)(2,1)} reshape(bf16[1024,3456]{1,0:T(8,128)(2,1)} %convolution_convert_fusion.4) | data formatting | bytes 14155776 | tf_op jit(solution)/shard_map/reshape | solution.py:188
  145.2 9.1 fusion.154
  154.3 7.3 copy.177
  161.6 7.1 copy.176
  168.7 7.1 copy.178
  175.8 10.5 fusion.35
  186.2 20.6 %fusion.159 = (f32[4,16,256]{2,1,0:T(8,128)S(1)}, f32[4,16,256,256]{2,3,1,0:T(8,128)}) fusion(f32[4,16,256,256]{2,3,1,0:T(8,128)} %fusion.35, pred[4,256]{1,0:T(4,128)(4,1)S(1)} %iota_compare_fusion), kind=kOutput, calls=%fused_computation.367 | output fusion | flops 25166080 | bytes 33620992 | tf_op jit(solution)/shard_map/sub | solution.py:196
  206.8 8.3 fusion.54
  215.1 8.2 fusion.153
  228.9 20.5 %fusion.160 = f32[1024,4608]{1,0:T(8,128)} fusion(bf16[1024,1152]{1,0:T(8,128)(2,1)} %bitcast.245, bf16[4608,1152]{1,0:T(8,128)(2,1)} %all-gather.10.cloned.1.call-done), kind=kOutput, calls=%fused_computation.368 | convolution fusion | flops 10871635968 | bytes 31850496 | tf_op jit(solution)/shard_map/dot_general | solution.py:28
  249.4 34.1 %all-gather.12.cloned.1.call-done = bf16[4608,1152]{1,0:T(8,128)(2,1)} async-done(((bf16[144,1152]{1,0:T(8,128)(2,1)}), bf16[4608,1152]{1,0:T(8,128)(2,1)}) %all-gather.12.cloned.1.call-update) | async-done | bytes 10616848 | tf_op jit(solution)/shard_map/all_gather | solution.py:74
  283.5 22.4 %fusion.138 = f32[1024,1152]{1,0:T(8,128)S(1)} fusion(bf16[4608,1152]{1,0:T(8,128)(2,1)} %all-gather.12.cloned.1.call-done, f32[1024,4608]{1,0:T(8,128)} %fusion.160), kind=kOutput, calls=%fused_computation.351 | convolution fusion | flops 10914103296 | bytes 34209792 | tf_op jit(solution)/shard_map/dot_general | solution.py:24
  315.2 7.4 fusion.19
  323.0 4.1 multiply_reduce_fusion.3
  329.7 26.7 %fusion.7 = bf16[1024,4608]{1,0:T(8,128)(2,1)S(1)} fusion(f32[1024,4608]{1,0:T(8,128)} %fusion.160, bf16[1024,1152]{1,0:T(8,128)(2,1)S(1)} %bitcast.243, bf16[4608,1152]{1,0:T(8,128)(2,1)} %all-gather.12.cloned.1.call-done), kind=kOutput, calls=%fused_computation.12 | convolution fusion | flops 10966007808 | bytes 41287680 | tf_op jit(solution)/shard_map/dot_general | solution.py:28
  356.4 21.7 %fusion.16 = (f32[1024]{0:T(1024)S(1)}, f32[1024,1152]{1,0:T(8,128)}) fusion(f32[4,1152]{1,0:T(4,128)S(1)} %bitcast.254, bf16[1024,4608]{1,0:T(8,128)(2,1)S(1)} %fusion.7, bf16[4608,1152]{1,0:T(8,128)(2,1)} %all-gather.10.cloned.1.call-done), kind=kOutput, calls=%fused_computation.37 | convolution fusion | flops 10873994240 | bytes 24795136 | tf_op jit(solution)/shard_map/dot_general | solution.py:24
  378.2 7.5 fusion.18
  386.1 5.6 multiply_reduce_fusion.4
  395.6 6.6 convolution_convert_fusion.5
  402.2 9.6 reshape.479
  411.7 7.1 copy.143
  418.9 10.7 fusion.46
  429.6 10.7 multiply_reduce_fusion
  440.3 11.8 multiply_convert_fusion.1
  458.8 4.5 convolution_convert_fusion.3
  467.1 11.4 copy.152
  478.5 5.5 copy.180
  484.0 9.7 convolution_convert_fusion.2
  493.7 15.6 %pad_maximum_fusion = bf16[4608,1152]{1,0:T(8,128)(2,1)} fusion(bf16[1152,1152]{1,0:T(8,128)(2,1)S(1)} %copy-done.30, bf16[3456,1152]{1,0:T(8,128)(2,1)S(1)} %convolution_convert_fusion.2), kind=kLoop, calls=%fused_computation.21 | loop fusion | flops 21233664 | bytes 21233664 | tf_op jit(solution)/shard_map/concatenate | solution.py:288
  509.4 18.1 %convolution_convert_fusion.1 = bf16[4608,1152]{1,0:T(8,128)(2,1)} fusion(bf16[1024,4608]{1,0:T(8,128)(2,1)} %copy-done.119, bf16[1024,1152]{1,0:T(8,128)(2,1)} %bitcast.246), kind=kOutput, calls=%fused_computation.5 | convolution fusion | flops 10876944384 | bytes 22413312 | tf_op jit(solution)/shard_map/dot_general | solution.py:34
  531.6 17.6 %multiply_reduce_fusion.2 = (f32[4,256]{1,0:T(4,128)S(1)}, bf16[4,1152]{1,0:T(4,128)(2,1)S(1)}, f32[4,256]{1,0:T(4,128)S(1)}, bf16[4,1152]{1,0:T(4,128)(2,1)S(1)}, f32[4,256,1152]{2,1,0:T(8,128)}) fusion(f32[4,256,1152]{2,1,0:T(8,128)} %copy-done.5, f32[4,1152]{1,0:T(4,128)S(1)} %copy-done.64, f32[4,256]{1,0:T(4,128)S(1)} %copy-done.86, ...), kind=kOutput, calls=%fused_computation.47 | convolution fusion | flops 8164332544 | bytes 24530944 | tf_op jit(solution)/shard_map/dot_general | solution.py:24
  550.3 4.3 fusion.53
  554.7 21.9 %convolution_convert_fusion = bf16[4608,1152]{1,0:T(8,128)(2,1)} fusion(bf16[1024,1152]{1,0:T(8,128)(2,1)} %bitcast.244, f32[1024,4608]{1,0:T(8,128)} %fusion.160), kind=kOutput, calls=%fused_computation.4 | convolution fusion | flops 10919411712 | bytes 31850496 | tf_op jit(solution)/shard_map/dot_general | solution.py:34
  583.1 6.2 all-to-all-done.3
  592.8 6.7 all-to-all-done.2
  603.2 48.6 %reduce-scatter.4.cloned.1.call-done = bf16[144,1152]{1,0:T(8,128)(2,1)} async-done(((bf16[4608,1152]{1,0:T(8,128)(2,1)}), bf16[144,1152]{1,0:T(8,128)(2,1)}) %reduce-scatter.4.cloned.1.call-update) | async-done | bytes 331792 | tf_op jit(solution)/shard_map/reduce_scatter | solution.py:82
  651.9 146.6 %reduce-scatter.6.cloned.1.call-done = bf16[144,1152]{1,0:T(8,128)(2,1)} async-done(((bf16[4608,1152]{1,0:T(8,128)(2,1)}), bf16[144,1152]{1,0:T(8,128)(2,1)}) %reduce-scatter.6.cloned.1.call-update) | async-done | bytes 331792 | tf_op jit(solution)/shard_map/reduce_scatter | solution.py:82
  800.7 4.9 all-reduce
  807.6 5.9 all_gather.48
  813.5 8.1 all_gather.57
  821.7 7.6 all_gather.56
  829.6 39.4 %psum.35 = f32[]{:T(128)} all-reduce(f32[]{:T(128)} %get-tuple-element.182), channel_id=1, replica_groups=mesh['dp'=4,'mp'=8] {'dp','mp'}, use_global_device_ids=true, to_apply=%region_9.10 | all-reduce | flops 1 | bytes 8 | tf_op jit(solution)/shard_map/psum | solution.py:338
  869.0 5.8 all_gather.53
  876.9 47.8 %all-reduce.11.cloned.1.call-done = (f32[16,1152]{1,0:T(8,128)}, f32[1152,16]{0,1:T(8,128)}) async-done(((f32[16,1152]{1,0:T(8,128)}, f32[1152,16]{0,1:T(8,128)}), (f32[16,1152]{1,0:T(8,128)}, f32[1152,16]{0,1:T(8,128)})) %all-reduce.11.cloned.1.call-update) | async-done | bytes 147472 | tf_op jit(solution)/shard_map/psum | solution.py:338
  927.7 6.5 all_gather.49
  937.7 137.1 %reduce-scatter.8.cloned.1.call-done = bf16[144,1152]{1,0:T(8,128)(2,1)} async-done(((bf16[4608,1152]{1,0:T(8,128)(2,1)}), bf16[144,1152]{1,0:T(8,128)(2,1)}) %reduce-scatter.8.cloned.1.call-update) | async-done | bytes 331792 | tf_op jit(solution)/shard_map/reduce_scatter | solution.py:82
  1074.9 72.6 %all-reduce.7.cloned.1.call-done = f32[32,1152]{1,0:T(8,128)} async-done(((f32[32,1152]{1,0:T(8,128)}), f32[32,1152]{1,0:T(8,128)}) %all-reduce.7.cloned.1.call-update) | async-done | bytes 147472 | tf_op jit(solution)/shard_map/psum | solution.py:324
  1147.5 7.9 all_gather.55
  1155.4 7.7 fusion.136
  1167.4 8.8 multiply_reduce_fusion.11
  1190.0 16.4 %all-gather.18.cloned.1.call-done = bf16[576,1152]{1,0:T(8,128)(2,1)} async-done(((bf16[144,1152]{1,0:T(8,128)(2,1)}), bf16[576,1152]{1,0:T(8,128)(2,1)}) %all-gather.18.cloned.1.call-update) | async-done | bytes 1327120 | tf_op jit(solution)/shard_map/all_gather | solution.py:74
  1210.5 37.1 %psum.36 = f32[6913]{0:T(1024)S(1)} all-reduce(f32[6913]{0:T(1024)S(1)} %constant_dynamic-update-slice_fusion.14), channel_id=1, replica_groups=mesh['dp'=4,'mp'=8] {'mp'}, use_global_device_ids=true, to_apply=%region_39.40 | all-reduce | flops 6913 | bytes 55304 | tf_op jit(solution)/shard_map/psum | solution.py:386
  1268.6 6.3 multiply_reduce_fusion.1
  1283.3 6.3 multiply_reduce_fusion.15
  1308.4 6.7 multiply_subtract_fusion
  1316.6 54.9 %all-reduce.9.cloned.1.call-done = f32[23088]{0:T(1024)} async-done(((f32[23088]{0:T(1024)}), f32[23088]{0:T(1024)}) %all-reduce.9.cloned.1.call-update) | async-done | bytes 92368
  1390.6 4.9 multiply_subtract_fusion.3
  (469 shorter events, 165.9 us)
Async XLA Ops:
  7.2 97.3 %all-gather.8.cloned.1.call-start = ((), (), s32[]{:S(2)}) async-start(), calls=%async_computation.7 | async-start | bytes 10948608 | tf_op jit(solution)/shard_map/all_gather | solution.py:74
  14.0 214.9 %all-gather.10.cloned.1.call-start = ((), (), s32[]{:S(2)}) async-start(), calls=%async_computation.8 | async-start | bytes 10948608 | tf_op jit(solution)/shard_map/all_gather | solution.py:74
  15.9 267.6 %all-gather.12.cloned.1.call-start = ((), (), s32[]{:S(2)}) async-start(), calls=%async_computation.9 | async-start | bytes 10948608 | tf_op jit(solution)/shard_map/all_gather | solution.py:74
  20.5 18.2 %copy-start.57 = (f32[16,1152]{1,0:T(8,128)S(1)}, f32[16,1152]{1,0:T(8,128)}, u32[]{:S(2)}) copy-start(f32[16,1152]{1,0:T(8,128)} %param.26) | copy-start | bytes 221188
  27.6 18.8 %all-to-all-start.1 = ((bf16[8,4,288]{2,1,0:T(4,128)(2,1)}), bf16[8,4,288]{2,1,0:T(4,128)(2,1)S(1)}, u32[]{:S(2)}, u32[]{:S(2)}) async-start(bf16[8,4,288]{2,1,0:T(4,128)(2,1)} %all_to_all.46), calls=%async_computation.1 | async-start | bytes 49152 | tf_op jit(solution)/shard_map/all_to_all | solution.py:161
  39.6 20.9 %copy-start.75 = (f32[4,256]{1,0:T(4,128)}, f32[4,256]{1,0:T(4,128)S(1)}, u32[]{:S(2)}) copy-start(f32[4,256]{1,0:T(4,128)S(1)} %broadcast_multiply_fusion.14) | copy-start | bytes 12292
  42.5 23.8 %copy-start.85 = (f32[4,256]{1,0:T(4,128)}, f32[4,256]{1,0:T(4,128)S(1)}, u32[]{:S(2)}) copy-start(f32[4,256]{1,0:T(4,128)S(1)} %add_rsqrt_fusion.2) | copy-start | bytes 12292
  46.4 13.2 all-to-all-start
  52.4 599.4 %reduce-scatter.4.cloned.1.call-start = ((), (), s32[]{:S(2)}) async-start(), calls=%async_computation.10 | async-start | bytes 10948608 | tf_op jit(solution)/shard_map/reduce_scatter | solution.py:82
  60.4 163.5 %copy-start.59 = (f32[4,1,1,1152]{3,0,1,2:T(4,128)}, f32[4,1,1,1152]{3,0,1,2:T(4,128)S(1)}, u32[]{:S(2)}) copy-start(f32[4,1,1,1152]{3,0,1,2:T(4,128)S(1)} %copy.192) | copy-start | bytes 55300
  60.5 154.6 %copy-start.70 = (f32[4,1,1,1152]{3,0,1,2:T(4,128)}, f32[4,1,1,1152]{3,0,1,2:T(4,128)S(1)}, u32[]{:S(2)}) copy-start(f32[4,1,1,1152]{3,0,1,2:T(4,128)S(1)} %copy.195) | copy-start | bytes 55300
  60.5 59.2 %copy-start.63 = (f32[4,1152]{1,0:T(4,128)}, f32[4,1152]{1,0:T(4,128)S(1)}, u32[]{:S(2)}) copy-start(f32[4,1152]{1,0:T(4,128)S(1)} %get-tuple-element.198) | copy-start | bytes 55300
  186.2 28.9 %slice-start.2 = ((s8[4718592]{0:T(1024)(128)(4,1)}), s8[524288]{0:T(1024)(128)(4,1)S(1)}, s32[]{:S(2)}) async-start(s8[4718592]{0:T(1024)(128)(4,1)} %bitcast.219), calls=%async_computation.21 | async-start | bytes 1048576
  224.0 25.4 %copy-start.83 = (f32[4,256]{1,0:T(4,128)}, f32[4,256]{1,0:T(4,128)S(1)}, u32[]{:S(2)}) copy-start(f32[4,256]{1,0:T(4,128)S(1)} %add_rsqrt_fusion.1) | copy-start | bytes 12292
  249.4 56.5 %copy-start.62 = (f32[4,1,1,1152]{3,0,1,2:T(4,128)S(1)}, f32[4,1,1,1152]{3,0,1,2:T(4,128)}, u32[]{:S(2)}) copy-start(f32[4,1,1,1152]{3,0,1,2:T(4,128)} %copy.193) | copy-start | bytes 55300
  283.5 22.4 %copy-start.3 = (f32[4,256,1152]{2,1,0:T(8,128)S(1)}, f32[4,256,1152]{2,1,0:T(8,128)}, u32[]{:S(2)}) copy-start(f32[4,256,1152]{2,1,0:T(8,128)} %copy-done.2) | copy-start | bytes 14155780
  329.6 26.8 %copy-start.37 = (bf16[4,256,1152]{2,1,0:T(8,128)(2,1)}, bf16[4,256,1152]{2,1,0:T(8,128)(2,1)S(1)}, u32[]{:S(2)}) copy-start(bf16[4,256,1152]{2,1,0:T(8,128)(2,1)S(1)} %multiply_convert_fusion.3) | copy-start | bytes 7077892
  329.6 26.8 %copy-start.60 = (f32[4,1,1,1152]{3,0,1,2:T(4,128)S(1)}, f32[4,1,1,1152]{3,0,1,2:T(4,128)}, u32[]{:S(2)}) copy-start(f32[4,1,1,1152]{3,0,1,2:T(4,128)} %copy-done.59) | copy-start | bytes 55300
  356.4 21.7 %copy-start.119 = (bf16[1024,4608]{1,0:T(8,128)(2,1)}, bf16[1024,4608]{1,0:T(8,128)(2,1)S(1)}, u32[]{:S(2)}) copy-start(bf16[1024,4608]{1,0:T(8,128)(2,1)S(1)} %fusion.7) | copy-start | bytes 28311556
  356.4 21.7 %copy-start.67 = (f32[4,256]{1,0:T(4,128)S(1)}, f32[4,256]{1,0:T(4,128)}, u32[]{:S(2)}) copy-start(f32[4,256]{1,0:T(4,128)} %copy-done.66) | copy-start | bytes 12292
  356.4 21.7 %copy-start.84 = (f32[4,256]{1,0:T(4,128)S(1)}, f32[4,256]{1,0:T(4,128)}, u32[]{:S(2)}) copy-start(f32[4,256]{1,0:T(4,128)} %copy-done.83) | copy-start | bytes 12292
  509.3 289.2 %reduce-scatter.6.cloned.1.call-start = ((), (), s32[]{:S(2)}) async-start(), calls=%async_computation.12 | async-start | bytes 10948608 | tf_op jit(solution)/shard_map/reduce_scatter | solution.py:82
  527.6 397.1 %all-reduce.11.cloned.1.call-start = ((), (), s32[]{:S(2)}) async-start(), calls=%async_computation.18 | async-start | bytes 294912 | tf_op jit(solution)/shard_map/psum | solution.py:338
  531.5 18.8 %slice-start.4 = ((s8[4718592]{0:T(1024)(128)(4,1)}), s8[4194304]{0:T(1024)(128)(4,1)S(1)}, s32[]{:S(2)}) async-start(s8[4718592]{0:T(1024)(128)(4,1)} %bitcast.221), calls=%async_computation.23 | async-start | bytes 8388608
  531.5 18.8 %slice-start.6 = ((s8[4718592]{0:T(1024)(128)(4,1)}), s8[4194304]{0:T(1024)(128)(4,1)S(1)}, s32[]{:S(2)}) async-start(s8[4718592]{0:T(1024)(128)(4,1)} %bitcast.224), calls=%async_computation.25 | async-start | bytes 8388608
  531.6 18.7 %slice-start.5 = ((s8[4718592]{0:T(1024)(128)(4,1)}), s8[524288]{0:T(1024)(128)(4,1)S(1)}, s32[]{:S(2)}) async-start(s8[4718592]{0:T(1024)(128)(4,1)} %bitcast.221), calls=%async_computation.24 | async-start | bytes 1048576
  531.6 18.7 %slice-start.7 = ((s8[4718592]{0:T(1024)(128)(4,1)}), s8[524288]{0:T(1024)(128)(4,1)S(1)}, s32[]{:S(2)}) async-start(s8[4718592]{0:T(1024)(128)(4,1)} %bitcast.224), calls=%async_computation.26 | async-start | bytes 1048576
  531.6 18.7 %copy-start.52 = (bf16[4,256,16]{1,2,0:T(8,128)(2,1)S(1)}, bf16[4,256,16]{1,2,0:T(8,128)(2,1)}, u32[]{:S(2)}) copy-start(bf16[4,256,16]{1,2,0:T(8,128)(2,1)} %copy-done.51) | copy-start | bytes 98308
  554.6 520.2 %reduce-scatter.8.cloned.1.call-start = ((), (), s32[]{:S(2)}) async-start(), calls=%async_computation.14 | async-start | bytes 10948608 | tf_op jit(solution)/shard_map/reduce_scatter | solution.py:82
  576.6 25.6 %copy-start.22 = (f32[1152,288]{0,1:T(8,128)S(1)}, f32[1152,288]{0,1:T(8,128)}, u32[]{:S(2)}) copy-start(f32[1152,288]{0,1:T(8,128)} %param.34) | copy-start | bytes 3981316
  576.7 222.0 %copy-start.118 = (u32[32]{0:T(128)S(1)}, u32[32]{0:T(128)}, u32[]{:S(2)}) copy-start(u32[32]{0:T(128)} %constant.300) | copy-start | bytes 388
  576.7 222.6 %copy-start.117 = (u32[32]{0:T(128)S(1)}, u32[32]{0:T(128)}, u32[]{:S(2)}) copy-start(u32[32]{0:T(128)} %constant.295) | copy-start | bytes 388
  576.7 223.8 %copy-start.116 = (s32[32]{0:T(128)S(1)}, s32[32]{0:T(128)}, u32[]{:S(2)}) copy-start(s32[32]{0:T(128)} %param.22) | copy-start | bytes 388
  576.7 229.0 %copy-start.65 = (f32[12944]{0:T(1024)S(1)}, f32[12944]{0:T(1024)}, u32[]{:S(2)}) copy-start(f32[12944]{0:T(1024)} %param.36) | copy-start | bytes 155332
  576.7 230.9 %copy-start.43 = (bf16[32,1152]{1,0:T(8,128)(2,1)S(1)}, bf16[32,1152]{1,0:T(8,128)(2,1)}, u32[]{:S(2)}) copy-start(bf16[32,1152]{1,0:T(8,128)(2,1)} %copy-done.42) | copy-start | bytes 221188
  576.7 236.8 %copy-start.41 = (f32[32,1152]{1,0:T(8,128)S(1)}, f32[32,1152]{1,0:T(8,128)}, u32[]{:S(2)}) copy-start(f32[32,1152]{1,0:T(8,128)} %copy-done.40) | copy-start | bytes 442372
  576.7 244.9 %copy-start.46 = (f32[32,1152]{1,0:T(8,128)S(1)}, f32[32,1152]{1,0:T(8,128)}, u32[]{:S(2)}) copy-start(f32[32,1152]{1,0:T(8,128)} %get-tuple-element.176) | copy-start | bytes 442372
  578.1 251.3 %copy-start.108 = (f32[128]{0:T(128)S(1)}, f32[128]{0:T(128)}, u32[]{:S(2)}) copy-start(f32[128]{0:T(128)} %copy-done.107) | copy-start | bytes 1540
  578.1 11.3 all-to-all-start.3
  589.3 10.1 all-to-all-start.2
  592.7 554.9 %all-reduce.7.cloned.1.call-start = ((), (), s32[]{:S(2)}) async-start(), calls=%async_computation.16 | async-start | bytes 294912 | tf_op jit(solution)/shard_map/psum | solution.py:324
  603.1 574.4 %all-gather.14.cloned.1.call-start = ((), (), s32[]{:S(2)}) async-start(), calls=%async_computation.11 | async-start | bytes 1658880 | tf_op jit(solution)/shard_map/all_gather | solution.py:74
  651.8 534.6 %all-gather.16.cloned.1.call-start = ((), (), s32[]{:S(2)}) async-start(), calls=%async_computation.13 | async-start | bytes 1658880 | tf_op jit(solution)/shard_map/all_gather | solution.py:74
  798.5 407.9 %all-gather.18.cloned.1.call-start = ((), (), s32[]{:S(2)}) async-start(), calls=%async_computation.15 | async-start | bytes 1658880 | tf_op jit(solution)/shard_map/all_gather | solution.py:74
  1074.8 296.7 %all-reduce.9.cloned.1.call-start = ((), (), s32[]{:S(2)}) async-start(), calls=%async_computation.17 | async-start | bytes 188416
  1185.0 74.7 %copy-start.56 = (f32[16,1152]{1,0:T(8,128)S(1)}, f32[16,1152]{1,0:T(8,128)}, u32[]{:S(2)}) copy-start(f32[16,1152]{1,0:T(8,128)} %get-tuple-element.67) | copy-start | bytes 221188
  1252.5 53.1 %copy-start.99 = (f32[256]{0:T(256)}, f32[256]{0:T(256)S(1)}, u32[]{:S(2)}) copy-start(f32[256]{0:T(256)S(1)} %get-tuple-element.106) | copy-start | bytes 3076
  1253.8 21.0 %copy-start.68 = (f32[1152]{0:T(1024)}, f32[1152]{0:T(1024)S(1)}, u32[]{:S(2)}) copy-start(f32[1152]{0:T(1024)S(1)} %get-tuple-element.76) | copy-start | bytes 13828
  1260.4 54.8 %copy-start.53 = (f32[16,1152]{1,0:T(8,128)}, f32[16,1152]{1,0:T(8,128)S(1)}, u32[]{:S(2)}) copy-start(f32[16,1152]{1,0:T(8,128)S(1)} %get-tuple-element.108) | copy-start | bytes 221188
  1277.3 103.1 %copy-start.19 = (f32[2,3,72,1152]{3,2,1,0:T(8,128)}, f32[2,3,72,1152]{3,2,1,0:T(8,128)S(1)}, u32[]{:S(2)}) copy-start(f32[2,3,72,1152]{3,2,1,0:T(8,128)S(1)} %copy.156) | copy-start | bytes 5971972
  1277.4 23.3 %copy-start.79 = (f32[576]{0:T(1024)}, f32[576]{0:T(1024)S(1)}, u32[]{:S(2)}) copy-start(f32[576]{0:T(1024)S(1)} %add_multiply_fusion.7) | copy-start | bytes 6916
  1278.2 22.4 %copy-start.93 = (f32[288]{0:T(512)}, f32[288]{0:T(512)S(1)}, u32[]{:S(2)}) copy-start(f32[288]{0:T(512)S(1)} %add_multiply_fusion.10) | copy-start | bytes 3460
  1279.0 21.7 %copy-start.81 = (f32[576]{0:T(1024)}, f32[576]{0:T(1024)S(1)}, u32[]{:S(2)}) copy-start(f32[576]{0:T(1024)S(1)} %add_multiply_fusion.8) | copy-start | bytes 6916
  1279.0 21.6 %copy-start.101 = (f32[144]{0:T(256)}, f32[144]{0:T(256)S(1)}, u32[]{:S(2)}) copy-start(f32[144]{0:T(256)S(1)} %add_multiply_fusion.12) | copy-start | bytes 1732
  1280.6 20.0 %copy-start.95 = (f32[432]{0:T(512)}, f32[432]{0:T(512)S(1)}, u32[]{:S(2)}) copy-start(f32[432]{0:T(512)S(1)} %add_multiply_fusion.11) | copy-start | bytes 5188
  1308.3 69.7 %copy-start.111 = (f32[23056]{0:T(1024)S(1)}, f32[23056]{0:T(1024)}, u32[]{:S(2)}) copy-start(f32[23056]{0:T(1024)} %get-tuple-element.134) | copy-start | bytes 276676
  1308.3 69.9 %copy-start.109 = (f32[16]{0:T(128)S(1)}, f32[16]{0:T(128)}, u32[]{:S(2)}) copy-start(f32[16]{0:T(128)} %get-tuple-element.59) | copy-start | bytes 196
  1308.3 70.6 %copy-start.55 = (f32[1152,16]{0,1:T(8,128)S(1)}, f32[1152,16]{0,1:T(8,128)}, u32[]{:S(2)}) copy-start(f32[1152,16]{0,1:T(8,128)} %get-tuple-element.68) | copy-start | bytes 221188
  1308.4 72.0 %copy-start.96 = (f32[432]{0:T(512)S(1)}, f32[432]{0:T(512)}, u32[]{:S(2)}) copy-start(f32[432]{0:T(512)} %copy-done.95) | copy-start | bytes 5188
  1315.1 68.7 %copy-start.100 = (f32[256]{0:T(256)S(1)}, f32[256]{0:T(256)}, u32[]{:S(2)}) copy-start(f32[256]{0:T(256)} %copy-done.99) | copy-start | bytes 3076
  1315.1 69.4 %copy-start.45 = (f32[1152,16]{0,1:T(8,128)S(1)}, f32[1152,16]{0,1:T(8,128)}, u32[]{:S(2)}) copy-start(f32[1152,16]{0,1:T(8,128)} %param.35) | copy-start | bytes 221188
  1315.1 70.1 %copy-start.29 = (f32[144,1152]{1,0:T(8,128)S(1)}, f32[144,1152]{1,0:T(8,128)}, u32[]{:S(2)}) copy-start(f32[144,1152]{1,0:T(8,128)} %param.31) | copy-start | bytes 1990660
  1315.1 70.1 %copy-start.102 = (f32[144]{0:T(256)S(1)}, f32[144]{0:T(256)}, u32[]{:S(2)}) copy-start(f32[144]{0:T(256)} %copy-done.101) | copy-start | bytes 1732
  1315.9 71.5 %copy-start.94 = (f32[288]{0:T(512)S(1)}, f32[288]{0:T(512)}, u32[]{:S(2)}) copy-start(f32[288]{0:T(512)} %copy-done.93) | copy-start | bytes 3460
  (80 other events, 560.4 us)
Sparse Core Ops, SparseCore 0:
  14.1 90.3 all-gather.7
  108.1 85.8 all-gather.9
  197.5 85.9 all-gather.11
  509.5 142.2 reduce-scatter.3
  657.7 140.7 reduce-scatter.5
  804.6 120.0 all-reduce.10
  930.8 143.9 reduce-scatter.7
  1078.7 68.7 all-reduce.6
  1149.2 17.3 all-gather.13
  1168.0 18.3 all-gather.15
  1188.1 18.2 all-gather.17
  1305.8 65.6 all-reduce.8

commit v2 on v1

--- a/solution.py
+++ b/solution.py
@@ -1,8 +1,11 @@
+import functools
 import math
 
 import jax
 import jax.numpy as jnp
 from jax import lax
+from jax.experimental import pallas as pl
+from jax.experimental.pallas import tpu as pltpu
 from jax.sharding import PartitionSpec as P
 
 HD = 72
@@ -18,6 +21,7 @@
 step_rate = 1.5
 neg_large = -1e30
 highest = lax.Precision.HIGHEST
+MESH = pl.DeviceIdType.MESH
 
 
 def product(operand, other_operand):
@@ -68,6 +72,613 @@
     freq = jnp.exp(-math.log(10000.0) * jnp.arange(half, dtype=jnp.float32) / half)
     angle = steps.astype(jnp.float32)[:, None] * freq[None, :]
     return jnp.concatenate([jnp.cos(angle), jnp.sin(angle)], axis=1)
+
+
+def peers(span):
+    dp, mp = lax.axis_index("dp"), lax.axis_index("mp")
+    copies, groups = lax.axis_size("dp"), lax.axis_size("mp")
+    if span == "mp":
+        return mp, groups, lambda place: (dp, place)
+    if span == "dp":
+        return dp, copies, lambda place: (place, mp)
+    return dp * groups + mp, copies * groups, lambda place: (place // groups, lax.rem(place, groups))
+
+
+def greet(span):
+    here, size, device = peers(span)
+    barrier = pltpu.get_barrier_semaphore()
+
+    @pl.loop(1, size)
+    def _(step):
+        pl.semaphore_signal(
+            barrier,
+            inc=1,
+            device_id=device(lax.rem(here + step, size)),
+            device_id_type=MESH,
+        )
+
+    pl.semaphore_wait(barrier, size - 1)
+
+
+def to_all(span, pick, landing, send_sems, recv_sems):
+    here, size, device = peers(span)
+
+    def copy(step):
+        place = lax.rem(here + step, size)
+        return pltpu.make_async_remote_copy(
+            src_ref=pick(place),
+            dst_ref=landing(here),
+            send_sem=send_sems.at[step],
+            recv_sem=recv_sems.at[step],
+            device_id=device(place),
+            device_id_type=MESH,
+        )
+
+    @pl.loop(1, size)
+    def _(step):
+        copy(step).start()
+
+    def wait():
+        @pl.loop(1, size)
+        def _(step):
+            copy(step).wait()
+
+    return wait
+
+
+def sum_over(ref):
+    return lax.fori_loop(1, ref.shape[0], lambda index, total: total + ref[index], ref[0])
+
+
+def swap_kernel(span, per_target, groups, x_ref, out_ref, send_sems, recv_sems):
+    here, _, _ = peers(span)
+
+    def pick(place):
+        return x_ref.at[lax.rem(place, groups)] if per_target else x_ref
+
+    greet(span)
+    wait = to_all(span, pick, lambda place: out_ref.at[place], send_sems, recv_sems)
+    out_ref[here] = x_ref[lax.rem(here, groups)] if per_target else x_ref[...]
+    wait()
+
+
+def total_kernel(span, x_ref, out_ref, land, send_sems, recv_sems):
+    here, _, _ = peers(span)
+    greet(span)
+    wait = to_all(span, lambda place: x_ref, lambda place: land.at[place], send_sems, recv_sems)
+    land[here] = x_ref[...]
+    wait()
+    out_ref[...] = sum_over(land)
+
+
+def both_kernel(all_ref, mp_ref, all_out, mp_out, all_land, mp_land, send_sems, recv_sems):
+    here, _, _ = peers("all")
+    member, _, _ = peers("mp")
+    greet("all")
+    wait_all = to_all(
+        "all",
+        lambda place: all_ref.at[place],
+        lambda place: all_land.at[place],
+        send_sems.at[0],
+        recv_sems.at[0],
+    )
+    wait_mp = to_all(
+        "mp",
+        lambda place: mp_ref.at[place],
+        lambda place: mp_land.at[place],
+        send_sems.at[1],
+        recv_sems.at[1],
+    )
+    all_land[here] = all_ref[here]
+    mp_land[member] = mp_ref[member]
+    wait_mp()
+    mp_out[here] = sum_over(mp_land)
+    wait_mp = to_all(
+        "all",
+        lambda place: mp_out.at[here],
+        lambda place: mp_out.at[place],
+        send_sems.at[2],
+        recv_sems.at[2],
+    )
+    wait_all()
+    all_out[here] = sum_over(all_land)
+    wait_all = to_all(
+        "all",
+        lambda place: all_out.at[here],
+        lambda place: all_out.at[place],
+        send_sems.at[3],
+        recv_sems.at[3],
+    )
+    wait_mp()
+    wait_all()
+
+
+def group_size(span):
+    sizes = {"dp": lax.axis_size("dp"), "mp": lax.axis_size("mp")}
+    return sizes.get(span, sizes["dp"] * sizes["mp"])
+
+
+def call(kernel, inputs, out_shapes, scratch, collective_id):
+    return pl.pallas_call(
+        kernel,
+        out_shape=[jax.ShapeDtypeStruct(shape, jnp.float32) for shape in out_shapes],
+        in_specs=[pl.BlockSpec(memory_space=pltpu.VMEM)] * len(inputs),
+        out_specs=[pl.BlockSpec(memory_space=pltpu.VMEM)] * len(out_shapes),
+        scratch_shapes=scratch,
+        compiler_params=pltpu.CompilerParams(
+            collective_id=collective_id, has_side_effects=True, vmem_limit_bytes=32 * 1024 * 1024
+        ),
+    )(*inputs)
+
+
+def swap(values, span, collective_id, per_target=True):
+    size = group_size(span)
+    slab = values.shape[-2:]
+    (result,) = call(
+        functools.partial(swap_kernel, span, per_target, lax.axis_size("mp")),
+        [values],
+        [(size,) + slab],
+        [pltpu.SemaphoreType.DMA((size,)), pltpu.SemaphoreType.DMA((size,))],
+        collective_id,
+    )
+    return result
+
+
+def total(values, span, collective_id):
+    size = group_size(span)
+    (result,) = call(
+        functools.partial(total_kernel, span),
+        [values],
+        [values.shape],
+        [
+            pltpu.VMEM((size,) + values.shape, jnp.float32),
+            pltpu.SemaphoreType.DMA((size,)),
+            pltpu.SemaphoreType.DMA((size,)),
+        ],
+        collective_id,
+    )
+    return result
+
+
+def both_totals(for_all, for_mp, collective_id):
+    size = group_size("all")
+    return call(
+        both_kernel,
+        [for_all, for_mp],
+        [for_all.shape, (size,) + for_mp.shape[1:]],
+        [
+            pltpu.VMEM(for_all.shape, jnp.float32),
+            pltpu.VMEM(for_mp.shape, jnp.float32),
+            pltpu.SemaphoreType.DMA((4, size)),
+            pltpu.SemaphoreType.DMA((4, size)),
+        ],
+        collective_id,
+    )
+
+
+def slabs(flat, blocks):
+    chunk = 1024 * blocks
+    short = (-flat.shape[0]) % chunk
+    return jnp.pad(flat, (0, short)).reshape(blocks, -1, 128)
+
+
+def reduce_kernel(counts, *refs):
+    copies, groups = counts
+    lines = {"a": 4, "b": groups // 4, "y": copies // 2}
+    chunks = (len(refs) - 8) // 2
+    parts = refs[:chunks]
+    outs = refs[chunks : 2 * chunks]
+    held, twin, first_b, first_y, second, third, send_sems, recv_sems = refs[2 * chunks :]
+    splits = parts[0].shape[4]
+    dp, mp = lax.axis_index("dp"), lax.axis_index("mp")
+    at = {"a": mp // lines["b"], "b": lax.rem(mp, lines["b"]), "y": dp // 2}
+    core = lax.rem(dp, 2)
+
+    def device(**moved):
+        place = {**at, "core": core, **moved}
+        return (place["y"] * 2 + place["core"], place["a"] * lines["b"] + place["b"])
+
+    barrier = pltpu.get_barrier_semaphore()
+    pl.semaphore_signal(barrier, inc=1, device_id=device(core=1 - core), device_id_type=MESH)
+    for axis, size in lines.items():
+        for step in range(1, size):
+            if axis != "y" and step not in (1, size - 1):
+                continue
+            other = lax.rem(at[axis] + step, size)
+            pl.semaphore_signal(
+                barrier, inc=1, device_id=device(**{axis: other}), device_id_type=MESH
+            )
+    total = 1 + sum(
+        (size - 1) if axis == "y" else len({1, size - 1} - {0}) for axis, size in lines.items()
+    )
+    pl.semaphore_wait(barrier, total)
+
+    units = [(chunk, split) for chunk in range(chunks) for split in range(splits)]
+    slots = {}
+
+    def sems(unit, name):
+        slot = slots.setdefault(name, len(slots))
+        return send_sems.at[unit, slot], recv_sems.at[unit, slot]
+
+    def add_into(target, source):
+        @pl.loop(0, target.shape[0])
+        def _(index):
+            target[index] = target[index] + source[index]
+
+    def twin_copy(unit):
+        chunk, split = units[unit]
+        send, recv = sems(unit, "twin")
+        return pltpu.make_async_remote_copy(
+            src_ref=parts[chunk].at[:, 1 - core, :, :, split],
+            dst_ref=twin.at[unit],
+            send_sem=send,
+            recv_sem=recv,
+            device_id=device(core=1 - core),
+            device_id_type=MESH,
+        )
+
+    def held_copy(unit):
+        chunk, split = units[unit]
+        return pltpu.make_async_copy(
+            parts[chunk].at[:, core, :, :, split], held.at[unit], sems(unit, "held")[1]
+        )
+
+    def line_steps(unit, axis, name, pick, landing):
+        size, here = lines[axis], at[axis]
+        tasks = []
+
+        def slot_of(up, hop):
+            return 0 if size == 2 else hop - 1 + (size - 1 if up else 0)
+
+        def copy(up, hop):
+            target = here + hop if up else here - hop
+            send, recv = sems(unit, (name, up, hop))
+            slot = slot_of(up, hop)
+            safe = lax.rem(target + size, size)
+            beside = here + 1 if up else here - 1
+            beside = lax.rem(beside + size, size)
+            return pltpu.make_async_remote_copy(
+                src_ref=pick(safe),
+                dst_ref=landing(slot),
+                send_sem=send,
+                recv_sem=recv,
+                device_id=device(**{axis: beside}),
+                device_id_type=MESH,
+            )
+
+        def sends(up, hop):
+            return here + hop <= size - 1 if up else here - hop >= 0
+
+        def arrives(up, hop):
+            if up:
+                return (here >= 1) & (here + hop - 1 <= size - 1)
+            return (here <= size - 2) & (here - hop + 1 >= 0)
+
+        def take(up, hop):
+            @pl.when(arrives(up, hop))
+            def _():
+                copy(up, hop).wait_recv()
+                slot = slot_of(up, hop)
+                target = here + hop - 1 if up else here - hop + 1
+                add_into(pick(lax.rem(target + size, size)), landing(slot))
+
+        def give(up, hop):
+            @pl.when(sends(up, hop))
+            def _():
+                copy(up, hop).start()
+
+        def finish(up, hop):
+            @pl.when(sends(up, hop))
+            def _():
+                copy(up, hop).wait_send()
+
+        for hop in range(size - 1, 0, -1):
+
+            def begin(hop=hop):
+                for up in (True, False):
+                    if hop < size - 1:
+                        take(up, hop + 1)
+                    give(up, hop)
+
+            tasks.append(begin)
+
+        def close():
+            for up in (True, False):
+                take(up, 1)
+
+        def drain():
+            for hop in range(1, size):
+                for up in (True, False):
+                    finish(up, hop)
+
+        return tasks, close, drain
+
+    def unit_tasks(unit):
+        chunk, split = units[unit]
+        block = held.at[unit]
+        halves = []
+        drains = []
+        for half, order in ((0, ("b", "y")), (1, ("y", "b"))):
+            rows_a = pl.ds(2 * half, 2)
+
+            def pick_one(target, axis=order[0], rows_a=rows_a):
+                if axis == "b":
+                    return block.at[:, rows_a, target]
+                return block.at[target, rows_a]
+
+            def pick_two(target, axis=order[1], rows_a=rows_a):
+                if axis == "b":
+                    return block.at[at["y"], rows_a, target]
+                return block.at[target, rows_a, at["b"]]
+
+            one = line_steps(
+                unit,
+                order[0],
+                ("one", half),
+                pick_one,
+                lambda slot, axis=order[0]: (first_b if axis == "b" else first_y).at[unit, slot],
+            )
+            two = line_steps(
+                unit,
+                order[1],
+                ("two", half),
+                pick_two,
+                lambda slot, half=half: second.at[unit, half, slot],
+            )
+            steps = list(one[0])
+            joined = two[0][0]
+
+            def pass_on(close=one[1], go=joined):
+                close()
+                go()
+
+            steps += [pass_on] + list(two[0][1:])
+            halves.append((steps, two[1]))
+            drains += [one[2], two[2]]
+        last = line_steps(
+            unit,
+            "a",
+            "last",
+            lambda target: block.at[at["y"], target, pl.ds(at["b"], 1)],
+            lambda slot: third.at[unit, slot],
+        )
+        drains.append(last[2])
+        out = outs[chunk]
+
+        def spread_copy(owner, to):
+            send, recv = sems(unit, ("spread", owner[2], to[2]))
+            return pltpu.make_async_remote_copy(
+                src_ref=out.at[owner[0], owner[1], split],
+                dst_ref=out.at[owner[0], owner[1], split],
+                send_sem=send,
+                recv_sem=recv,
+                device_id=device(y=to[0], core=to[1]),
+                device_id_type=MESH,
+            )
+
+        size_y = lines["y"]
+        me = (at["y"], core, 0)
+        twin_place = (at["y"], 1 - core, "twin")
+
+        def far(step):
+            return (lax.rem(at["y"] + step, size_y), core, step)
+
+        def start():
+            held_copy(unit).wait()
+            twin_copy(unit).wait_recv()
+
+            @pl.loop(0, block.shape[0])
+            def _(row):
+                @pl.loop(0, block.shape[1])
+                def _(group):
+                    block[row, group] = block[row, group] + twin[unit, row, group]
+
+            for steps, _ in halves:
+                steps[0]()
+
+        tasks = [start]
+        for index in range(1, len(halves[0][0])):
+
+            def middle(index=index):
+                for steps, _ in halves:
+                    steps[index]()
+
+            tasks.append(middle)
+
+        def to_last():
+            for _, close in halves:
+                close()
+            last[0][0]()
+
+        tasks.append(to_last)
+        tasks += list(last[0][1:])
+
+        def sum_done():
+            last[1]()
+            out[at["y"], core, split] = block[at["y"], at["a"], at["b"]]
+            for step in range(1, size_y):
+                spread_copy(me, far(step)).start()
+            spread_copy(me, twin_place).start()
+
+        tasks.append(sum_done)
+
+        def before(step):
+            return (lax.rem(at["y"] + size_y - step, size_y), core, step)
+
+        def forward():
+            for step in range(1, size_y):
+                spread_copy((at["y"], core, 0), far(step)).wait_recv()
+                source = before(step)
+                spread_copy(source, twin_place).start()
+
+        tasks.append(forward)
+
+        def end():
+            spread_copy(me, twin_place).wait()
+            for step in range(1, size_y):
+                spread_copy(before(step), twin_place).wait()
+                spread_copy(me, far(step)).wait_send()
+            twin_copy(unit).wait_send()
+            for drain in drains:
+                drain()
+
+        tasks.append(end)
+        return tasks
+
+    for unit in range(len(units)):
+        twin_copy(unit).start()
+        held_copy(unit).start()
+    queues = [unit_tasks(unit) for unit in range(len(units))]
+    depth = len(queues[0])
+    for tick in range(len(units) + depth - 1):
+        for unit in reversed(range(len(units))):
+            task = tick - unit
+            if 0 <= task < depth:
+                queues[unit][task]()
+
+
+def reduce_weights(partials, collective_id):
+    copies, groups = lax.axis_size("dp"), lax.axis_size("mp")
+    rows, width = partials[0].shape
+    size_b, size_y = groups // 4, copies // 2
+    piece = rows // (copies * groups)
+    share = 48 if piece % 48 == 0 else piece
+    splits = piece // share
+    shaped = [
+        part.reshape(size_y, 2, 4, size_b, splits, share, width) for part in partials
+    ]
+    units = splits * len(partials)
+    slab = (share, width)
+    slots_b = 1 if size_b == 2 else 2 * (size_b - 1)
+    slots_y = 1 if size_y == 2 else 2 * (size_y - 1)
+    scratch = [
+        pltpu.VMEM((units, size_y, 4, size_b) + slab, jnp.bfloat16),
+        pltpu.VMEM((units, size_y, 4, size_b) + slab, jnp.bfloat16),
+        pltpu.VMEM((units, slots_b, size_y, 2) + slab, jnp.bfloat16),
+        pltpu.VMEM((units, slots_y, 2, size_b) + slab, jnp.bfloat16),
+        pltpu.VMEM((units, 2, max(slots_b, slots_y), 2) + slab, jnp.bfloat16),
+        pltpu.VMEM((units, 6, 1) + slab, jnp.bfloat16),
+        pltpu.SemaphoreType.DMA((units, 40)),
+        pltpu.SemaphoreType.DMA((units, 40)),
+    ]
+    results = pl.pallas_call(
+        functools.partial(reduce_kernel, (copies, groups)),
+        out_shape=[jax.ShapeDtypeStruct((size_y, 2, splits) + slab, jnp.bfloat16)] * len(partials),
+        in_specs=[pl.BlockSpec(memory_space=pl.ANY)] * len(partials),
+        out_specs=[pl.BlockSpec(memory_space=pltpu.VMEM)] * len(partials),
+        scratch_shapes=scratch,
+        compiler_params=pltpu.CompilerParams(
+            collective_id=collective_id, has_side_effects=True, vmem_limit_bytes=60 * 1024 * 1024
+        ),
+    )(*shaped)
+    return [result.reshape(copies * piece, width) for result in results]
+
+
+def weights_of(keys, queries, live):
+    scores = product_left(keys, queries) * HD ** (-0.5)
+    scores = jnp.where(live, scores, neg_large)
+    exponent = jnp.exp(scores - jnp.max(scores, axis=0, keepdims=True))
+    return exponent / jnp.sum(exponent, axis=0, keepdims=True)
+
+
+def attend_kernel(length_ref, q_ref, k_ref, v_ref, out_ref):
+    patches = q_ref.shape[1]
+    pair = 2 * HD
+    live = lax.broadcasted_iota(jnp.int32, (patches, patches), 0) < length_ref[pl.program_id(0)]
+    upper = lax.broadcasted_iota(jnp.int32, (pair, patches), 0) < HD
+
+    @pl.loop(0, q_ref.shape[0] // pair)
+    def _(index):
+        rows = pl.ds(pl.multiple_of(index * pair, 16), pair)
+        queries, keys, values = q_ref[rows, :], k_ref[rows, :], v_ref[rows, :]
+        zero = jnp.zeros_like(queries)
+        mixed = []
+        for half in range(2):
+            own = upper if half == 0 else ~upper
+            probs = weights_of(keys, jnp.where(own, queries, zero), live)
+            mixed.append(product(values, probs.astype(jnp.bfloat16)))
+        out_ref[rows, :] = jnp.where(upper, mixed[0], mixed[1]).astype(jnp.bfloat16)
+
+
+def attend_back_kernel(length_ref, q_ref, k_ref, v_ref, up_ref, down_ref):
+    patches = q_ref.shape[1]
+    pair = 2 * HD
+    live = lax.broadcasted_iota(jnp.int32, (patches, patches), 0) < length_ref[pl.program_id(0)]
+    upper = lax.broadcasted_iota(jnp.int32, (pair, patches), 0) < HD
+
+    @pl.loop(0, q_ref.shape[0] // pair)
+    def _(index):
+        rows = pl.ds(pl.multiple_of(index * pair, 16), pair)
+        queries, keys, values, upstream = (
+            q_ref[rows, :],
+            k_ref[rows, :],
+            v_ref[rows, :],
+            up_ref[rows, :],
+        )
+        zero = jnp.zeros_like(queries)
+        found = []
+        for half in range(2):
+            own = upper if half == 0 else ~upper
+            probs = weights_of(keys, jnp.where(own, queries, zero), live)
+            probs_grad = product_left(values, jnp.where(own, upstream, zero))
+            weighted = probs * probs_grad
+            score_grad = (
+                weighted - probs * jnp.sum(weighted, axis=0, keepdims=True)
+            ).astype(jnp.bfloat16)
+            found.append(
+                (
+                    product(keys, score_grad),
+                    product_right(queries, score_grad),
+                    product_right(upstream, probs.astype(jnp.bfloat16)),
+                )
+            )
+        scale = HD ** (-0.5)
+        down_ref[0, rows, :] = (jnp.where(upper, found[0][0], found[1][0]) * scale).astype(jnp.bfloat16)
+        down_ref[1, rows, :] = (jnp.where(upper, found[0][1], found[1][1]) * scale).astype(jnp.bfloat16)
+        down_ref[2, rows, :] = jnp.where(upper, found[0][2], found[1][2]).astype(jnp.bfloat16)
+
+
+def _specs(width, patches):
+    def spec(block):
+        return pl.BlockSpec((width, patches), lambda image, lengths: (block, image))
+
+    return spec
+
+
+def attend(qkv, lengths, images):
+    width, rows = qkv.shape[0] // 3, qkv.shape[1]
+    patches = rows // images
+    spec = _specs(width, patches)
+    return pl.pallas_call(
+        attend_kernel,
+        grid_spec=pltpu.PrefetchScalarGridSpec(
+            num_scalar_prefetch=1,
+            grid=(images,),
+            in_specs=[spec(0), spec(1), spec(2)],
+            out_specs=spec(0),
+        ),
+        out_shape=jax.ShapeDtypeStruct((width, rows), jnp.bfloat16),
+        compiler_params=pltpu.CompilerParams(vmem_limit_bytes=48 * 1024 * 1024),
+        cost_estimate=pl.CostEstimate(flops=4 * rows * patches * width, bytes_accessed=8 * rows * width, transcendentals=0),
+    )(lengths, qkv, qkv, qkv)
+
+
+def attend_back(qkv, upstream, lengths, images):
+    width, rows = upstream.shape
+    patches = rows // images
+    spec = _specs(width, patches)
+    return pl.pallas_call(
+        attend_back_kernel,
+        grid_spec=pltpu.PrefetchScalarGridSpec(
+            num_scalar_prefetch=1,
+            grid=(images,),
+            in_specs=[spec(0), spec(1), spec(2), spec(0)],
+            out_specs=pl.BlockSpec((3, width, patches), lambda image, lengths: (0, 0, image)),
+        ),
+        out_shape=jax.ShapeDtypeStruct((3, width, rows), jnp.bfloat16),
+        compiler_params=pltpu.CompilerParams(vmem_limit_bytes=48 * 1024 * 1024),
+        cost_estimate=pl.CostEstimate(flops=10 * rows * patches * width, bytes_accessed=14 * rows * width, transcendentals=0),
+    )(lengths, qkv, qkv, qkv, upstream).reshape(3 * width, rows)
 
 
 def across(values, axes):
@@ -148,23 +759,28 @@
     expand_use = gathered[1]
     contract_use = gathered[2]
 
-    features = time_features(timesteps, FREQ)
-    class_rows = jnp.take(class_vectors, labels, axis=0).astype(jnp.float32)
+    group_images = groups * images
+    asked = jnp.stack([timesteps, labels]).astype(jnp.float32)
+    asked = jnp.pad(asked, ((0, 6), (0, 128 - group_images)))
+    asked = swap(asked, "dp", 1, per_target=False)[:, :2, :group_images]
+    steps_all, labels_all = asked.transpose(1, 0, 2).reshape(2, copies * group_images).astype(jnp.int32)
+    features = time_features(steps_all, FREQ)
+    class_rows = jnp.take(class_vectors, labels_all, axis=0).astype(jnp.float32)
     hidden_pre = jnp.dot(features, time_first, precision=highest)
     condition = jnp.dot(jax.nn.silu(hidden_pre), time_second, precision=highest) + class_rows
-    signal = jax.nn.silu(condition).astype(jnp.bfloat16)
+    signal_all = jax.nn.silu(condition).astype(jnp.bfloat16)
+    signal = lax.dynamic_slice_in_dim(signal_all, copy * group_images, group_images)
     modulator_low = modulator.astype(jnp.bfloat16)
     finisher_low = finisher.astype(jnp.bfloat16)
-    steer_part = product(signal, modulator_low).astype(jnp.bfloat16)
-    final_part = product(signal, finisher_low).astype(jnp.bfloat16)
-    steer_own = lax.all_to_all(steer_part, "mp", split_axis=0, concat_axis=1, tiled=True)
-    final_own = lax.all_to_all(final_part, "mp", split_axis=0, concat_axis=1, tiled=True)
-    steering = steer_own.astype(jnp.float32).reshape(images, 6, 1, width)
-    final_steer = final_own.astype(jnp.float32).reshape(images, 2, 1, width)
-    features_all = time_features(across(timesteps, "dp"), FREQ)
-    hidden_pre_all = across(hidden_pre, "dp")
-    condition_all = across(condition, "dp")
-    signal_all = across(signal, "dp")
+    steer_here, final_here = modulator.shape[1], finisher.shape[1]
+    mods_part = jnp.concatenate(
+        [product(signal, modulator_low), product(signal, finisher_low)], axis=1
+    )
+    mods_part = mods_part.astype(jnp.bfloat16).astype(jnp.float32)
+    mods_own = swap(mods_part.reshape(groups, -1, 128), "mp", 2)
+    mods_own = mods_own.reshape(groups, images, steer_here + final_here).transpose(1, 0, 2)
+    steering = mods_own[:, :, :steer_here].reshape(images, 6, 1, width)
+    final_steer = mods_own[:, :, steer_here:].reshape(images, 2, 1, width)
 
     embedder_low = embedder.astype(jnp.bfloat16)
     readout_low = readout.astype(jnp.bfloat16)
@@ -184,25 +800,9 @@
         .astype(jnp.bfloat16)
         .reshape(rows, width)
     )
-    qkv = product_right(input_one, inputs_use).astype(jnp.bfloat16)
-    qkv = qkv.reshape(images, patches, 3, heads, HD)
-    queries, key_part, value_part = qkv[:, :, 0], qkv[:, :, 1], qkv[:, :, 2]
-    scores = (
-        jnp.einsum("gqhe,gkhe->ghqk", queries, key_part, preferred_element_type=jnp.float32)
-        * HD ** (-0.5)
-    )
-    scores = jnp.where(live[:, None, None, :], scores, neg_large)
-    peak = jnp.max(scores, axis=-1, keepdims=True)
-    exponent = jnp.exp(scores - peak)
-    attend = exponent / jnp.sum(exponent, axis=-1, keepdims=True)
-    mixed = jnp.einsum(
-        "ghqk,gkhe->gqhe",
-        attend.astype(jnp.bfloat16),
-        value_part,
-        preferred_element_type=jnp.float32,
-    )
-    mixed = mixed.astype(jnp.bfloat16).reshape(rows, width)
-    branch_one = product(mixed, outputs_use).reshape(images, patches, width)
+    qkv = product_right(inputs_use, input_one).astype(jnp.bfloat16)
+    mixed = attend(qkv, own_lengths, images)
+    branch_one = product_left(mixed, outputs_use).reshape(images, patches, width)
     residual_one = residual_zero + steering[:, 2] * branch_one
     normed_two = layer_norm(residual_one)
     input_two = (
@@ -245,39 +845,11 @@
     )
     gate_one_grad = jnp.sum(grad_residual * branch_one, axis=1)
     branch_one_grad = (steering[:, 2] * grad_residual).astype(jnp.bfloat16).reshape(rows, width)
-    outputs_part = product_left(mixed, branch_one_grad).astype(jnp.bfloat16)
-    mixed_grad = (
-        product_right(branch_one_grad, outputs_use)
-        .astype(jnp.bfloat16)
-        .reshape(images, patches, heads, HD)
-    )
-    attend_grad = jnp.einsum(
-        "gqhe,gkhe->ghqk", mixed_grad, value_part, preferred_element_type=jnp.float32
-    )
-    score_grad = (
-        attend * (attend_grad - jnp.sum(attend * attend_grad, axis=-1, keepdims=True))
-    ).astype(jnp.bfloat16)
-    query_grad = (
-        jnp.einsum("ghqk,gkhe->gqhe", score_grad, key_part, preferred_element_type=jnp.float32)
-        * HD ** (-0.5)
-    )
-    key_grad = (
-        jnp.einsum("ghqk,gqhe->gkhe", score_grad, queries, preferred_element_type=jnp.float32)
-        * HD ** (-0.5)
-    )
-    value_grad = jnp.einsum(
-        "ghqk,gqhe->gkhe",
-        attend.astype(jnp.bfloat16),
-        mixed_grad,
-        preferred_element_type=jnp.float32,
-    )
-    qkv_grad = (
-        jnp.stack([query_grad, key_grad, value_grad], axis=2)
-        .astype(jnp.bfloat16)
-        .reshape(rows, 3 * width)
-    )
-    inputs_part = product_left(qkv_grad, input_one).astype(jnp.bfloat16)
-    input_one_grad = product(qkv_grad, inputs_use).reshape(images, patches, width)
+    outputs_part = product(mixed, branch_one_grad).astype(jnp.bfloat16)
+    mixed_grad = product_right(outputs_use, branch_one_grad).astype(jnp.bfloat16)
+    qkv_grad = attend_back(qkv, mixed_grad, own_lengths, images)
+    inputs_part = product(qkv_grad, input_one).astype(jnp.bfloat16)
+    input_one_grad = product_left(qkv_grad, inputs_use).reshape(images, patches, width)
     shift_one_grad = jnp.sum(input_one_grad, axis=1)
     scale_one_grad = jnp.sum(input_one_grad * normed_one, axis=1)
     grad_residual = grad_residual + norm_back(
@@ -292,8 +864,9 @@
         .reshape(4 * width, width)
     )
     contract_sum = reduce_weight(contract_part).astype(jnp.float32)
-    expand_sum = reduce_weight(expand_part).astype(jnp.float32).T
-    mixer_sum = reduce_weight(mixer_part).astype(jnp.float32)
+    expand_sum, mixer_sum = reduce_weights([expand_part, mixer_part], 3)
+    expand_sum = expand_sum.astype(jnp.float32).T
+    mixer_sum = mixer_sum.astype(jnp.float32)
     held = heads_here * HD
     inputs_sum = (
         mixer_sum[: 3 * held]
@@ -318,24 +891,43 @@
     steer_back = steer_back.reshape(images, 6 * width).astype(jnp.bfloat16)
     final_back = jnp.stack([final_shift_grad, final_scale_grad], axis=1)
     final_back = final_back.reshape(images, 2 * width).astype(jnp.bfloat16)
-    steer_cols = lax.all_to_all(steer_back, "mp", split_axis=1, concat_axis=0, tiled=True)
-    final_cols = lax.all_to_all(final_back, "mp", split_axis=1, concat_axis=0, tiled=True)
-    signal_grad = product_right(steer_cols, modulator_low) + product_right(final_cols, finisher_low)
-    signal_grad = across(lax.psum(signal_grad, "mp"), "dp")
-    modulator_sum = product_left(signal_all, across(steer_cols, "dp"))
-    finisher_sum = product_left(signal_all, across(final_cols, "dp"))
-    hidden_all, hidden_pull = jax.vjp(jax.nn.silu, hidden_pre_all)
-    condition_grad = jax.vjp(jax.nn.silu, condition_all)[1](signal_grad)[0]
+    back = jnp.concatenate(
+        [
+            steer_back.reshape(images, groups, steer_here),
+            final_back.reshape(images, groups, final_here),
+        ],
+        axis=2,
+    )
+    back = back.transpose(1, 0, 2).astype(jnp.float32).reshape(groups, -1, 128)
+    cols_all = swap(back, "all", 4).astype(jnp.bfloat16)
+    cols_all = cols_all.reshape(copies * group_images, steer_here + final_here)
+    cols = lax.dynamic_slice_in_dim(cols_all, copy * group_images, group_images)
+    signal_grad = product_right(cols[:, :steer_here], modulator_low) + product_right(
+        cols[:, steer_here:], finisher_low
+    )
+    shared = slabs(
+        jnp.concatenate([embed_part.reshape(-1), readout_part.reshape(-1), loss_part[None]]),
+        copies * groups,
+    )
+    shared, signal_grad = both_totals(shared, signal_grad.reshape(groups, -1, 128), 5)
+    shared = shared.reshape(-1)
+    embed_sum = shared[: embedder.size].reshape(embedder.shape)
+    readout_sum = shared[embedder.size : embedder.size + readout.size].reshape(readout.shape)
+    loss_sum = shared[embedder.size + readout.size]
+    signal_grad = signal_grad.reshape(copies * group_images, width)
+    modulator_sum = product_left(signal_all, cols_all[:, :steer_here])
+    finisher_sum = product_left(signal_all, cols_all[:, steer_here:])
+    hidden, hidden_pull = jax.vjp(jax.nn.silu, hidden_pre)
+    condition_grad = jax.vjp(jax.nn.silu, condition)[1](signal_grad)[0]
     time_second_sum = lax.dot_general(
-        hidden_all, condition_grad, (((0,), (0,)), ((), ())), precision=highest
+        hidden, condition_grad, (((0,), (0,)), ((), ())), precision=highest
     )
     hidden_grad = hidden_pull(
         lax.dot_general(condition_grad, time_second, (((1,), (1,)), ((), ())), precision=highest)
     )[0]
     time_first_sum = lax.dot_general(
-        features_all, hidden_grad, (((0,), (0,)), ((), ())), precision=highest
-    )
-    embed_sum, readout_sum, loss_sum = lax.psum((embed_part, readout_part, loss_part), ("dp", "mp"))
+        features, hidden_grad, (((0,), (0,)), ((), ())), precision=highest
+    )
 
     gradients = (
         embed_sum,
@@ -383,8 +975,9 @@
         for slot in split_slots
     ]
     lengths_out = [part.shape[0] for part in crossing]
-    crossed = lax.psum(jnp.concatenate(crossing + [split_square[None]]), "mp")
-    grad_norm = jnp.sqrt(crossed[-1] + local_square)
+    crossing = jnp.concatenate(crossing + [split_square[None]])
+    crossed = total(slabs(crossing, 1)[0], "mp", 6).reshape(-1)
+    grad_norm = jnp.sqrt(crossed[crossing.shape[0] - 1] + local_square)
     factor = clip_limit / jnp.maximum(grad_norm, clip_limit)
     factor_square = factor * factor
     start = 0
@@ -428,7 +1021,8 @@
     shares = [jnp.stack([records[slot][2] for slot in split_slots])]
     for slot in split_slots:
         shares.append(records[slot][4] if layouts[slot] == "columns" else records[slot][3])
-    spread = lax.all_gather(jnp.concatenate(shares), "mp", axis=0)
+    spread = swap(slabs(jnp.concatenate(shares), 1)[0], "mp", 7, per_target=False)
+    spread = spread.reshape(groups, -1)
     energies = jnp.sum(spread[:, : len(split_slots)], axis=0)
     start = len(split_slots)
     next_list = []

time: 1420 us -> 905 us (0.64)
  waiting for transfers between devices: 616 us -> 150 us
  Pallas kernels: 0 us -> 286 us
  blocking collectives: 123 us -> 0 us
  local copies, waits for them, and re-layouts: 138 us -> 55 us
  other arithmetic: 187 us -> 130 us
  matrix products: 284 us -> 233 us
  starting transfers between devices: 21.4 us -> 0.21 us
    reduce_scatter x3 -> x1, waiting for transfers between devices: 332 us -> 0.01 us  [reduce_weight(): lax.psum_scatter(partial, ('dp', 'mp'), scatter_dimension=0, tiled=True)]
    pallas_call x0 -> x9, Pallas kernels: none -> 286 us  [the longest x1 131 us: reduce_weights(): pl.pallas_call(functools.partial(reduce_kernel, (copies, groups)), out_sh...]
    psum x2 -> x0, waiting for transfers between devices: 120 us -> none  [the longest x1 72.6 us: body(): signal_grad = across(lax.psum(signal_grad, 'mp'), 'dp')]
    psum x2 -> x0, blocking collectives: 76.5 us -> none  [the longest x1 39.4 us: body(): lax.psum((embed_part, readout_part, loss_part), ('dp', 'mp'))]
    all_gather x6 -> x4, waiting for transfers between devices: 89.5 us -> 150 us  [across(): return lax.all_gather(values, axes, axis=0, tiled=True)]
    unnamed x13 -> x5, waiting for transfers between devices: 55.1 us -> 0.08 us
    dot_general x8 -> x2, matrix products: 56.3 us -> 12 us  [the longest x1 9.08 us: body(): lax.dot_general(hidden, condition_grad, (((0,), (0,)), ((), ())), precisi...]
    all_gather x6 -> x0, blocking collectives: 41.9 us -> none  [across(): return lax.all_gather(values, axes, axis=0, tiled=True)]
  transfers between devices with their start and end apart: 16 -> 5, of which waited for: 13 -> 3; matrix products, arithmetic and copies ran while one was open for 21% -> 21% of each run, Pallas kernels for 0% -> 26%
where the time goes in v2:
time: 905 us; the launch traced here: 896 us
  Pallas kernels  286 us (32%)
  matrix products  233 us (26%)
  waiting for transfers between devices  150 us (17%)
  other arithmetic  130 us (14%)
  local copies, waits for them, and re-layouts  55 us (6%)
  between operations  41.6 us (5%)
    all_gather x4, waiting for transfers between devices, across(): return lax.all_gather(values, axes, axis=0, tiled=True)  150 us
    pallas_call x1, Pallas kernels, reduce_weights(): pl.pallas_call(functools.partial(reduce_kernel, (copies, groups)), out_sh...  131 us
    pallas_call x6, Pallas kernels, call(): pl.pallas_call(kernel, out_shape=[jax.ShapeDtypeStruct(shape, jnp.float32...  86.4 us
    dot_general x8, matrix products, product_left(): lax.dot_general(operand, other_operand, (((0,), (0,)), ((), ())), preferr...  73.2 us
    dot_general x7, matrix products, product_right(): lax.dot_general(operand, other_operand, (((1,), (1,)), ((), ())), preferr...  68.8 us
    dot_general x8, matrix products, product(): return jnp.dot(operand, other_operand, preferred_element_type=jnp.float32)  63.9 us
    pallas_call x1, Pallas kernels, attend_back(): pl.pallas_call(attend_back_kernel, grid_spec=pltpu.PrefetchScalarGridSpec...  38.4 us
    pallas_call x1, Pallas kernels, attend(): pl.pallas_call(attend_kernel, grid_spec=pltpu.PrefetchScalarGridSpec(num_...  30.3 us
  transfers between devices with their start and end apart: 5, of which 3 were waited for; matrix products, arithmetic and copies ran while one was open for 21% of the time, Pallas kernels for 26%

profile of v2, /device:TPU:0, one launch (start us, length us, event | category | flops | bytes accessed | tf_op | source)
XLA Modules:
  0.0 895.9 jit_solution(14256104233163704861)
XLA Ops:
  10.9 1.9 fusion.45
  12.9 1.9 fusion.44
  14.8 1.9 dynamic-slice_convert_fusion
  16.8 4.7 shard_map.378
  24.7 6.9 multiply_convert_fusion.3
  32.8 8.6 shard_map.379
  46.9 2.8 multiply_cosine_fusion
  53.8 2.0 add_convert_fusion.3
  55.8 47.3 %all-gather.5.cloned.1.call-done = bf16[4608,1152]{1,0:T(8,128)(2,1)} async-done(((bf16[144,1152]{1,0:T(8,128)(2,1)}), bf16[4608,1152]{1,0:T(8,128)(2,1)}) %all-gather.5.cloned.1.call-update) | async-done | bytes 10616848 | tf_op jit(solution)/shard_map/all_gather | solution.py:685
  103.1 14.6 %convolution_convert_fusion.4.q_ref.k_ref.v_ref = bf16[3456,1024]{1,0:T(8,128)(2,1)} fusion(bf16[1024,1152]{1,0:T(8,128)(2,1)S(1)} %bitcast.228, bf16[4608,1152]{1,0:T(8,128)(2,1)} %all-gather.5.cloned.1.call-done), kind=kOutput, calls=%fused_computation.18 | convolution fusion | flops 8157265920 | bytes 17399808 | tf_op jit(solution)/shard_map/dot_general | solution.py:32
  117.7 30.3 %shard_map.380 = bf16[1152,1024]{1,0:T(8,128)(2,1)S(1)} custom-call(s32[4]{0:T(128)S(1)} %dynamic_slice.83.length_ref, bf16[3456,1024]{1,0:T(8,128)(2,1)} %convolution_convert_fusion.4.q_ref.k_ref.v_ref, bf16[3456,1024]{1,0:T(8,128)(2,1)} %convolution_convert_fusion.4.q_ref.k_ref.v_ref, bf16[3456,1024]{1,0:T(8,128)(2,1)} %convolution_convert_fusion.4.q_ref.k_ref.v_ref), custom_call_target="tpu_custom_call" | custom-call | flops 1207959552 | bytes 9437184 | tf_op jit(solution)/shard_map/pallas_call | solution.py:652
  148.0 6.3 fusion.23
  158.9 2.0 add_convert_fusion.2
  160.9 31.8 %all-gather.7.cloned.1.call-done = bf16[4608,1152]{1,0:T(8,128)(2,1)} async-done(((bf16[144,1152]{1,0:T(8,128)(2,1)}), bf16[4608,1152]{1,0:T(8,128)(2,1)}) %all-gather.7.cloned.1.call-update) | async-done | bytes 10616848 | tf_op jit(solution)/shard_map/all_gather | solution.py:685
  192.7 18.8 %fusion.114 = f32[1024,4608]{1,0:T(8,128)} fusion(bf16[1024,1152]{1,0:T(8,128)(2,1)S(1)} %bitcast.230, bf16[4608,1152]{1,0:T(8,128)(2,1)} %all-gather.7.cloned.1.call-done), kind=kOutput, calls=%fused_computation.329 | convolution fusion | flops 10871635968 | bytes 31850496 | tf_op jit(solution)/shard_map/dot_general | solution.py:32
  211.5 70.7 %all-gather.9.cloned.1.call-done = bf16[4608,1152]{1,0:T(8,128)(2,1)} async-done(((bf16[144,1152]{1,0:T(8,128)(2,1)}), bf16[4608,1152]{1,0:T(8,128)(2,1)}) %all-gather.9.cloned.1.call-update) | async-done | bytes 10616848 | tf_op jit(solution)/shard_map/all_gather | solution.py:685
  282.1 22.5 %fusion.94 = f32[1024,1152]{1,0:T(8,128)S(1)} fusion(bf16[4608,1152]{1,0:T(8,128)(2,1)} %all-gather.9.cloned.1.call-done, f32[1024,4608]{1,0:T(8,128)} %fusion.114), kind=kOutput, calls=%fused_computation.313 | convolution fusion | flops 10914103296 | bytes 34209792 | tf_op jit(solution)/shard_map/dot_general | solution.py:28
  307.4 2.0 add_convert_fusion.1
  311.8 2.3 fusion.14
  314.1 6.6 multiply_reduce_fusion.1
  320.7 2.1 copy-done.11
  323.3 21.1 %convolution_convert_fusion = bf16[4608,1152]{1,0:T(8,128)(2,1)} fusion(bf16[1024,1152]{1,0:T(8,128)(2,1)S(1)} %bitcast.234, f32[1024,4608]{1,0:T(8,128)} %fusion.114), kind=kOutput, calls=%fused_computation.3 | convolution fusion | flops 10919411712 | bytes 31850496 | tf_op jit(solution)/shard_map/dot_general | solution.py:38
  344.4 26.3 %fusion.6 = bf16[1024,4608]{1,0:T(8,128)(2,1)S(1)} fusion(f32[1024,4608]{1,0:T(8,128)} %fusion.114, bf16[1024,1152]{1,0:T(8,128)(2,1)S(1)} %bitcast.235, bf16[4608,1152]{1,0:T(8,128)(2,1)} %all-gather.9.cloned.1.call-done), kind=kOutput, calls=%fused_computation.11 | convolution fusion | flops 10966007808 | bytes 41287680 | tf_op jit(solution)/shard_map/dot_general | solution.py:32
  370.8 20.7 %fusion.11 = (f32[1024]{0:T(1024)S(1)}, f32[1024,1152]{1,0:T(8,128)S(1)}) fusion(f32[4,1152]{1,0:T(4,128)S(1)} %bitcast.250, bf16[1024,4608]{1,0:T(8,128)(2,1)S(1)} %fusion.6, bf16[4608,1152]{1,0:T(8,128)(2,1)} %all-gather.7.cloned.1.call-done), kind=kOutput, calls=%fused_computation.26 | convolution fusion | flops 10873994240 | bytes 24795136 | tf_op jit(solution)/shard_map/dot_general | solution.py:28
  391.5 5.0 fusion.13
  396.6 7.4 multiply_reduce_fusion.2
  407.6 5.2 convolution_convert_fusion.5.up_ref
  412.9 38.4 %shard_map.381 = bf16[3,1152,1024]{2,1,0:T(8,128)(2,1)} custom-call(s32[4]{0:T(128)S(1)} %dynamic_slice.83.length_ref, bf16[3456,1024]{1,0:T(8,128)(2,1)} %convolution_convert_fusion.4.q_ref.k_ref.v_ref, bf16[3456,1024]{1,0:T(8,128)(2,1)} %convolution_convert_fusion.4.q_ref.k_ref.v_ref, bf16[3456,1024]{1,0:T(8,128)(2,1)} %convolution_convert_fusion.4.q_ref.k_ref.v_ref, ...), custom_call_target="tpu_custom_call" | custom-call | flops 3019898880 | bytes 16515072 | tf_op jit(solution)/shard_map/pallas_call | solution.py:670
  451.2 9.7 %copy.79 = bf16[1024,3456]{1,0:T(8,128)(2,1)} copy(bf16[1024,3456]{0,1:T(8,128)(2,1)} %bitcast.217) | data formatting | bytes 14155776 | tf_op jit(solution)/shard_map/dot_general | solution.py:38
  461.7 17.0 %multiply_reduce_fusion.3 = (bf16[4,1152]{1,0:T(4,128)(2,1)S(1)}, f32[4,256]{1,0:T(4,128)S(1)}, f32[4,256]{1,0:T(4,128)S(1)}, bf16[4,1152]{1,0:T(4,128)(2,1)S(1)}, f32[4,256,1152]{2,1,0:T(8,128)}) fusion(f32[4,256,1152]{2,1,0:T(8,128)} %copy-done.6, f32[4,256]{1,0:T(4,128)S(1)} %copy-done.87, f32[4,256]{1,0:T(4,128)S(1)} %copy-done.79, ...), kind=kOutput, calls=%fused_computation.37 | convolution fusion | flops 8164332544 | bytes 24530944 | tf_op jit(solution)/shard_map/dot_general | solution.py:38
  479.9 6.7 fusion.25
  487.3 18.6 %shard_map.382 = f32[32,36,128]{2,1,0:T(8,128)S(1)} custom-call(f32[8,36,128]{2,1,0:T(8,128)S(1)} %reshape.561.x_ref), custom_call_target="tpu_custom_call" | custom-call | tf_op jit(solution)/shard_map/pallas_call | solution.py:202
  506.3 2.7 fusion.29
  509.4 5.2 convolution_convert_fusion.3
  514.7 12.2 %convolution_convert_fusion.2 = bf16[3456,1152]{1,0:T(8,128)(2,1)S(1)} fusion(bf16[3456,1024]{1,0:T(8,128)(2,1)} %bitcast.218, bf16[1024,1152]{1,0:T(8,128)(2,1)S(1)} %bitcast.229), kind=kOutput, calls=%fused_computation.13 | convolution fusion | flops 8157708288 | bytes 17399808 | tf_op jit(solution)/shard_map/dot_general | solution.py:28
  527.0 15.6 %pad_maximum_fusion = bf16[4608,1152]{1,0:T(8,128)(2,1)} fusion(bf16[1152,1152]{1,0:T(8,128)(2,1)S(1)} %convolution_convert_fusion.3, bf16[3456,1152]{1,0:T(8,128)(2,1)S(1)} %convolution_convert_fusion.2), kind=kLoop, calls=%fused_computation.14 | loop fusion | flops 21233664 | bytes 21233664 | tf_op jit(solution)/shard_map/concatenate | solution.py:860
  542.6 14.8 %convolution_convert_fusion.1 = bf16[4608,1152]{1,0:T(8,128)(2,1)} fusion(bf16[1024,4608]{1,0:T(8,128)(2,1)S(1)} %bitcast.264, bf16[1024,1152]{1,0:T(8,128)(2,1)S(1)} %bitcast.231), kind=kOutput, calls=%fused_computation.4 | convolution fusion | flops 10876944384 | bytes 22413312 | tf_op jit(solution)/shard_map/dot_general | solution.py:38
  557.4 130.6 %shard_map.384 = (bf16[2,2,3,48,1152]{4,3,2,1,0:T(8,128)(2,1)}, bf16[2,2,3,48,1152]{4,3,2,1,0:T(8,128)(2,1)}) custom-call(bf16[2,2,4,2,3,48,1152]{6,5,4,3,2,1,0:T(8,128)(2,1)} %bitcast.223, bf16[2,2,4,2,3,48,1152]{6,5,4,3,2,1,0:T(8,128)(2,1)} %bitcast.213), custom_call_target="tpu_custom_call" | custom-call | tf_op jit(solution)/shard_map/pallas_call | solution.py:564
  690.4 39.1 %shard_map.383 = (f32[32,16,128]{2,1,0:T(8,128)S(1)}, f32[32,36,128]{2,1,0:T(8,128)S(1)}) custom-call(f32[32,16,128]{2,1,0:T(8,128)S(1)} %bitcast.208, f32[8,36,128]{2,1,0:T(8,128)S(1)} %reshape.547.mp_ref), custom_call_target="tpu_custom_call" | custom-call | tf_op jit(solution)/shard_map/pallas_call | solution.py:202
  732.7 3.4 multiply_reduce_fusion.15
  736.1 1.9 fusion.41
  743.8 7.9 fusion.92
  751.7 2.9 multiply_reduce_fusion.26
  756.0 9.1 %multiply_reduce_fusion.10 = (f32[1152]{0:T(1024)}, f32[1152]{0:T(1024)S(1)}, f32[]{:T(128)}, f32[1152,1152]{1,0:T(8,128)}) fusion(f32[128,1152]{1,0:T(8,128)S(1)} %copy-done.42, f32[128,1152]{1,0:T(8,128)S(1)} %copy-done.43, f32[128,1152]{1,0:T(8,128)} %copy-done.44), kind=kOutput, calls=%fused_computation.54 | convolution fusion | flops 2045654784 | bytes 7087108 | tf_op jit(solution)/shard_map/dot_general | solution.py:922
  767.7 3.0 multiply_reduce_fusion.23
  770.7 2.7 fusion.15
  774.8 7.4 shard_map.385
  783.5 3.0 slice_multiply_fusion
  796.7 2.7 multiply_reduce_fusion.29
  799.4 6.4 multiply_reduce_fusion.14
  808.5 1.9 multiply_reduce_fusion.21
  810.5 3.2 multiply_reduce_fusion.18
  813.7 4.0 concatenate.42
  817.6 8.0 shard_map.386
  834.4 1.9 multiply_reduce_fusion.22
  837.6 6.6 multiply_reduce_fusion
  847.2 4.0 multiply_subtract_fusion.4
  852.6 2.2 multiply_subtract_fusion.3
  858.9 2.1 multiply_subtract_fusion.8
  861.0 1.9 copy.87
  867.4 2.1 multiply_subtract_fusion.6
  869.4 6.5 multiply_subtract_fusion
  877.8 3.0 multiply_subtract_fusion.1
  882.3 2.2 multiply_subtract_fusion.2
  (432 shorter events, 70.2 us)
Async XLA Ops:
  7.2 14.7 %copy-start = (bf16[1000,1152]{1,0:T(8,128)(2,1)S(1)}, bf16[1000,1152]{1,0:T(8,128)(2,1)}, u32[]{:S(2)}) copy-start(bf16[1000,1152]{1,0:T(8,128)(2,1)} %param.25) | copy-start | bytes 6912004
  7.2 95.9 %all-gather.5.cloned.1.call-start = ((), (), s32[]{:S(2)}) async-start(), calls=%async_computation.1 | async-start | bytes 10948608 | tf_op jit(solution)/shard_map/all_gather | solution.py:685
  9.1 14.7 %copy-start.32 = (f32[256,1152]{1,0:T(8,128)S(1)}, f32[256,1152]{1,0:T(8,128)}, u32[]{:S(2)}) copy-start(f32[256,1152]{1,0:T(8,128)} %param.27) | copy-start | bytes 3538948
  12.8 179.9 %all-gather.7.cloned.1.call-start = ((), (), s32[]{:S(2)}) async-start(), calls=%async_computation.2 | async-start | bytes 10948608 | tf_op jit(solution)/shard_map/all_gather | solution.py:685
  14.8 267.4 %all-gather.9.cloned.1.call-start = ((), (), s32[]{:S(2)}) async-start(), calls=%async_computation.3 | async-start | bytes 10948608 | tf_op jit(solution)/shard_map/all_gather | solution.py:685
  16.7 719.4 %reduce-scatter.2.cloned.1.call-start = ((), (), s32[]{:S(2)}) async-start(), calls=%async_computation.4 | async-start | bytes 10948608 | tf_op jit(solution)/shard_map/reduce_scatter | solution.py:693
  31.6 10.0 %copy-start.115 = (s32[128]{0:T(128)S(1)}, s32[128]{0:T(128)}, u32[]{:S(2)}) copy-start(s32[128]{0:T(128)} %param.24) | copy-start | bytes 1540
  31.6 10.8 %copy-start.112 = (f32[32]{0:T(128)S(1)}, f32[32]{0:T(128)}, u32[]{:S(2)}) copy-start(f32[32]{0:T(128)} %param.21) | copy-start | bytes 388
  31.6 10.9 %copy-start.80 = (f32[4,256,16]{1,2,0:T(8,128)S(1)}, f32[4,256,16]{1,2,0:T(8,128)}, u32[]{:S(2)}) copy-start(f32[4,256,16]{1,2,0:T(8,128)} %param.20) | copy-start | bytes 196612
  31.6 10.9 %copy-start.81 = (f32[4,256,16]{1,2,0:T(8,128)S(1)}, f32[4,256,16]{1,2,0:T(8,128)}, u32[]{:S(2)}) copy-start(f32[4,256,16]{1,2,0:T(8,128)} %param.19) | copy-start | bytes 196612
  31.6 12.1 %copy-start.54 = (f32[1152,16]{0,1:T(8,128)S(1)}, f32[1152,16]{0,1:T(8,128)}, u32[]{:S(2)}) copy-start(f32[1152,16]{0,1:T(8,128)} %param.35) | copy-start | bytes 221188
  32.7 17.9 %copy-start.59 = (f32[16,1152]{1,0:T(8,128)S(1)}, f32[16,1152]{1,0:T(8,128)}, u32[]{:S(2)}) copy-start(f32[16,1152]{1,0:T(8,128)} %param.26) | copy-start | bytes 221188
  42.4 268.5 %copy-start.96 = (pred[1024]{0:T(1024)(128)(4,1)}, pred[1024]{0:T(1024)(128)(4,1)S(1)}, u32[]{:S(2)}) copy-start(pred[1024]{0:T(1024)(128)(4,1)S(1)} %lt.94) | copy-start | bytes 3076
  42.9 114.3 %copy-start.60 = (f32[4,1,1,1152]{3,0,1,2:T(4,128)}, f32[4,1,1,1152]{3,0,1,2:T(4,128)S(1)}, u32[]{:S(2)}) copy-start(f32[4,1,1,1152]{3,0,1,2:T(4,128)S(1)} %copy.112) | copy-start | bytes 55300
  52.2 65.4 %copy-start.86 = (f32[4,256]{1,0:T(4,128)}, f32[4,256]{1,0:T(4,128)S(1)}, u32[]{:S(2)}) copy-start(f32[4,256]{1,0:T(4,128)S(1)} %add_rsqrt_fusion.2) | copy-start | bytes 12292
  52.3 65.4 %copy-start.66 = (f32[4,1152]{1,0:T(4,128)}, f32[4,1152]{1,0:T(4,128)S(1)}, u32[]{:S(2)}) copy-start(f32[4,1152]{1,0:T(4,128)S(1)} %get-tuple-element.296) | copy-start | bytes 55300
  52.3 102.0 %copy-start.68 = (f32[4,1152]{1,0:T(4,128)}, f32[4,1152]{1,0:T(4,128)S(1)}, u32[]{:S(2)}) copy-start(f32[4,1152]{1,0:T(4,128)S(1)} %get-tuple-element.297) | copy-start | bytes 55300
  55.8 61.9 %copy-start.46 = (bf16[4,256,1152]{2,1,0:T(8,128)(2,1)}, bf16[4,256,1152]{2,1,0:T(8,128)(2,1)S(1)}, u32[]{:S(2)}) copy-start(bf16[4,256,1152]{2,1,0:T(8,128)(2,1)S(1)} %add_convert_fusion.3) | copy-start | bytes 7077892
  157.1 54.3 %copy-start.84 = (f32[4,256]{1,0:T(4,128)}, f32[4,256]{1,0:T(4,128)S(1)}, u32[]{:S(2)}) copy-start(f32[4,256]{1,0:T(4,128)S(1)} %add_rsqrt_fusion.1) | copy-start | bytes 12292
  160.9 50.5 %copy-start.48 = (bf16[4,256,1152]{2,1,0:T(8,128)(2,1)}, bf16[4,256,1152]{2,1,0:T(8,128)(2,1)S(1)}, u32[]{:S(2)}) copy-start(bf16[4,256,1152]{2,1,0:T(8,128)(2,1)S(1)} %add_convert_fusion.2) | copy-start | bytes 7077892
  282.1 22.5 %copy-start.5 = (f32[4,256,1152]{2,1,0:T(8,128)S(1)}, f32[4,256,1152]{2,1,0:T(8,128)}, u32[]{:S(2)}) copy-start(f32[4,256,1152]{2,1,0:T(8,128)} %copy-done.4) | copy-start | bytes 14155780
  344.4 26.3 %copy-start.61 = (f32[4,1,1,1152]{3,0,1,2:T(4,128)S(1)}, f32[4,1,1,1152]{3,0,1,2:T(4,128)}, u32[]{:S(2)}) copy-start(f32[4,1,1,1152]{3,0,1,2:T(4,128)} %copy-done.60) | copy-start | bytes 55300
  370.7 20.7 %copy-start.116 = (bf16[1024,4608]{1,0:T(8,128)(2,1)}, bf16[1024,4608]{1,0:T(8,128)(2,1)S(1)}, u32[]{:S(2)}) copy-start(bf16[1024,4608]{1,0:T(8,128)(2,1)S(1)} %fusion.6) | copy-start | bytes 28311556
  370.7 20.7 %copy-start.72 = (f32[4,256]{1,0:T(4,128)S(1)}, f32[4,256]{1,0:T(4,128)}, u32[]{:S(2)}) copy-start(f32[4,256]{1,0:T(4,128)} %copy-done.71) | copy-start | bytes 12292
  370.7 20.7 %copy-start.85 = (f32[4,256]{1,0:T(4,128)S(1)}, f32[4,256]{1,0:T(4,128)}, u32[]{:S(2)}) copy-start(f32[4,256]{1,0:T(4,128)} %copy-done.84) | copy-start | bytes 12292
  461.0 309.8 %all-gather.11.cloned.1.call-start = ((), (), s32[]{:S(2)}) async-start(), calls=%async_computation.5 | async-start | bytes 1658880 | tf_op jit(solution)/shard_map/all_gather | solution.py:685
  461.7 17.1 %copy-start.16 = (bf16[4,256,1152]{2,1,0:T(8,128)(2,1)S(1)}, bf16[4,256,1152]{2,1,0:T(8,128)(2,1)}, u32[]{:S(2)}) copy-start(bf16[4,256,1152]{2,1,0:T(8,128)(2,1)} %copy-done.15) | copy-start | bytes 7077892
  461.7 17.1 %copy-start.56 = (f32[1024,16]{0,1:T(8,128)S(1)}, f32[1024,16]{0,1:T(8,128)}, u32[]{:S(2)}) copy-start(f32[1024,16]{0,1:T(8,128)} %copy-done.55) | copy-start | bytes 196612
  461.7 17.1 %copy-start.97 = (pred[1024]{0:T(1024)(128)(4,1)S(1)}, pred[1024]{0:T(1024)(128)(4,1)}, u32[]{:S(2)}) copy-start(pred[1024]{0:T(1024)(128)(4,1)} %copy-done.96) | copy-start | bytes 3076
  487.0 22.4 %copy-start.3 = (bf16[1152,1024]{1,0:T(8,128)(2,1)S(1)}, bf16[1152,1024]{1,0:T(8,128)(2,1)}, u32[]{:S(2)}) copy-start(bf16[1152,1024]{1,0:T(8,128)(2,1)} %copy-done.2) | copy-start | bytes 7077892
  509.4 33.1 %slice-start = ((s8[9437184]{0:T(1024)(128)(4,1)}), s8[4194304]{0:T(1024)(128)(4,1)S(1)}, s32[]{:S(2)}) async-start(s8[9437184]{0:T(1024)(128)(4,1)} %bitcast.263), calls=%async_computation.6 | async-start | bytes 8388608
  514.7 27.8 %slice-start.1 = ((s8[9437184]{0:T(1024)(128)(4,1)}), s8[4194304]{0:T(1024)(128)(4,1)S(1)}, s32[]{:S(2)}) async-start(s8[9437184]{0:T(1024)(128)(4,1)} %bitcast.263), calls=%async_computation.7 | async-start | bytes 8388608
  514.7 27.8 %slice-start.2 = ((s8[9437184]{0:T(1024)(128)(4,1)}), s8[1048576]{0:T(1024)(128)(4,1)S(1)}, s32[]{:S(2)}) async-start(s8[9437184]{0:T(1024)(128)(4,1)} %bitcast.263), calls=%async_computation.8 | async-start | bytes 2097152
  527.0 15.6 %copy-start.49 = (bf16[4,256,1152]{2,1,0:T(8,128)(2,1)S(1)}, bf16[4,256,1152]{2,1,0:T(8,128)(2,1)}, u32[]{:S(2)}) copy-start(bf16[4,256,1152]{2,1,0:T(8,128)(2,1)} %copy-done.48) | copy-start | bytes 7077892
  688.0 42.7 %copy-start.31 = (bf16[2,2,3,48,1152]{4,3,2,1,0:T(8,128)(2,1)S(1)}, bf16[2,2,3,48,1152]{4,3,2,1,0:T(8,128)(2,1)}, u32[]{:S(2)}) copy-start(bf16[2,2,3,48,1152]{4,3,2,1,0:T(8,128)(2,1)} %get-tuple-element.31) | copy-start | bytes 3981316
  688.0 44.7 %copy-start.36 = (bf16[128,1152]{1,0:T(8,128)(2,1)S(1)}, bf16[128,1152]{1,0:T(8,128)(2,1)}, u32[]{:S(2)}) copy-start(bf16[128,1152]{1,0:T(8,128)(2,1)} %copy-done.35) | copy-start | bytes 884740
  688.0 44.7 %copy-start.52 = (bf16[128,1152]{1,0:T(8,128)(2,1)S(1)}, bf16[128,1152]{1,0:T(8,128)(2,1)}, u32[]{:S(2)}) copy-start(bf16[128,1152]{1,0:T(8,128)(2,1)} %copy-done.51) | copy-start | bytes 884740
  689.7 39.8 %copy-start.17 = (f32[576,1152]{1,0:T(8,128)}, f32[576,1152]{1,0:T(8,128)S(1)}, u32[]{:S(2)}) copy-start(f32[576,1152]{1,0:T(8,128)S(1)} %convert.52) | copy-start | bytes 7962628
  730.6 13.2 %copy-start.42 = (f32[128,1152]{1,0:T(8,128)S(1)}, f32[128,1152]{1,0:T(8,128)}, u32[]{:S(2)}) copy-start(f32[128,1152]{1,0:T(8,128)} %get-tuple-element.278) | copy-start | bytes 1769476
  738.0 13.7 %copy-start.63 = (f32[128,128]{1,0:T(8,128)S(1)}, f32[128,128]{1,0:T(8,128)}, u32[]{:S(2)}) copy-start(f32[128,128]{1,0:T(8,128)} %copy-done.62) | copy-start | bytes 196612
  738.0 13.7 %copy-start.65 = (f32[128,128]{1,0:T(8,128)S(1)}, f32[128,128]{1,0:T(8,128)}, u32[]{:S(2)}) copy-start(f32[128,128]{1,0:T(8,128)} %copy-done.64) | copy-start | bytes 196612
  743.8 12.1 %copy-start.43 = (f32[128,1152]{1,0:T(8,128)S(1)}, f32[128,1152]{1,0:T(8,128)}, u32[]{:S(2)}) copy-start(f32[128,1152]{1,0:T(8,128)} %reshape.551) | copy-start | bytes 1769476
  755.9 10.4 %copy-start.95 = (f32[6913]{0:T(1024)S(1)}, f32[6913]{0:T(1024)}, u32[]{:S(2)}) copy-start(f32[6913]{0:T(1024)} %custom-call.1) | copy-start | bytes 82960
  770.7 18.1 %copy-start.70 = (f32[12944]{0:T(1024)S(1)}, f32[12944]{0:T(1024)}, u32[]{:S(2)}) copy-start(f32[12944]{0:T(1024)} %param.36) | copy-start | bytes 155332
  786.5 9.6 %copy-start.94 = (f32[23056]{0:T(1024)S(1)}, f32[23056]{0:T(1024)}, u32[]{:S(2)}) copy-start(f32[23056]{0:T(1024)} %param.37) | copy-start | bytes 276676
  786.5 9.6 %copy-start.113 = (f32[23056]{0:T(1024)S(1)}, f32[23056]{0:T(1024)}, u32[]{:S(2)}) copy-start(f32[23056]{0:T(1024)} %custom-call) | copy-start | bytes 276676
  786.5 9.6 %copy-start.104 = (f32[1152]{0:T(1024)S(1)}, f32[1152]{0:T(1024)}, u32[]{:S(2)}) copy-start(f32[1152]{0:T(1024)} %get-tuple-element.164) | copy-start | bytes 13828
  786.5 9.6 %copy-start.105 = (f32[1152]{0:T(1024)S(1)}, f32[1152]{0:T(1024)}, u32[]{:S(2)}) copy-start(f32[1152]{0:T(1024)} %get-tuple-element.135) | copy-start | bytes 13828
  786.5 9.8 %copy-start.107 = (f32[144]{0:T(256)S(1)}, f32[144]{0:T(256)}, u32[]{:S(2)}) copy-start(f32[144]{0:T(256)} %get-tuple-element.149) | copy-start | bytes 1732
  792.7 13.0 %copy-start.22 = (f32[2,3,72,1152]{3,2,1,0:T(8,128)}, f32[2,3,72,1152]{3,2,1,0:T(8,128)S(1)}, u32[]{:S(2)}) copy-start(f32[2,3,72,1152]{3,2,1,0:T(8,128)S(1)} %copy.84) | copy-start | bytes 5971972
  796.1 33.5 %copy-start.75 = (f32[1152]{0:T(1024)}, f32[1152]{0:T(1024)S(1)}, u32[]{:S(2)}) copy-start(f32[1152]{0:T(1024)S(1)} %get-tuple-element.181) | copy-start | bytes 13828
  796.1 38.3 %copy-start.74 = (f32[1152]{0:T(1024)}, f32[1152]{0:T(1024)S(1)}, u32[]{:S(2)}) copy-start(f32[1152]{0:T(1024)S(1)} %get-tuple-element.179) | copy-start | bytes 13828
  796.2 41.4 %copy-start.76 = (f32[1152]{0:T(1024)}, f32[1152]{0:T(1024)S(1)}, u32[]{:S(2)}) copy-start(f32[1152]{0:T(1024)S(1)} %get-tuple-element.239) | copy-start | bytes 13828
  796.4 17.2 %copy-start.100 = (f32[144]{0:T(256)}, f32[144]{0:T(256)S(1)}, u32[]{:S(2)}) copy-start(f32[144]{0:T(256)S(1)} %add_multiply_fusion.10) | copy-start | bytes 1732
  796.6 17.1 %copy-start.82 = (f32[576]{0:T(1024)}, f32[576]{0:T(1024)S(1)}, u32[]{:S(2)}) copy-start(f32[576]{0:T(1024)S(1)} %add_multiply_fusion.5) | copy-start | bytes 6916
  796.7 17.0 %copy-start.91 = (f32[288]{0:T(512)}, f32[288]{0:T(512)S(1)}, u32[]{:S(2)}) copy-start(f32[288]{0:T(512)S(1)} %add_multiply_fusion.8) | copy-start | bytes 3460
  808.5 20.5 %copy-start.108 = (f32[16]{0:T(128)S(1)}, f32[16]{0:T(128)}, u32[]{:S(2)}) copy-start(f32[16]{0:T(128)} %reduce_sum.748) | copy-start | bytes 196
  808.5 24.5 %copy-start.109 = (f32[256]{0:T(256)S(1)}, f32[256]{0:T(256)}, u32[]{:S(2)}) copy-start(f32[256]{0:T(256)} %get-tuple-element.165) | copy-start | bytes 3076
  808.5 25.9 %copy-start.53 = (f32[256,1152]{1,0:T(8,128)S(1)}, f32[256,1152]{1,0:T(8,128)}, u32[]{:S(2)}) copy-start(f32[256,1152]{1,0:T(8,128)} %get-tuple-element.290) | copy-start | bytes 3538948
  828.9 15.3 %copy-start.114 = (f32[23056]{0:T(1024)}, f32[23056]{0:T(1024)S(1)}, u32[]{:S(2)}) copy-start(f32[23056]{0:T(1024)S(1)} %get-tuple-element.174) | copy-start | bytes 276676
  833.7 10.5 %copy-start.98 = (f32[256]{0:T(256)}, f32[256]{0:T(256)S(1)}, u32[]{:S(2)}) copy-start(f32[256]{0:T(256)S(1)} %get-tuple-element.209) | copy-start | bytes 3076
  854.8 12.6 %copy-start.33 = (f32[256,1152]{1,0:T(8,128)S(1)}, f32[256,1152]{1,0:T(8,128)}, u32[]{:S(2)}) copy-start(f32[256,1152]{1,0:T(8,128)} %param.27) | copy-start | bytes 3538948
  854.8 12.6 %copy-start.34 = (f32[256,1152]{1,0:T(8,128)S(1)}, f32[256,1152]{1,0:T(8,128)}, u32[]{:S(2)}) copy-start(f32[256,1152]{1,0:T(8,128)} %get-tuple-element.207) | copy-start | bytes 3538948
  854.8 14.7 %copy-start.77 = (f32[1152]{0:T(1024)S(1)}, f32[1152]{0:T(1024)}, u32[]{:S(2)}) copy-start(f32[1152]{0:T(1024)} %copy-done.76) | copy-start | bytes 13828
  (61 other events, 294.5 us)
Sparse Core Ops, SparseCore 0:
  12.9 90.1 all-gather.4
  106.7 85.9 all-gather.6
  196.3 85.8 all-gather.8
  461.1 151.6 reduce-scatter.1
  736.2 17.1 all-gather.10

commit v3 on v2

--- a/solution.py
+++ b/solution.py
@@ -140,57 +140,6 @@
     wait = to_all(span, pick, lambda place: out_ref.at[place], send_sems, recv_sems)
     out_ref[here] = x_ref[lax.rem(here, groups)] if per_target else x_ref[...]
     wait()
-
-
-def total_kernel(span, x_ref, out_ref, land, send_sems, recv_sems):
-    here, _, _ = peers(span)
-    greet(span)
-    wait = to_all(span, lambda place: x_ref, lambda place: land.at[place], send_sems, recv_sems)
-    land[here] = x_ref[...]
-    wait()
-    out_ref[...] = sum_over(land)
-
-
-def both_kernel(all_ref, mp_ref, all_out, mp_out, all_land, mp_land, send_sems, recv_sems):
-    here, _, _ = peers("all")
-    member, _, _ = peers("mp")
-    greet("all")
-    wait_all = to_all(
-        "all",
-        lambda place: all_ref.at[place],
-        lambda place: all_land.at[place],
-        send_sems.at[0],
-        recv_sems.at[0],
-    )
-    wait_mp = to_all(
-        "mp",
-        lambda place: mp_ref.at[place],
-        lambda place: mp_land.at[place],
-        send_sems.at[1],
-        recv_sems.at[1],
-    )
-    all_land[here] = all_ref[here]
-    mp_land[member] = mp_ref[member]
-    wait_mp()
-    mp_out[here] = sum_over(mp_land)
-    wait_mp = to_all(
-        "all",
-        lambda place: mp_out.at[here],
-        lambda place: mp_out.at[place],
-        send_sems.at[2],
-        recv_sems.at[2],
-    )
-    wait_all()
-    all_out[here] = sum_over(all_land)
-    wait_all = to_all(
-        "all",
-        lambda place: all_out.at[here],
-        lambda place: all_out.at[place],
-        send_sems.at[3],
-        recv_sems.at[3],
-    )
-    wait_mp()
-    wait_all()
 
 
 def group_size(span):
@@ -224,38 +173,6 @@
     return result
 
 
-def total(values, span, collective_id):
-    size = group_size(span)
-    (result,) = call(
-        functools.partial(total_kernel, span),
-        [values],
-        [values.shape],
-        [
-            pltpu.VMEM((size,) + values.shape, jnp.float32),
-            pltpu.SemaphoreType.DMA((size,)),
-            pltpu.SemaphoreType.DMA((size,)),
-        ],
-        collective_id,
-    )
-    return result
-
-
-def both_totals(for_all, for_mp, collective_id):
-    size = group_size("all")
-    return call(
-        both_kernel,
-        [for_all, for_mp],
-        [for_all.shape, (size,) + for_mp.shape[1:]],
-        [
-            pltpu.VMEM(for_all.shape, jnp.float32),
-            pltpu.VMEM(for_mp.shape, jnp.float32),
-            pltpu.SemaphoreType.DMA((4, size)),
-            pltpu.SemaphoreType.DMA((4, size)),
-        ],
-        collective_id,
-    )
-
-
 def slabs(flat, blocks):
     chunk = 1024 * blocks
     short = (-flat.shape[0]) % chunk
@@ -265,10 +182,15 @@
 def reduce_kernel(counts, *refs):
     copies, groups = counts
     lines = {"a": 4, "b": groups // 4, "y": copies // 2}
-    chunks = (len(refs) - 8) // 2
+    chunks = (len(refs) - 20) // 2
     parts = refs[:chunks]
-    outs = refs[chunks : 2 * chunks]
-    held, twin, first_b, first_y, second, third, send_sems, recv_sems = refs[2 * chunks :]
+    back_ref, low_ref, shared_ref = refs[chunks : chunks + 3]
+    outs = refs[chunks + 3 : 2 * chunks + 3]
+    cols_out, shared_out, signal_out = refs[2 * chunks + 3 : 2 * chunks + 6]
+    held, twin, first_b, first_y, second, third, send_sems, recv_sems = refs[
+        2 * chunks + 6 : 2 * chunks + 14
+    ]
+    shared_land, signal_land, signal_part, stack, side_sends, side_recvs = refs[2 * chunks + 14 :]
     splits = parts[0].shape[4]
     dp, mp = lax.axis_index("dp"), lax.axis_index("mp")
     at = {"a": mp // lines["b"], "b": lax.rem(mp, lines["b"]), "y": dp // 2}
@@ -278,20 +200,46 @@
         place = {**at, "core": core, **moved}
         return (place["y"] * 2 + place["core"], place["a"] * lines["b"] + place["b"])
 
-    barrier = pltpu.get_barrier_semaphore()
-    pl.semaphore_signal(barrier, inc=1, device_id=device(core=1 - core), device_id_type=MESH)
-    for axis, size in lines.items():
-        for step in range(1, size):
-            if axis != "y" and step not in (1, size - 1):
-                continue
-            other = lax.rem(at[axis] + step, size)
-            pl.semaphore_signal(
-                barrier, inc=1, device_id=device(**{axis: other}), device_id_type=MESH
-            )
-    total = 1 + sum(
-        (size - 1) if axis == "y" else len({1, size - 1} - {0}) for axis, size in lines.items()
-    )
-    pl.semaphore_wait(barrier, total)
+    greet("all")
+
+    here = dp * groups + mp
+    waits = []
+
+    def side(slot, span, pick, landing):
+        waits.append(to_all(span, pick, landing, side_sends.at[slot], side_recvs.at[slot]))
+
+    def side_start():
+        side(0, "all", lambda place: back_ref.at[lax.rem(place, groups)], cols_out_at)
+        side(1, "all", lambda place: shared_ref.at[place], lambda place: shared_land.at[place])
+        cols_out[here] = back_ref[mp]
+        shared_land[here] = shared_ref[here]
+
+    def cols_out_at(place):
+        return cols_out.at[place]
+
+    def side_signal():
+        waits[0]()
+        images = cols_out.shape[1]
+        stack[...] = jnp.zeros_like(stack)
+        for member in range(groups):
+            stack[8 * member : 8 * member + images] = cols_out[dp * groups + member]
+        found = product_right(stack[...].astype(jnp.bfloat16), low_ref[...])
+        for member in range(groups):
+            signal_part[member] = found[8 * member : 8 * member + images]
+        signal_land[mp] = signal_part[mp]
+        side(2, "mp", lambda place: signal_part.at[place], lambda place: signal_land.at[place])
+
+    def side_show():
+        waits[1]()
+        shared_out[here] = sum_over(shared_land)
+        side(3, "all", lambda place: shared_out.at[here], lambda place: shared_out.at[place])
+        waits[2]()
+        signal_out[here] = sum_over(signal_land)
+        side(4, "all", lambda place: signal_out.at[here], lambda place: signal_out.at[place])
+
+    def side_end():
+        waits[3]()
+        waits[4]()
 
     units = [(chunk, split) for chunk in range(chunks) for split in range(splits)]
     slots = {}
@@ -528,6 +476,7 @@
     for unit in range(len(units)):
         twin_copy(unit).start()
         held_copy(unit).start()
+    side_start()
     queues = [unit_tasks(unit) for unit in range(len(units))]
     depth = len(queues[0])
     for tick in range(len(units) + depth - 1):
@@ -535,9 +484,14 @@
             task = tick - unit
             if 0 <= task < depth:
                 queues[unit][task]()
-
-
-def reduce_weights(partials, collective_id):
+        if tick == 1:
+            side_signal()
+        if tick == 3:
+            side_show()
+    side_end()
+
+
+def reduce_weights(partials, back, low_weights, shared, collective_id):
     copies, groups = lax.axis_size("dp"), lax.axis_size("mp")
     rows, width = partials[0].shape
     size_b, size_y = groups // 4, copies // 2
@@ -560,18 +514,489 @@
         pltpu.VMEM((units, 6, 1) + slab, jnp.bfloat16),
         pltpu.SemaphoreType.DMA((units, 40)),
         pltpu.SemaphoreType.DMA((units, 40)),
+        pltpu.VMEM(shared.shape, jnp.float32),
+        pltpu.VMEM((groups, back.shape[1], width), jnp.float32),
+        pltpu.VMEM((groups, back.shape[1], width), jnp.float32),
+        pltpu.VMEM((8 * groups, back.shape[2]), jnp.float32),
+        pltpu.SemaphoreType.DMA((5, copies * groups)),
+        pltpu.SemaphoreType.DMA((5, copies * groups)),
     ]
     results = pl.pallas_call(
         functools.partial(reduce_kernel, (copies, groups)),
-        out_shape=[jax.ShapeDtypeStruct((size_y, 2, splits) + slab, jnp.bfloat16)] * len(partials),
-        in_specs=[pl.BlockSpec(memory_space=pl.ANY)] * len(partials),
-        out_specs=[pl.BlockSpec(memory_space=pltpu.VMEM)] * len(partials),
+        out_shape=[jax.ShapeDtypeStruct((size_y, 2, splits) + slab, jnp.bfloat16)] * len(partials)
+        + [
+            jax.ShapeDtypeStruct((copies * groups,) + back.shape[1:], jnp.float32),
+            jax.ShapeDtypeStruct(shared.shape, jnp.float32),
+            jax.ShapeDtypeStruct((copies * groups, back.shape[1], width), jnp.float32),
+        ],
+        in_specs=[pl.BlockSpec(memory_space=pl.ANY)] * len(partials)
+        + [pl.BlockSpec(memory_space=pltpu.VMEM)] * 3,
+        out_specs=[pl.BlockSpec(memory_space=pltpu.VMEM)] * (len(partials) + 3),
         scratch_shapes=scratch,
         compiler_params=pltpu.CompilerParams(
             collective_id=collective_id, has_side_effects=True, vmem_limit_bytes=60 * 1024 * 1024
         ),
-    )(*shaped)
-    return [result.reshape(copies * piece, width) for result in results]
+    )(*shaped, back, low_weights, shared)
+    sums = [result.reshape(copies * piece, width) for result in results[: len(partials)]]
+    return sums, *results[len(partials) :]
+
+
+def gather_kernel(counts, piece_ref, out_ref, send_sems, recv_sems, local_sems):
+    copies, groups = counts
+    size_a, size_b, size_y = 4, groups // 4, copies // 2
+    splits = piece_ref.shape[0]
+    dp, mp = lax.axis_index("dp"), lax.axis_index("mp")
+    a, b, y, core = mp // size_b, lax.rem(mp, size_b), dp // 2, lax.rem(dp, 2)
+
+    def device(a=a, b=b, y=y, core=core):
+        return (y * 2 + core, a * size_b + b)
+
+    def along(axis, step):
+        if axis == "a":
+            return device(a=lax.rem(a + step, size_a))
+        if axis == "b":
+            return device(b=lax.rem(b + step, size_b))
+        return device(y=lax.rem(y + step, size_y))
+
+    lines = {"a": size_a, "b": size_b, "y": size_y}
+    barrier = pltpu.get_barrier_semaphore()
+    pl.semaphore_signal(barrier, inc=1, device_id=device(core=1 - core), device_id_type=MESH)
+    for axis, size in lines.items():
+        for step in range(1, size):
+            pl.semaphore_signal(
+                barrier, inc=1, device_id=along(axis, step), device_id_type=MESH
+            )
+    pl.semaphore_wait(barrier, 1 + sum(size - 1 for size in lines.values()))
+    slots = {}
+
+    def place(split, ys, cores, as_, bs):
+        return out_ref.at[ys, cores, as_, bs, split]
+
+    def own_copy(split):
+        return pltpu.make_async_copy(
+            piece_ref.at[split], place(split, y, core, a, b), local_sems.at[split]
+        )
+
+    def a_copies(split):
+        copies_ = []
+        for step in range(1, size_a):
+            slot = slots.setdefault(("a", step), len(slots))
+            copies_.append(
+                pltpu.make_async_remote_copy(
+                    src_ref=piece_ref.at[split],
+                    dst_ref=place(split, y, core, a, b),
+                    send_sem=send_sems.at[split, slot],
+                    recv_sem=recv_sems.at[split, slot],
+                    device_id=along("a", step),
+                    device_id_type=MESH,
+                )
+            )
+        return copies_
+
+    low, high = pl.ds(0, 2), pl.ds(2, 2)
+    every_b, every_y, every_a = pl.ds(0, size_b), pl.ds(0, size_y), pl.ds(0, size_a)
+
+    def spread(split, name, axis, source):
+        copies_ = []
+        for step in range(1, lines[axis]):
+            slot = slots.setdefault((name, step), len(slots))
+            copies_.append(
+                pltpu.make_async_remote_copy(
+                    src_ref=source,
+                    dst_ref=source,
+                    send_sem=send_sems.at[split, slot],
+                    recv_sem=recv_sems.at[split, slot],
+                    device_id=along(axis, step),
+                    device_id_type=MESH,
+                )
+            )
+        return copies_
+
+    def first(split):
+        return (
+            spread(split, "low_b", "b", place(split, y, core, low, b)),
+            spread(split, "high_y", "y", place(split, y, core, high, b)),
+        )
+
+    def second(split):
+        return (
+            spread(split, "low_y", "y", place(split, y, core, low, every_b)),
+            spread(split, "high_b", "b", place(split, every_y, core, high, b)),
+        )
+
+    def twin(split):
+        slot = slots.setdefault("twin", len(slots))
+        source = place(split, every_y, core, every_a, every_b)
+        return pltpu.make_async_remote_copy(
+            src_ref=source,
+            dst_ref=source,
+            send_sem=send_sems.at[split, slot],
+            recv_sem=recv_sems.at[split, slot],
+            device_id=device(core=1 - core),
+            device_id_type=MESH,
+        )
+
+    for split in range(splits):
+        own_copy(split).start()
+        for item in a_copies(split):
+            item.start()
+
+    def to_first(split):
+        own_copy(split).wait()
+        for item in a_copies(split):
+            item.wait_recv()
+        for items in first(split):
+            for item in items:
+                item.start()
+
+    def to_second(split):
+        for items, following in zip(first(split), second(split)):
+            for item in items:
+                item.wait_recv()
+            for item in following:
+                item.start()
+
+    def to_twin(split):
+        for items in second(split):
+            for item in items:
+                item.wait_recv()
+        twin(split).start()
+
+    stages = (to_first, to_second, to_twin)
+    for tick in range(splits + len(stages) - 1):
+        for split in reversed(range(splits)):
+            if 0 <= tick - split < len(stages):
+                stages[tick - split](split)
+    for split in range(splits):
+        twin(split).wait()
+        for item in a_copies(split):
+            item.wait_send()
+        for items in first(split) + second(split):
+            for item in items:
+                item.wait_send()
+
+
+def gather_pieces(piece, collective_id):
+    copies, groups = lax.axis_size("dp"), lax.axis_size("mp")
+    rows, width = piece.shape
+    share = 48 if rows % 48 == 0 else rows
+    splits = rows // share
+    size_b, size_y = groups // 4, copies // 2
+    sems = 4 + 2 * (size_b + size_y)
+    gathered = pl.pallas_call(
+        functools.partial(gather_kernel, (copies, groups)),
+        out_shape=jax.ShapeDtypeStruct(
+            (size_y, 2, 4, size_b, splits, share, width), jnp.bfloat16
+        ),
+        in_specs=[pl.BlockSpec(memory_space=pl.ANY)],
+        out_specs=pl.BlockSpec(memory_space=pl.ANY),
+        scratch_shapes=[
+            pltpu.SemaphoreType.DMA((splits, sems)),
+            pltpu.SemaphoreType.DMA((splits, sems)),
+            pltpu.SemaphoreType.DMA((splits,)),
+        ],
+        compiler_params=pltpu.CompilerParams(collective_id=collective_id, has_side_effects=True),
+    )(piece.reshape(splits, share, width))
+    return gathered.reshape(copies * groups * rows, width)
+
+
+def row_block(rows):
+    for block in (128, 144):
+        if rows % block == 0:
+            return block
+    return rows
+
+
+def scale_kernel(layouts, flipped, *refs):
+    slots = len(layouts)
+    grads = refs[:slots]
+    row_old, column_old = refs[slots : slots + 2]
+    row_coef, column_coef, row_new, column_new, shown, norms = refs[slots + 2 : slots + 8]
+    by_row, land, mine, send_sems, recv_sems = refs[slots + 8 :]
+    member, groups, _ = peers("mp")
+    wide = row_old.shape[1]
+    lane = lax.broadcasted_iota(jnp.int32, (1, 128), 1)
+    place = lax.broadcasted_iota(jnp.int32, (1, wide), 1)
+    split = [slot for slot in range(slots) if layouts[slot] != "whole"]
+    one = jnp.ones((1, 1), jnp.float32)
+
+    def all_sum(values):
+        return jnp.sum(jnp.sum(values, axis=1, keepdims=True), axis=0, keepdims=True)
+
+    greet("mp")
+    by_row[...] = jnp.zeros_like(by_row)
+    column_sums = []
+    squares = []
+    for slot in range(slots):
+        count, across_ = grads[slot].shape
+        block = row_block(count)
+
+        def step(index, total, slot=slot, block=block):
+            at = pl.ds(pl.multiple_of(index * block, block), block)
+            values = grads[slot][at, :].astype(jnp.float32)
+            square = values * values
+            by_row[at, :] += jnp.where(lane == slot, jnp.sum(square, axis=1, keepdims=True), 0.0)
+            return total + jnp.sum(square, axis=0, keepdims=True)
+
+        total = lax.fori_loop(0, count // block, step, jnp.zeros((1, across_), jnp.float32))
+        column_sums.append(total)
+        squares.append(jnp.sum(total, axis=1, keepdims=True))
+    row_sums = by_row[...].T
+
+    mine[...] = jnp.zeros_like(mine)
+    for index, slot in enumerate(split):
+        mine[0, index : index + 1, :] = column_sums[slot]
+    mine[0, 6:7, :] = sum(squares[slot] for slot in split) * jnp.ones((1, wide), jnp.float32)
+    wait = to_all(
+        "mp",
+        lambda place_: mine.at[0],
+        lambda place_: land.at[place_],
+        send_sems.at[0],
+        recv_sems.at[0],
+    )
+    land[member] = mine[0]
+    wait()
+    crossed = sum_over(land)
+    local_square = sum(squares[slot] for slot in range(slots) if slot not in split)
+    norm = jnp.sqrt(crossed[6:7, :1] + local_square)
+    factor = clip_limit / jnp.maximum(norm, clip_limit)
+    factor_square = factor * factor
+    norms[...] = jnp.where(lax.broadcasted_iota(jnp.int32, (8, 128), 0) == 0, norm, factor)
+
+    averages = []
+    many = []
+    next_rows = []
+    next_columns = []
+    inverse = [jnp.ones((1, wide), jnp.float32)] * slots
+    for slot, layout in enumerate(layouts):
+        count, across_ = grads[slot].shape
+        many_rows = count * (groups if layout == "rows" else 1)
+        many_columns = across_
+        many.append((many_rows, many_columns))
+        row_sum = row_sums[slot : slot + 1, :]
+        column_sum = column_sums[slot]
+        if layout == "rows":
+            column_sum = crossed[split.index(slot) : split.index(slot) + 1, :]
+        row_mean = row_sum * factor_square / many_columns + eps_factor
+        column_mean = column_sum * factor_square / many_rows + eps_factor
+        next_row = state_decay * row_old[slot : slot + 1, :] + (1.0 - state_decay) * row_mean
+        next_column = (
+            state_decay * column_old[slot : slot + 1, :across_] + (1.0 - state_decay) * column_mean
+        )
+        if flipped[slot]:
+            average = jnp.sum(next_column, axis=1, keepdims=True) / across_
+        elif layout == "rows":
+            first = slots + sum(
+                many[other][0] // wide for other in split if other < slot and not flipped[other]
+            )
+            old = row_old[first : first + many_rows // wide, :]
+            average = (
+                state_decay * all_sum(old) / many_rows
+                + (1.0 - state_decay) * jnp.sum(column_mean, axis=1, keepdims=True) / across_
+            )
+        else:
+            average = (
+                jnp.sum(jnp.where(place < count, next_row, 0.0), axis=1, keepdims=True) / many_rows
+            )
+        averages.append(average)
+        next_rows.append(next_row)
+        next_columns.append(next_column)
+        row_new[slot : slot + 1, :] = next_row
+        column_new[slot : slot + 1, :] = next_column
+        inverse[slot] = jnp.where(place < count, 1.0 / next_row, 0.0)
+    blank = jnp.zeros((128 - slots, wide), jnp.float32)
+    by_row[...] = jnp.concatenate(inverse + [blank], axis=0).T
+
+    energies = []
+    for slot in range(slots):
+        count, across_ = grads[slot].shape
+        block = row_block(count)
+        inverse_column = 1.0 / next_columns[slot]
+
+        def step(index, total, slot=slot, block=block, inverse_column=inverse_column):
+            at = pl.ds(pl.multiple_of(index * block, block), block)
+            values = grads[slot][at, :].astype(jnp.float32)
+            weighted = jnp.sum(values * values * inverse_column, axis=1, keepdims=True)
+            return total + jnp.sum(
+                jnp.where(lane == slot, by_row[at, :], 0.0) * weighted, axis=0, keepdims=True
+            )
+
+        total = lax.fori_loop(0, count // block, step, jnp.zeros((1, 128), jnp.float32))
+        energies.append(
+            jnp.sum(total, axis=1, keepdims=True) * factor_square * averages[slot]
+        )
+
+    mine[1, :, :] = jnp.zeros_like(mine[1])
+    for index, slot in enumerate(split):
+        mine[1, index : index + 1, :] = next_rows[slot]
+    spread = jnp.zeros((1, wide), jnp.float32)
+    for slot in split:
+        spread = jnp.where(place == slot, energies[slot], spread)
+    mine[1, 6:7, :] = spread
+    wait = to_all(
+        "mp",
+        lambda place_: mine.at[1],
+        lambda place_: shown.at[place_],
+        send_sems.at[1],
+        recv_sems.at[1],
+    )
+    shown[member] = mine[1]
+    wait()
+    spread = sum_over(shown)[6:7, :]
+    coefs = []
+    for slot, layout in enumerate(layouts):
+        many_rows, many_columns = many[slot]
+        energy = energies[slot]
+        if layout != "whole":
+            energy = jnp.sum(jnp.where(place == slot, spread, 0.0), axis=1, keepdims=True)
+        scale_down = jnp.maximum(one, jnp.sqrt(energy / (many_rows * many_columns)))
+        shrink = (
+            step_rate / math.sqrt(many[slot][1 if flipped[slot] else 0]) * factor * jnp.sqrt(averages[slot]) / scale_down
+        )
+        coefs.append(shrink * lax.rsqrt(next_rows[slot]))
+        column_coef[slot : slot + 1, :] = lax.rsqrt(next_columns[slot])
+    row_coef[...] = jnp.concatenate(coefs + [blank], axis=0).T
+
+
+def scales(gradients, row_old, column_old, layouts, flipped, collective_id):
+    groups = lax.axis_size("mp")
+    wide = row_old.shape[1]
+    shape = lambda *dims: jax.ShapeDtypeStruct(dims, jnp.float32)
+    vmem = pl.BlockSpec(memory_space=pltpu.VMEM)
+    return pl.pallas_call(
+        functools.partial(scale_kernel, layouts, flipped),
+        out_shape=[
+            shape(wide, 128),
+            shape(16, wide),
+            shape(16, wide),
+            shape(16, wide),
+            shape(groups, 8, wide),
+            shape(8, 128),
+        ],
+        in_specs=[vmem] * (len(gradients) + 2),
+        out_specs=[vmem] * 6,
+        scratch_shapes=[
+            pltpu.VMEM((wide, 128), jnp.float32),
+            pltpu.VMEM((groups, 8, wide), jnp.float32),
+            pltpu.VMEM((2, 8, wide), jnp.float32),
+            pltpu.SemaphoreType.DMA((2, groups)),
+            pltpu.SemaphoreType.DMA((2, groups)),
+        ],
+        compiler_params=pltpu.CompilerParams(
+            collective_id=collective_id, has_side_effects=True, vmem_limit_bytes=56 * 1024 * 1024
+        ),
+    )(*gradients, row_old, column_old)
+
+
+def apply_kernel(layouts, flipped, groups, *refs):
+    slots = len(layouts)
+    grads, weights = refs[:slots], refs[slots : 2 * slots]
+    row_coef, column_coef, row_new, column_new, shown, norms = refs[2 * slots : 2 * slots + 6]
+    rest = refs[2 * slots + 6 :]
+    nexts, clips = rest[:slots], rest[slots : 2 * slots]
+    row_stats, column_stats = rest[2 * slots : 2 * slots + 2]
+    held, clipped = rest[2 * slots + 2 : 3 * slots + 2], rest[3 * slots + 2 : 4 * slots + 2]
+    sems = rest[4 * slots + 2]
+    low = [grads[slot].dtype == jnp.bfloat16 for slot in range(slots)]
+    order = sorted(range(slots), key=lambda slot: -weights[slot].size)
+
+    def weight_in(slot):
+        return pltpu.make_async_copy(weights[slot], held[slot], sems.at[0, slot])
+
+    def grad_in(slot):
+        return pltpu.make_async_copy(grads[slot], clipped[slot], sems.at[1, slot])
+
+    def weight_out(slot):
+        return pltpu.make_async_copy(held[slot], nexts[slot], sems.at[2, slot])
+
+    def grad_out(slot):
+        return pltpu.make_async_copy(clipped[slot], clips[slot], sems.at[3, slot])
+
+    for slot in order:
+        weight_in(slot).start()
+        if not low[slot]:
+            grad_in(slot).start()
+
+    split = [slot for slot in range(slots) if layouts[slot] != "whole"]
+    ends = [0, 0]
+    for slot, layout in enumerate(layouts):
+        count, across_ = weights[slot].shape
+        own, other = (column_stats, row_stats) if flipped[slot] else (row_stats, column_stats)
+        own_end, other_end = (1, 0) if flipped[slot] else (0, 1)
+        at = ends[own_end]
+        if layout == "rows":
+            spot = split.index(slot)
+            for member in range(groups):
+                own[:, at : at + count] = shown[member, spot : spot + 1, :count]
+                at += count
+        else:
+            own[:, at : at + count] = row_new[slot : slot + 1, :count]
+            at += count
+        ends[own_end] = at
+        other[:, ends[other_end] : ends[other_end] + across_] = column_new[slot : slot + 1, :]
+        ends[other_end] += across_
+
+    factor = norms[1:2, :1]
+    for slot in order:
+        count, across_ = weights[slot].shape
+        block = row_block(count)
+        weight_in(slot).wait()
+        if not low[slot]:
+            grad_in(slot).wait()
+        source = grads[slot] if low[slot] else clipped[slot]
+        by_column = column_coef[slot : slot + 1, :across_]
+
+        @pl.loop(0, count // block)
+        def _(index, slot=slot, block=block, source=source, by_column=by_column):
+            at = pl.ds(pl.multiple_of(index * block, block), block)
+            gradient = source[at, :].astype(jnp.float32)
+            step_size = row_coef[at, slot : slot + 1] * by_column
+            held[slot][at, :] = held[slot][at, :] - gradient * step_size
+            clipped[slot][at, :] = gradient * factor
+
+        weight_out(slot).start()
+        grad_out(slot).start()
+    for slot in order:
+        weight_out(slot).wait()
+        grad_out(slot).wait()
+
+
+def apply_scales(gradients, weights, found, layouts, flipped):
+    groups = lax.axis_size("mp")
+    vmem = pl.BlockSpec(memory_space=pltpu.VMEM)
+    stay = pl.BlockSpec(memory_space=pl.ANY)
+    many_rows = 0
+    many_columns = 0
+    for weight, layout, flip in zip(weights, layouts, flipped):
+        extents = (weight.shape[0] * (groups if layout == "rows" else 1), weight.shape[1])
+        many_rows += extents[1 if flip else 0]
+        many_columns += extents[0 if flip else 1]
+    shapes = [jax.ShapeDtypeStruct(weight.shape, jnp.float32) for weight in weights]
+    buffers = [pltpu.VMEM(weight.shape, jnp.float32) for weight in weights]
+    size = sum(weight.size for weight in weights)
+    results = pl.pallas_call(
+        functools.partial(apply_kernel, layouts, flipped, groups),
+        out_shape=shapes
+        + shapes
+        + [
+            jax.ShapeDtypeStruct((1, many_rows), jnp.float32),
+            jax.ShapeDtypeStruct((1, many_columns), jnp.float32),
+        ],
+        in_specs=[vmem if part.dtype == jnp.bfloat16 else stay for part in gradients]
+        + [stay] * len(weights)
+        + [vmem] * 6,
+        out_specs=[stay] * (2 * len(weights)) + [vmem] * 2,
+        scratch_shapes=buffers + buffers + [pltpu.SemaphoreType.DMA((4, len(weights)))],
+        compiler_params=pltpu.CompilerParams(vmem_limit_bytes=58 * 1024 * 1024),
+        cost_estimate=pl.CostEstimate(flops=4 * size, bytes_accessed=16 * size, transcendentals=0),
+    )(*gradients, *weights, *found)
+    count = len(weights)
+    return (
+        results[:count],
+        results[count : 2 * count],
+        results[2 * count].reshape(-1),
+        results[2 * count + 1].reshape(-1),
+    )
 
 
 def weights_of(keys, queries, live):
@@ -587,7 +1012,7 @@
     live = lax.broadcasted_iota(jnp.int32, (patches, patches), 0) < length_ref[pl.program_id(0)]
     upper = lax.broadcasted_iota(jnp.int32, (pair, patches), 0) < HD
 
-    @pl.loop(0, q_ref.shape[0] // pair)
+    @pl.loop(0, q_ref.shape[0] // pair, unroll=4)
     def _(index):
         rows = pl.ds(pl.multiple_of(index * pair, 16), pair)
         queries, keys, values = q_ref[rows, :], k_ref[rows, :], v_ref[rows, :]
@@ -606,7 +1031,7 @@
     live = lax.broadcasted_iota(jnp.int32, (patches, patches), 0) < length_ref[pl.program_id(0)]
     upper = lax.broadcasted_iota(jnp.int32, (pair, patches), 0) < HD
 
-    @pl.loop(0, q_ref.shape[0] // pair)
+    @pl.loop(0, q_ref.shape[0] // pair, unroll=4)
     def _(index):
         rows = pl.ds(pl.multiple_of(index * pair, 16), pair)
         queries, keys, values, upstream = (
@@ -742,10 +1167,10 @@
         contractor.astype(jnp.bfloat16),
     )
     gathered = []
-    for shard in shards:
+    for slot, shard in enumerate(shards):
         piece_rows = shard.shape[0] // copies
         piece = lax.dynamic_slice_in_dim(shard, copy * piece_rows, piece_rows)
-        gathered.append(gather_weight(piece))
+        gathered.append(gather_pieces(piece, 8) if slot == 0 else gather_weight(piece))
     parts = copies // 4
     piece_rows = shards[0].shape[0] // copies
     mixer_all = (
@@ -770,13 +1195,12 @@
     condition = jnp.dot(jax.nn.silu(hidden_pre), time_second, precision=highest) + class_rows
     signal_all = jax.nn.silu(condition).astype(jnp.bfloat16)
     signal = lax.dynamic_slice_in_dim(signal_all, copy * group_images, group_images)
-    modulator_low = modulator.astype(jnp.bfloat16)
-    finisher_low = finisher.astype(jnp.bfloat16)
+    mods_low = jnp.concatenate(
+        [modulator.astype(jnp.bfloat16), finisher.astype(jnp.bfloat16)], axis=1
+    )
     steer_here, final_here = modulator.shape[1], finisher.shape[1]
-    mods_part = jnp.concatenate(
-        [product(signal, modulator_low), product(signal, finisher_low)], axis=1
-    )
-    mods_part = mods_part.astype(jnp.bfloat16).astype(jnp.float32)
+    mods_part = product(signal, mods_low)
+    mods_part = lax.reduce_precision(mods_part, 8, 7)
     mods_own = swap(mods_part.reshape(groups, -1, 128), "mp", 2)
     mods_own = mods_own.reshape(groups, images, steer_here + final_here).transpose(1, 0, 2)
     steering = mods_own[:, :, :steer_here].reshape(images, 6, 1, width)
@@ -825,7 +1249,7 @@
     loss_part = jnp.sum(jnp.where(live_rows, misfit * misfit, 0.0))
 
     output_grad = jnp.where(live_rows, 2.0 * misfit / valid_total, 0.0).astype(jnp.bfloat16)
-    readout_part = product_left(input_final, output_grad)
+    readout_part = product_left(output_grad, input_final)
     final_grad = product_right(output_grad, readout_low).reshape(images, patches, width)
     final_shift_grad = jnp.sum(final_grad, axis=1)
     final_scale_grad = jnp.sum(final_grad * normed_final, axis=1)
@@ -863,20 +1287,6 @@
         .transpose(0, 2, 1, 3, 4)
         .reshape(4 * width, width)
     )
-    contract_sum = reduce_weight(contract_part).astype(jnp.float32)
-    expand_sum, mixer_sum = reduce_weights([expand_part, mixer_part], 3)
-    expand_sum = expand_sum.astype(jnp.float32).T
-    mixer_sum = mixer_sum.astype(jnp.float32)
-    held = heads_here * HD
-    inputs_sum = (
-        mixer_sum[: 3 * held]
-        .reshape(3, heads_here, HD, width)
-        .transpose(1, 0, 2, 3)
-        .reshape(3 * held, width)
-        .T
-    )
-    outputs_sum = mixer_sum[3 * held :]
-
     steer_back = jnp.stack(
         [
             shift_one_grad,
@@ -888,9 +1298,9 @@
         ],
         axis=1,
     )
-    steer_back = steer_back.reshape(images, 6 * width).astype(jnp.bfloat16)
+    steer_back = lax.reduce_precision(steer_back.reshape(images, 6 * width), 8, 7)
     final_back = jnp.stack([final_shift_grad, final_scale_grad], axis=1)
-    final_back = final_back.reshape(images, 2 * width).astype(jnp.bfloat16)
+    final_back = lax.reduce_precision(final_back.reshape(images, 2 * width), 8, 7)
     back = jnp.concatenate(
         [
             steer_back.reshape(images, groups, steer_here),
@@ -898,25 +1308,35 @@
         ],
         axis=2,
     )
-    back = back.transpose(1, 0, 2).astype(jnp.float32).reshape(groups, -1, 128)
-    cols_all = swap(back, "all", 4).astype(jnp.bfloat16)
-    cols_all = cols_all.reshape(copies * group_images, steer_here + final_here)
-    cols = lax.dynamic_slice_in_dim(cols_all, copy * group_images, group_images)
-    signal_grad = product_right(cols[:, :steer_here], modulator_low) + product_right(
-        cols[:, steer_here:], finisher_low
-    )
+    back = back.transpose(1, 0, 2)
     shared = slabs(
         jnp.concatenate([embed_part.reshape(-1), readout_part.reshape(-1), loss_part[None]]),
         copies * groups,
     )
-    shared, signal_grad = both_totals(shared, signal_grad.reshape(groups, -1, 128), 5)
+    contract_sum = reduce_weight(contract_part)
+    expand_piece = lax.psum_scatter(
+        expand_part, ("dp", "mp"), scatter_dimension=0, tiled=True
+    )
+    (mixer_sum,), cols_all, shared, signal_grad = reduce_weights(
+        [mixer_part], back, mods_low, shared, 3
+    )
+    held = heads_here * HD
+    inputs_sum = (
+        mixer_sum[: 3 * held]
+        .reshape(3, heads_here, HD, width)
+        .transpose(1, 0, 2, 3)
+        .reshape(3 * held, width)
+    )
+    outputs_sum = mixer_sum[3 * held :]
+    cols_all = cols_all.astype(jnp.bfloat16).reshape(copies * group_images, -1)
     shared = shared.reshape(-1)
     embed_sum = shared[: embedder.size].reshape(embedder.shape)
-    readout_sum = shared[embedder.size : embedder.size + readout.size].reshape(readout.shape)
+    readout_sum = shared[embedder.size : embedder.size + readout.size].reshape(-1, width)
     loss_sum = shared[embedder.size + readout.size]
     signal_grad = signal_grad.reshape(copies * group_images, width)
-    modulator_sum = product_left(signal_all, cols_all[:, :steer_here])
-    finisher_sum = product_left(signal_all, cols_all[:, steer_here:])
+    expand_sum = across(jnp.where(loss_sum >= 0.0, expand_piece, 0.0), "dp")
+    modulator_sum = product_left(cols_all[:, :steer_here], signal_all)
+    finisher_sum = product_left(cols_all[:, steer_here:], signal_all)
     hidden, hidden_pull = jax.vjp(jax.nn.silu, hidden_pre)
     condition_grad = jax.vjp(jax.nn.silu, condition)[1](signal_grad)[0]
     time_second_sum = lax.dot_general(
@@ -945,112 +1365,49 @@
         embedder,
         time_first,
         time_second,
-        modulator,
-        mixer_input,
+        modulator.T,
+        mixer_input.T,
         mixer_output,
-        expander,
+        expander.T,
         contractor,
-        finisher,
-        readout,
-    )
-    layouts = (
-        "whole",
-        "whole",
-        "whole",
-        "columns",
-        "columns",
-        "rows",
-        "columns",
-        "rows",
-        "columns",
-        "whole",
-    )
-    row_squares = [jnp.sum(gradient * gradient, axis=1) for gradient in gradients]
-    column_squares = [jnp.sum(gradient * gradient, axis=0) for gradient in gradients]
-    split_slots = [slot for slot in range(10) if layouts[slot] != "whole"]
-    local_square = sum(jnp.sum(row_squares[slot]) for slot in range(10) if slot not in split_slots)
-    split_square = sum(jnp.sum(row_squares[slot]) for slot in split_slots)
-    crossing = [
-        row_squares[slot] if layouts[slot] == "columns" else column_squares[slot]
-        for slot in split_slots
-    ]
-    lengths_out = [part.shape[0] for part in crossing]
-    crossing = jnp.concatenate(crossing + [split_square[None]])
-    crossed = total(slabs(crossing, 1)[0], "mp", 6).reshape(-1)
-    grad_norm = jnp.sqrt(crossed[crossing.shape[0] - 1] + local_square)
-    factor = clip_limit / jnp.maximum(grad_norm, clip_limit)
-    factor_square = factor * factor
-    start = 0
-    for slot, length in zip(split_slots, lengths_out):
-        part = crossed[start : start + length]
-        start += length
-        if layouts[slot] == "columns":
-            row_squares[slot] = part
-        else:
-            column_squares[slot] = part
-
-    row_at = 0
-    column_at = 0
-    records = []
-    for slot in range(10):
-        layout = layouts[slot]
-        local_rows, local_cols = weights[slot].shape
-        many_rows = local_rows * (groups if layout == "rows" else 1)
-        many_cols = local_cols * (groups if layout == "columns" else 1)
-        row_mean = row_squares[slot] * factor_square / many_cols + eps_factor
-        column_mean = column_squares[slot] * factor_square / many_rows + eps_factor
-        row_start = row_at + (member * local_rows if layout == "rows" else 0)
-        column_start = column_at + (member * local_cols if layout == "columns" else 0)
-        row_old = lax.dynamic_slice_in_dim(row_states, row_start, local_rows)
-        column_old = lax.dynamic_slice_in_dim(column_states, column_start, local_cols)
-        row_next = state_decay * row_old + (1.0 - state_decay) * row_mean
-        column_next = state_decay * column_old + (1.0 - state_decay) * column_mean
-        if layout == "rows":
-            row_average = state_decay * jnp.mean(row_states[row_at : row_at + many_rows]) + (
-                1.0 - state_decay
-            ) * jnp.mean(column_mean)
-        else:
-            row_average = jnp.mean(row_next)
-        clipped = gradients[slot] * factor
-        update = clipped * lax.rsqrt(row_next[:, None] * column_next[None, :] / row_average)
-        records.append(
-            (clipped, update, jnp.sum(update * update), row_next, column_next, many_rows, many_cols)
-        )
-        row_at += many_rows
-        column_at += many_cols
-    shares = [jnp.stack([records[slot][2] for slot in split_slots])]
-    for slot in split_slots:
-        shares.append(records[slot][4] if layouts[slot] == "columns" else records[slot][3])
-    spread = swap(slabs(jnp.concatenate(shares), 1)[0], "mp", 7, per_target=False)
-    spread = spread.reshape(groups, -1)
-    energies = jnp.sum(spread[:, : len(split_slots)], axis=0)
-    start = len(split_slots)
-    next_list = []
-    row_list = []
-    column_list = []
-    for slot in range(10):
-        clipped, update, energy, row_next, column_next, many_rows, many_cols = records[slot]
-        if layouts[slot] != "whole":
-            energy = energies[split_slots.index(slot)]
-            length = column_next.shape[0] if layouts[slot] == "columns" else row_next.shape[0]
-            joined = spread[:, start : start + length].reshape(-1)
-            start += length
-            if layouts[slot] == "columns":
-                column_next = joined
-            else:
-                row_next = joined
-        scale_down = jnp.maximum(1.0, jnp.sqrt(energy / (many_rows * many_cols)))
-        next_list.append(weights[slot] - step_rate / math.sqrt(many_rows) * (update / scale_down))
-        row_list.append(row_next)
-        column_list.append(column_next)
+        finisher.T,
+        readout.T,
+    )
+    layouts = ("whole",) * 3 + ("rows",) * 6 + ("whole",)
+    flipped = (False, False, False, True, True, False, True, False, True, True)
+    ends = {"row": 0, "column": 0}
+    row_parts = []
+    column_parts = []
+    whole_rows = []
+    for weight, layout, flip in zip(weights, layouts, flipped):
+        count = weight.shape[0]
+        many = count * (groups if layout == "rows" else 1)
+        own, other = ("column", "row") if flip else ("row", "column")
+        states = {"row": row_states, "column": column_states}
+        start = ends[own] + (member * count if layout == "rows" else 0)
+        part = lax.dynamic_slice_in_dim(states[own], start, count)
+        row_parts.append(jnp.pad(part, (0, width - count), constant_values=1.0))
+        column_parts.append(states[other][ends[other] : ends[other] + width])
+        if layout == "rows" and not flip:
+            whole_rows.append(states[own][ends[own] : ends[own] + many].reshape(-1, width))
+        ends[own] += many
+        ends[other] += width
+    row_old = jnp.concatenate([jnp.stack(row_parts)] + whole_rows)
+    column_old = jnp.stack(column_parts)
+    found = scales(gradients, row_old, column_old, layouts, flipped, 6)
+    next_list, clipped_list, row_stats, column_stats = apply_scales(
+        gradients, weights, found, layouts, flipped
+    )
+    next_list = [part.T if flip else part for part, flip in zip(next_list, flipped)]
+    clipped_list = [part.T if flip else part for part, flip in zip(clipped_list, flipped)]
     return (
         loss_sum,
         valid_total,
-        grad_norm,
+        found[5][0, 0],
         *next_list,
-        *[record[0] for record in records],
-        jnp.concatenate(row_list),
-        jnp.concatenate(column_list),
+        *clipped_list,
+        row_stats,
+        column_stats,
     )
 
 

time: 905 us -> 750 us (0.83)
  waiting for transfers between devices: 150 us -> 4.45 us
  Pallas kernels: 286 us -> 362 us
  other arithmetic: 130 us -> 68.9 us
  between operations: 41.6 us -> 18.2 us
    all_gather x4, waiting for transfers between devices: 150 us -> 4.32 us  [across(): return lax.all_gather(values, axes, axis=0, tiled=True)]
    pallas_call x0 -> x3, Pallas kernels: none -> 144 us  [the longest x1 82.6 us: gather_pieces(): pl.pallas_call(functools.partial(gather_kernel, (copies, groups)), out_sh...]
    pallas_call x6 -> x2, Pallas kernels: 86.4 us -> 15 us  [call(): pl.pallas_call(kernel, out_shape=[jax.ShapeDtypeStruct(shape, jnp.float32...]
    reduce_sum x23 -> x0, other arithmetic: 40.4 us -> none  [the longest x9 26.6 us: body(): jnp.sum(update * update)]
    sub x10 -> x0, other arithmetic: 26.2 us -> none  [body(): weights[slot] - step_rate / math.sqrt(many_rows) * (update / scale_down)]
    pallas_call x1, Pallas kernels: 131 us -> 145 us  [reduce_weights(): pl.pallas_call(functools.partial(reduce_kernel, (copies, groups)), out_sh...]
    dot_general x7 -> x5, matrix products: 68.8 us -> 72.2 us  [product_right(): lax.dot_general(operand, other_operand, (((1,), (1,)), ((), ())), preferr...]
    unnamed x267 -> x134, local copies, waits for them, and re-layouts: 18.9 us -> 16.8 us
  transfers between devices with their start and end apart: 5 -> 6, of which waited for: 3 -> 1; matrix products, arithmetic and copies ran while one was open for 21% -> 36% of each run, Pallas kernels for 26% -> 41%
where the time goes in v3:
time: 750 us; the launch traced here: 740 us
  Pallas kernels  362 us (48%)
  matrix products  234 us (31%)
  other arithmetic  68.9 us (9%)
  local copies, waits for them, and re-layouts  52 us (7%)
  between operations  18.2 us (2%)
    pallas_call x1, Pallas kernels, reduce_weights(): pl.pallas_call(functools.partial(reduce_kernel, (copies, groups)), out_sh...  145 us
    pallas_call x1, Pallas kernels, gather_pieces(): pl.pallas_call(functools.partial(gather_kernel, (copies, groups)), out_sh...  82.6 us
    dot_general x5, matrix products, product_right(): lax.dot_general(operand, other_operand, (((1,), (1,)), ((), ())), preferr...  72.2 us
    dot_general x8, matrix products, product_left(): lax.dot_general(operand, other_operand, (((0,), (0,)), ((), ())), preferr...  71.7 us
    dot_general x7, matrix products, product(): return jnp.dot(operand, other_operand, preferred_element_type=jnp.float32)  65.4 us
    pallas_call x1, Pallas kernels, scales(): pl.pallas_call(functools.partial(scale_kernel, layouts, flipped), out_sha...  35.9 us
    pallas_call x1, Pallas kernels, attend_back(): pl.pallas_call(attend_back_kernel, grid_spec=pltpu.PrefetchScalarGridSpec...  32.7 us
    pallas_call x1, Pallas kernels, attend(): pl.pallas_call(attend_kernel, grid_spec=pltpu.PrefetchScalarGridSpec(num_...  25.8 us
  transfers between devices with their start and end apart: 6, of which 1 were waited for; matrix products, arithmetic and copies ran while one was open for 36% of the time, Pallas kernels for 41%

profile of v3, /device:TPU:0, one launch (start us, length us, event | category | flops | bytes accessed | tf_op | source)
XLA Modules:
  0.0 739.7 jit_solution(11327742113895906428)
XLA Ops:
  7.3 2.0 fusion.29
  9.4 1.9 dynamic-slice_convert_fusion
  12.0 4.7 shard_map.379
  17.0 1.4 convert_element_type.144
  19.7 3.6 convert_element_type.143
  23.3 4.2 copy.61
  27.5 1.6 gather_fusion
  31.7 6.7 multiply_convert_fusion.3
  39.1 1.4 copy-done.12
  41.2 10.3 %shard_map.380 = f32[8,36,128]{2,1,0:T(8,128)S(1)} custom-call(f32[8,36,128]{2,1,0:T(8,128)S(1)} %reshape.379.x_ref), custom_call_target="tpu_custom_call" | custom-call | tf_op jit(solution)/shard_map/pallas_call | solution.py:151
  55.9 82.6 %shard_map.378 = bf16[2,2,4,2,3,48,1152]{6,5,4,3,2,1,0:T(8,128)(2,1)} custom-call(bf16[3,48,1152]{2,1,0:T(8,128)(2,1)} %bitcast.175), custom_call_target="tpu_custom_call" | custom-call | tf_op jit(solution)/shard_map/pallas_call | solution.py:686
  138.5 2.8 multiply_cosine_fusion
  143.9 2.0 add_convert_fusion.3
  145.9 15.5 %convolution_convert_fusion.4.q_ref.k_ref.v_ref = bf16[3456,1024]{1,0:T(8,128)(2,1)} fusion(bf16[1024,1152]{1,0:T(8,128)(2,1)S(1)} %bitcast.167, bf16[4608,1152]{1,0:T(8,128)(2,1)} %bitcast.154), kind=kOutput, calls=%fused_computation.18 | convolution fusion | flops 8157265920 | bytes 17399808 | tf_op jit(solution)/shard_map/dot_general | solution.py:32
  161.5 25.8 %shard_map.381 = bf16[1152,1024]{1,0:T(8,128)(2,1)S(1)} custom-call(s32[4]{0:T(128)S(1)} %dynamic_slice.46.length_ref, bf16[3456,1024]{1,0:T(8,128)(2,1)} %convolution_convert_fusion.4.q_ref.k_ref.v_ref, bf16[3456,1024]{1,0:T(8,128)(2,1)} %convolution_convert_fusion.4.q_ref.k_ref.v_ref, bf16[3456,1024]{1,0:T(8,128)(2,1)} %convolution_convert_fusion.4.q_ref.k_ref.v_ref), custom_call_target="tpu_custom_call" | custom-call | flops 1207959552 | bytes 9437184 | tf_op jit(solution)/shard_map/pallas_call | solution.py:1077
  187.3 6.2 fusion.17
  194.4 1.4 copy-done.13
  196.4 1.5 copy-done.4
  197.8 2.0 add_convert_fusion.2
  199.9 19.7 %fusion.69 = f32[1024,4608]{1,0:T(8,128)} fusion(bf16[1024,1152]{1,0:T(8,128)(2,1)S(1)} %bitcast.169, bf16[4608,1152]{1,0:T(8,128)(2,1)} %all-gather.5.cloned.1.call-done), kind=kOutput, calls=%fused_computation.177 | convolution fusion | flops 10871635968 | bytes 31850496 | tf_op jit(solution)/shard_map/dot_general | solution.py:32
  219.7 22.6 %fusion.61 = f32[1024,1152]{1,0:T(8,128)S(1)} fusion(bf16[4608,1152]{1,0:T(8,128)(2,1)} %all-gather.7.cloned.1.call-done, f32[1024,4608]{1,0:T(8,128)} %fusion.69), kind=kOutput, calls=%fused_computation.169 | convolution fusion | flops 10914103296 | bytes 34209792 | tf_op jit(solution)/shard_map/dot_general | solution.py:28
  242.9 1.5 copy-done.14
  245.1 1.5 copy-done.7
  246.6 2.0 add_convert_fusion.1
  248.7 1.3 select_reduce_fusion
  250.0 2.9 fusion.12
  252.9 6.5 fusion.14
  259.4 4.7 multiply_reduce_fusion.1
  264.1 2.2 copy-done.10
  266.8 1.4 copy-done.31
  268.2 21.4 %convolution_convert_fusion = bf16[4608,1152]{1,0:T(8,128)(2,1)} fusion(bf16[1024,1152]{1,0:T(8,128)(2,1)S(1)} %bitcast.173, f32[1024,4608]{1,0:T(8,128)} %fusion.69), kind=kOutput, calls=%fused_computation.3 | convolution fusion | flops 10919411712 | bytes 31850496 | tf_op jit(solution)/shard_map/dot_general | solution.py:38
  289.6 28.6 %fusion.6 = bf16[1024,4608]{1,0:T(8,128)(2,1)} fusion(f32[1024,4608]{1,0:T(8,128)} %fusion.69, bf16[1024,1152]{1,0:T(8,128)(2,1)} %bitcast.174, bf16[4608,1152]{1,0:T(8,128)(2,1)} %all-gather.7.cloned.1.call-done), kind=kOutput, calls=%fused_computation.11 | convolution fusion | flops 10966007808 | bytes 41287680 | tf_op jit(solution)/shard_map/dot_general | solution.py:32
  318.2 18.7 %convolution_convert_fusion.1 = bf16[4608,1152]{1,0:T(8,128)(2,1)} fusion(bf16[1024,4608]{1,0:T(8,128)(2,1)} %fusion.6, bf16[1024,1152]{1,0:T(8,128)(2,1)S(1)} %bitcast.170), kind=kOutput, calls=%fused_computation.4 | convolution fusion | flops 10876944384 | bytes 22413312 | tf_op jit(solution)/shard_map/dot_general | solution.py:38
  338.5 19.6 %fusion.11 = (f32[1024]{0:T(1024)S(1)}, f32[1024,1152]{1,0:T(8,128)}) fusion(f32[4,1152]{1,0:T(4,128)S(1)} %bitcast.187, bf16[1024,4608]{1,0:T(8,128)(2,1)} %fusion.6, bf16[4608,1152]{1,0:T(8,128)(2,1)} %all-gather.5.cloned.1.call-done), kind=kOutput, calls=%fused_computation.23 | convolution fusion | flops 10873994240 | bytes 24795136 | tf_op jit(solution)/shard_map/dot_general | solution.py:28
  358.2 6.6 fusion.13
  364.8 6.3 multiply_reduce_fusion.2
  371.7 1.7 copy-done.9
  373.4 1.4 copy-done.30
  374.8 5.4 convolution_convert_fusion.5.up_ref
  380.2 32.7 %shard_map.382 = bf16[3,1152,1024]{2,1,0:T(8,128)(2,1)} custom-call(s32[4]{0:T(128)S(1)} %dynamic_slice.46.length_ref, bf16[3456,1024]{1,0:T(8,128)(2,1)} %convolution_convert_fusion.4.q_ref.k_ref.v_ref, bf16[3456,1024]{1,0:T(8,128)(2,1)} %convolution_convert_fusion.4.q_ref.k_ref.v_ref, bf16[3456,1024]{1,0:T(8,128)(2,1)} %convolution_convert_fusion.4.q_ref.k_ref.v_ref, ...), custom_call_target="tpu_custom_call" | custom-call | flops 3019898880 | bytes 16515072 | tf_op jit(solution)/shard_map/pallas_call | solution.py:1095
  412.9 9.8 %copy.66 = bf16[1024,3456]{1,0:T(8,128)(2,1)} copy(bf16[1024,3456]{0,1:T(8,128)(2,1)} %bitcast.147) | data formatting | bytes 14155776 | tf_op jit(solution)/shard_map/dot_general | solution.py:38
  422.7 16.0 %multiply_reduce_fusion = (f32[4,256]{1,0:T(4,128)S(1)}, f32[4,1152]{1,0:T(4,128)S(1)}, f32[4,256]{1,0:T(4,128)S(1)}, f32[4,1152]{1,0:T(4,128)S(1)}, f32[4,256,1152]{2,1,0:T(8,128)S(1)}) fusion(f32[4,256,1152]{2,1,0:T(8,128)} %copy-done.6, f32[4,1152]{1,0:T(4,128)S(1)} %copy-done.45, f32[4,256]{1,0:T(4,128)S(1)} %copy-done.59, f32[4,256]{1,0:T(4,128)S(1)} %copy-done.53, ...), kind=kOutput, calls=%fused_computation.33 | convolution fusion | flops 8164332544 | bytes 24549376 | tf_op jit(solution)/shard_map/dot_general | solution.py:38
  438.7 4.9 fusion.19
  444.8 6.4 convolution_convert_fusion.3
  451.2 1.4 select_maximum_fusion
  452.6 13.8 %convolution_convert_fusion.2 = bf16[3456,1152]{1,0:T(8,128)(2,1)} fusion(bf16[3456,1024]{1,0:T(8,128)(2,1)} %bitcast.148, bf16[1024,1152]{1,0:T(8,128)(2,1)S(1)} %bitcast.168), kind=kOutput, calls=%fused_computation.13 | convolution fusion | flops 8157708288 | bytes 17399808 | tf_op jit(solution)/shard_map/dot_general | solution.py:28
  466.5 14.6 %pad_maximum_fusion = bf16[4608,1152]{1,0:T(8,128)(2,1)} fusion(bf16[1152,1152]{1,0:T(8,128)(2,1)S(1)} %copy-done.25, bf16[3456,1152]{1,0:T(8,128)(2,1)} %convolution_convert_fusion.2), kind=kLoop, calls=%fused_computation.14 | loop fusion | flops 21233664 | bytes 21233664 | tf_op jit(solution)/shard_map/concatenate | solution.py:1284
  481.1 144.5 %shard_map.383 = (bf16[2,2,3,48,1152]{4,3,2,1,0:T(8,128)(2,1)}, f32[32,4,1152]{2,1,0:T(4,128)}, f32[32,16,128]{2,1,0:T(8,128)}, f32[32,4,1152]{2,1,0:T(4,128)}) custom-call(bf16[2,2,4,2,3,48,1152]{6,5,4,3,2,1,0:T(8,128)(2,1)} %bitcast.145, f32[8,4,1152]{2,1,0:T(4,128)} %maximum_bitcast_fusion.refs_1_, bf16[1152,1152]{1,0:T(8,128)(2,1)} %copy-done.12, ...), custom_call_target="tpu_custom_call" | custom-call | tf_op jit(solution)/shard_map/pallas_call | solution.py:524
  625.6 1.3 slice.159
  627.6 1.7 broadcast_select_fusion
  630.4 1.3 stack.135.refs_11_
  631.7 1.3 concatenate.31.refs_10_
  633.0 1.8 slice.162.refs_5_
  634.8 1.3 slice.161
  639.9 1.5 fusion.38.refs_8_
  641.4 7.6 %fusion.59 = f32[128,1152]{1,0:T(8,128)S(1)} fusion(f32[1152,1152]{1,0:T(8,128)} %refs_12_.1, f32[128,1152]{1,0:T(8,128)S(1)} %copy-done.17, f32[128,1152]{1,0:T(8,128)S(1)} %reshape.399), kind=kOutput, calls=%fused_computation.168 | convolution fusion | flops 2039758848 | bytes 7077888 | tf_op jit(solution)/shard_map/dot_general | solution.py:1346
  649.1 2.4 fusion.24.refs_1_
  651.4 2.7 fusion.32.refs_3_
  654.1 7.0 fusion.35.refs_2_
  661.1 4.3 all-gather.9.cloned.1.call-done.refs_6_
  665.4 35.9 %shard_map.384 = (f32[1152,128]{1,0:T(8,128)}, f32[16,1152]{1,0:T(8,128)}, f32[16,1152]{1,0:T(8,128)}, f32[16,1152]{1,0:T(8,128)}, f32[8,8,1152]{2,1,0:T(8,128)}, /*index=5*/f32[8,128]{1,0:T(8,128)}) custom-call(f32[16,1152]{1,0:T(8,128)} %reshape.398.refs_0_, f32[256,1152]{1,0:T(8,128)} %fusion.24.refs_1_, f32[1152,1152]{1,0:T(8,128)} %fusion.35.refs_2_, ...), custom_call_target="tpu_custom_call" | custom-call | tf_op jit(solution)/shard_map/pallas_call | solution.py:866
  702.5 25.6 %shard_map.385 = (f32[16,1152]{1,0:T(8,128)}, f32[256,1152]{1,0:T(8,128)}, f32[1152,1152]{1,0:T(8,128)}, f32[864,1152]{1,0:T(8,128)}, f32[432,1152]{1,0:T(8,128)...) custom-call(f32[16,1152]{1,0:T(8,128)} %reshape.398.refs_0_, ...), custom_call_target="tpu_custom_call" | custom-call | flops 19906560 | bytes 79626240 | tf_op jit(solution)/shard_map/pallas_call | solution.py:977
  728.2 1.6 reduce.5
  729.7 1.7 reduce.6
  (273 shorter events, 24.7 us)
Async XLA Ops:
  7.2 20.3 %copy-start = (bf16[1000,1152]{1,0:T(8,128)(2,1)S(1)}, bf16[1000,1152]{1,0:T(8,128)(2,1)}, u32[]{:S(2)}) copy-start(bf16[1000,1152]{1,0:T(8,128)(2,1)} %param.25) | copy-start | bytes 6912004
  7.2 192.7 %all-gather.5.cloned.1.call-start = ((), (), s32[]{:S(2)}) async-start(), calls=%async_computation.2 | async-start | bytes 10948608 | tf_op jit(solution)/shard_map/all_gather | solution.py:1110
  9.3 210.3 %all-gather.7.cloned.1.call-start = ((), (), s32[]{:S(2)}) async-start(), calls=%async_computation.3 | async-start | bytes 10948608 | tf_op jit(solution)/shard_map/all_gather | solution.py:1110
  11.2 455.2 %reduce-scatter.5.cloned.1.call-start = ((), (), s32[]{:S(2)}) async-start(), calls=%async_computation.6 | async-start | bytes 10948608 | tf_op jit(solution)/shard_map/reduce_scatter | solution.py:1118
  23.3 6.8 copy-start.20
  29.1 9.3 %copy-start.15 = (bf16[1152,864]{1,0:T(8,128)(2,1)S(1)}, bf16[1152,864]{1,0:T(8,128)(2,1)}, u32[]{:S(2)}) copy-start(bf16[1152,864]{1,0:T(8,128)(2,1)} %copy.61) | copy-start | bytes 5971972
  29.1 9.3 %copy-start.21 = (bf16[1152,288]{1,0:T(8,128)(2,1)S(1)}, bf16[1152,288]{1,0:T(8,128)(2,1)}, u32[]{:S(2)}) copy-start(bf16[1152,288]{1,0:T(8,128)(2,1)} %copy.62) | copy-start | bytes 1990660
  30.9 0.8 copy-start.18
  38.4 13.8 %copy-start.63 = (s32[128]{0:T(128)S(1)}, s32[128]{0:T(128)}, u32[]{:S(2)}) copy-start(s32[128]{0:T(128)} %param.24) | copy-start | bytes 1540
  38.4 15.3 %copy-start.62 = (f32[32]{0:T(128)S(1)}, f32[32]{0:T(128)}, u32[]{:S(2)}) copy-start(f32[32]{0:T(128)} %param.21) | copy-start | bytes 388
  38.4 15.4 %copy-start.54 = (f32[4,256,16]{1,2,0:T(8,128)S(1)}, f32[4,256,16]{1,2,0:T(8,128)}, u32[]{:S(2)}) copy-start(f32[4,256,16]{1,2,0:T(8,128)} %param.19) | copy-start | bytes 196612
  38.5 15.4 %copy-start.55 = (f32[4,256,16]{1,2,0:T(8,128)S(1)}, f32[4,256,16]{1,2,0:T(8,128)}, u32[]{:S(2)}) copy-start(f32[4,256,16]{1,2,0:T(8,128)} %param.20) | copy-start | bytes 196612
  38.5 15.5 %copy-start.24 = (f32[144,1152]{1,0:T(8,128)S(1)}, f32[144,1152]{1,0:T(8,128)}, u32[]{:S(2)}) copy-start(f32[144,1152]{1,0:T(8,128)} %refs_15_.1) | copy-start | bytes 1990660
  38.5 15.5 %copy-start.16 = (f32[1152,432]{0,1:T(8,128)S(1)}, f32[1152,432]{0,1:T(8,128)}, u32[]{:S(2)}) copy-start(f32[1152,432]{0,1:T(8,128)} %param.30) | copy-start | bytes 5971972
  39.1 1.5 copy-start.12
  53.9 88.3 %copy-start.34 = (bf16[4,256,16]{1,2,0:T(8,128)(2,1)}, bf16[4,256,16]{1,2,0:T(8,128)(2,1)S(1)}, u32[]{:S(2)}) copy-start(bf16[4,256,16]{1,2,0:T(8,128)(2,1)S(1)} %get-tuple-element.116) | copy-start | bytes 98308
  55.0 141.4 %copy-start.37 = (f32[4,1,1,1152]{3,0,1,2:T(4,128)}, f32[4,1,1,1152]{3,0,1,2:T(4,128)S(1)}, u32[]{:S(2)}) copy-start(f32[4,1,1,1152]{3,0,1,2:T(4,128)S(1)} %copy.89) | copy-start | bytes 55300
  55.9 86.3 %copy-start.36 = (f32[16,1152]{1,0:T(8,128)S(1)}, f32[16,1152]{1,0:T(8,128)}, u32[]{:S(2)}) copy-start(f32[16,1152]{1,0:T(8,128)} %refs_10_.1) | copy-start | bytes 221188
  143.2 50.4 %copy-start.6 = (f32[4,256,1152]{2,1,0:T(8,128)}, f32[4,256,1152]{2,1,0:T(8,128)S(1)}, u32[]{:S(2)}) copy-start(f32[4,256,1152]{2,1,0:T(8,128)S(1)} %get-tuple-element.147) | copy-start | bytes 14155780
  143.2 2.7 copy-start.52
  143.8 17.7 %copy-start.58 = (f32[4,256]{1,0:T(4,128)}, f32[4,256]{1,0:T(4,128)S(1)}, u32[]{:S(2)}) copy-start(f32[4,256]{1,0:T(4,128)S(1)} %add_rsqrt_fusion.2) | copy-start | bytes 12292
  143.9 17.6 %copy-start.44 = (f32[4,1152]{1,0:T(4,128)}, f32[4,1152]{1,0:T(4,128)S(1)}, u32[]{:S(2)}) copy-start(f32[4,1152]{1,0:T(4,128)S(1)} %get-tuple-element.160) | copy-start | bytes 55300
  145.9 15.6 %copy-start.26 = (bf16[4,256,1152]{2,1,0:T(8,128)(2,1)}, bf16[4,256,1152]{2,1,0:T(8,128)(2,1)S(1)}, u32[]{:S(2)}) copy-start(bf16[4,256,1152]{2,1,0:T(8,128)(2,1)S(1)} %add_convert_fusion.3) | copy-start | bytes 7077892
  187.3 6.3 copy-start.2
  187.3 6.3 copy-start.46
  193.5 2.2 copy-start.13
  195.7 2.1 copy-start.4
  195.7 4.1 copy-start.49
  196.4 23.3 %copy-start.56 = (f32[4,256]{1,0:T(4,128)}, f32[4,256]{1,0:T(4,128)S(1)}, u32[]{:S(2)}) copy-start(f32[4,256]{1,0:T(4,128)S(1)} %add_rsqrt_fusion.1) | copy-start | bytes 12292
  199.9 19.8 %copy-start.28 = (bf16[4,256,1152]{2,1,0:T(8,128)(2,1)}, bf16[4,256,1152]{2,1,0:T(8,128)(2,1)S(1)}, u32[]{:S(2)}) copy-start(bf16[4,256,1152]{2,1,0:T(8,128)(2,1)S(1)} %add_convert_fusion.2) | copy-start | bytes 7077892
  219.7 22.7 %copy-start.5 = (f32[4,256,1152]{2,1,0:T(8,128)S(1)}, f32[4,256,1152]{2,1,0:T(8,128)}, u32[]{:S(2)}) copy-start(f32[4,256,1152]{2,1,0:T(8,128)} %copy-done.4) | copy-start | bytes 14155780
  242.3 2.2 copy-start.14
  244.5 2.1 copy-start.7
  245.1 3.5 copy-start.32
  252.9 6.5 copy-start.8
  264.1 2.2 copy-start.10
  266.7 1.4 copy-start.31
  289.5 338.1 %reduce-scatter.3.cloned.1.call-start = ((), (), s32[]{:S(2)}) async-start(), calls=%async_computation.4 | async-start | bytes 10948608 | tf_op jit(solution)/shard_map/reduce_scatter | solution.py:1317
  289.6 28.6 %copy-start.29 = (bf16[4,256,1152]{2,1,0:T(8,128)(2,1)S(1)}, bf16[4,256,1152]{2,1,0:T(8,128)(2,1)}, u32[]{:S(2)}) copy-start(bf16[4,256,1152]{2,1,0:T(8,128)(2,1)} %copy-done.28) | copy-start | bytes 7077892
  336.9 1.6 copy-start.38
  336.9 324.2 %all-gather.11.cloned.1.call-start = ((), (), s32[]{:S(2)}) async-start(), calls=%async_computation.7 | async-start | bytes 1658880 | tf_op jit(solution)/shard_map/all_gather | solution.py:1110
  338.4 19.7 %copy-start.50 = (f32[4,256]{1,0:T(4,128)S(1)}, f32[4,256]{1,0:T(4,128)}, u32[]{:S(2)}) copy-start(f32[4,256]{1,0:T(4,128)} %copy-done.49) | copy-start | bytes 12292
  338.5 19.7 %copy-start.57 = (f32[4,256]{1,0:T(4,128)S(1)}, f32[4,256]{1,0:T(4,128)}, u32[]{:S(2)}) copy-start(f32[4,256]{1,0:T(4,128)} %copy-done.56) | copy-start | bytes 12292
  358.1 6.7 copy-start.11
  364.8 6.4 copy-start.47
  371.2 2.2 copy-start.9
  373.4 1.4 copy-start.30
  412.9 9.8 %copy-start.45 = (f32[4,1152]{1,0:T(4,128)S(1)}, f32[4,1152]{1,0:T(4,128)}, u32[]{:S(2)}) copy-start(f32[4,1152]{1,0:T(4,128)} %copy-done.44) | copy-start | bytes 55300
  412.9 9.8 %copy-start.53 = (f32[4,256]{1,0:T(4,128)S(1)}, f32[4,256]{1,0:T(4,128)}, u32[]{:S(2)}) copy-start(f32[4,256]{1,0:T(4,128)} %copy-done.52) | copy-start | bytes 12292
  412.9 9.8 %copy-start.59 = (f32[4,256]{1,0:T(4,128)S(1)}, f32[4,256]{1,0:T(4,128)}, u32[]{:S(2)}) copy-start(f32[4,256]{1,0:T(4,128)} %copy-done.58) | copy-start | bytes 12292
  422.7 16.0 %copy-start.35 = (bf16[4,256,16]{1,2,0:T(8,128)(2,1)S(1)}, bf16[4,256,16]{1,2,0:T(8,128)(2,1)}, u32[]{:S(2)}) copy-start(bf16[4,256,16]{1,2,0:T(8,128)(2,1)} %copy-done.34) | copy-start | bytes 98308
  438.7 6.1 copy-start.3
  444.8 7.8 %copy-start.27 = (bf16[4,256,1152]{2,1,0:T(8,128)(2,1)S(1)}, bf16[4,256,1152]{2,1,0:T(8,128)(2,1)}, u32[]{:S(2)}) copy-start(bf16[4,256,1152]{2,1,0:T(8,128)(2,1)} %copy-done.26) | copy-start | bytes 7077892
  452.6 13.9 %copy-start.25 = (bf16[1152,1152]{1,0:T(8,128)(2,1)S(1)}, bf16[1152,1152]{1,0:T(8,128)(2,1)}, u32[]{:S(2)}) copy-start(bf16[1152,1152]{1,0:T(8,128)(2,1)} %convolution_convert_fusion.3) | copy-start | bytes 7962628
  466.5 198.9 %all-gather.9.cloned.1.call-start = ((), (), s32[]{:S(2)}) async-start(), calls=%async_computation.5 | async-start | bytes 1658880 | tf_op jit(solution)/shard_map/all_gather | solution.py:1110
  481.1 148.3 %copy-start.60 = (f32[23056]{0:T(1024)S(1)}, f32[23056]{0:T(1024)}, u32[]{:S(2)}) copy-start(f32[23056]{0:T(1024)} %param.37) | copy-start | bytes 276676
  625.6 10.5 %copy-start.33 = (f32[32,4,1152]{2,1,0:T(4,128)S(1)}, f32[32,4,1152]{2,1,0:T(4,128)}, u32[]{:S(2)}) copy-start(f32[32,4,1152]{2,1,0:T(4,128)} %get-tuple-element.58) | copy-start | bytes 1769476
  625.6 10.7 %copy-start.51 = (f32[32,16,128]{2,1,0:T(8,128)S(1)}, f32[32,16,128]{2,1,0:T(8,128)}, u32[]{:S(2)}) copy-start(f32[32,16,128]{2,1,0:T(8,128)} %get-tuple-element.57) | copy-start | bytes 786436
  629.3 10.6 %copy-start.23 = (bf16[128,1152]{1,0:T(8,128)(2,1)S(1)}, bf16[128,1152]{1,0:T(8,128)(2,1)}, u32[]{:S(2)}) copy-start(bf16[128,1152]{1,0:T(8,128)(2,1)} %copy-done.22) | copy-start | bytes 884740
  633.0 8.4 %copy-start.17 = (f32[128,1152]{1,0:T(8,128)S(1)}, f32[128,1152]{1,0:T(8,128)}, u32[]{:S(2)}) copy-start(f32[128,1152]{1,0:T(8,128)} %get-tuple-element.145) | copy-start | bytes 1769476
  639.9 9.1 %copy-start.19 = (f32[128,1152]{1,0:T(8,128)S(1)}, f32[128,1152]{1,0:T(8,128)}, u32[]{:S(2)}) copy-start(f32[128,1152]{1,0:T(8,128)} %copy-done.18) | copy-start | bytes 1769476
  639.9 9.1 %copy-start.40 = (f32[128,128]{1,0:T(8,128)S(1)}, f32[128,128]{1,0:T(8,128)}, u32[]{:S(2)}) copy-start(f32[128,128]{1,0:T(8,128)} %copy-done.39) | copy-start | bytes 196612
  639.9 9.1 %copy-start.42 = (f32[128,128]{1,0:T(8,128)S(1)}, f32[128,128]{1,0:T(8,128)}, u32[]{:S(2)}) copy-start(f32[128,128]{1,0:T(8,128)} %copy-done.41) | copy-start | bytes 196612
  702.5 29.0 %copy-start.1 = (bf16[1000,1152]{1,0:T(8,128)(2,1)S(1)}, bf16[1000,1152]{1,0:T(8,128)(2,1)}, u32[]{:S(2)}) copy-start(bf16[1000,1152]{1,0:T(8,128)(2,1)} %param.25) | copy-start | bytes 6912004
  (6 other events, 4.4 us)
Sparse Core Ops, SparseCore 0:
  11.6 110.6 all-gather.4
  125.8 90.6 all-gather.6
  289.7 146.4 reduce-scatter.4
  442.1 184.3 reduce-scatter.2
  627.9 17.1 all-gather.10
  647.1 18.2 all-gather.8

commit v4 on v3

--- a/solution.py
+++ b/solution.py
@@ -182,15 +182,26 @@
 def reduce_kernel(counts, *refs):
     copies, groups = counts
     lines = {"a": 4, "b": groups // 4, "y": copies // 2}
-    chunks = (len(refs) - 20) // 2
+    chunks = (len(refs) - 27) // 2
     parts = refs[:chunks]
-    back_ref, low_ref, shared_ref = refs[chunks : chunks + 3]
-    outs = refs[chunks + 3 : 2 * chunks + 3]
-    cols_out, shared_out, signal_out = refs[2 * chunks + 3 : 2 * chunks + 6]
+    back_ref, low_ref, shared_ref, features_ref, hidden_ref, condition_ref, second_ref = refs[
+        chunks : chunks + 7
+    ]
+    outs = refs[chunks + 7 : 2 * chunks + 7]
+    cols_out, shared_out, first_out, second_out = refs[2 * chunks + 7 : 2 * chunks + 11]
     held, twin, first_b, first_y, second, third, send_sems, recv_sems = refs[
-        2 * chunks + 6 : 2 * chunks + 14
+        2 * chunks + 11 : 2 * chunks + 19
     ]
-    shared_land, signal_land, signal_part, stack, side_sends, side_recvs = refs[2 * chunks + 14 :]
+    (
+        shared_land,
+        signal_land,
+        signal_part,
+        stack,
+        side_sends,
+        side_recvs,
+        signal_out,
+        later_grad,
+    ) = refs[2 * chunks + 19 :]
     splits = parts[0].shape[4]
     dp, mp = lax.axis_index("dp"), lax.axis_index("mp")
     at = {"a": mp // lines["b"], "b": lax.rem(mp, lines["b"]), "y": dp // 2}
@@ -223,7 +234,7 @@
         stack[...] = jnp.zeros_like(stack)
         for member in range(groups):
             stack[8 * member : 8 * member + images] = cols_out[dp * groups + member]
-        found = product_right(stack[...].astype(jnp.bfloat16), low_ref[...])
+        found = product(stack[...].astype(jnp.bfloat16), low_ref[...])
         for member in range(groups):
             signal_part[member] = found[8 * member : 8 * member + images]
         signal_land[mp] = signal_part[mp]
@@ -237,9 +248,33 @@
         signal_out[here] = sum_over(signal_land)
         side(4, "all", lambda place: signal_out.at[here], lambda place: signal_out.at[place])
 
+    def silu_slope(values):
+        gate = lax.logistic(values)
+        return gate * (1.0 + values * (1.0 - gate))
+
+    def exact(left, right, dims):
+        return lax.dot_general(
+            left, right, (dims, ((), ())), precision=highest, preferred_element_type=jnp.float32
+        )
+
+    def side_second():
+        waits[4]()
+        images = signal_out.shape[1]
+        for device_ in range(copies * groups):
+            later_grad[device_ * images : (device_ + 1) * images] = signal_out[device_]
+        later_grad[...] = later_grad[...] * silu_slope(condition_ref[...])
+        hidden = hidden_ref[...]
+        second_out[...] = exact(hidden * lax.logistic(hidden), later_grad[...], ((0,), (0,)))
+
+    def side_hidden():
+        back = exact(later_grad[...], second_ref[...], ((1,), (1,)))
+        later_grad[...] = back * silu_slope(hidden_ref[...])
+
+    def side_first():
+        first_out[...] = exact(features_ref[...], later_grad[...], ((0,), (0,)))
+
     def side_end():
         waits[3]()
-        waits[4]()
 
     units = [(chunk, split) for chunk in range(chunks) for split in range(splits)]
     slots = {}
@@ -488,11 +523,18 @@
             side_signal()
         if tick == 3:
             side_show()
+        if tick == 6:
+            side_second()
+        if tick == 7:
+            side_hidden()
+        if tick == 8:
+            side_first()
     side_end()
 
 
-def reduce_weights(partials, back, low_weights, shared, collective_id):
+def reduce_weights(partials, sides, collective_id):
     copies, groups = lax.axis_size("dp"), lax.axis_size("mp")
+    back, _, shared, features, _, condition, _ = sides
     rows, width = partials[0].shape
     size_b, size_y = groups // 4, copies // 2
     piece = rows // (copies * groups)
@@ -520,6 +562,8 @@
         pltpu.VMEM((8 * groups, back.shape[2]), jnp.float32),
         pltpu.SemaphoreType.DMA((5, copies * groups)),
         pltpu.SemaphoreType.DMA((5, copies * groups)),
+        pltpu.VMEM((copies * groups, back.shape[1], width), jnp.float32),
+        pltpu.VMEM(condition.shape, jnp.float32),
     ]
     results = pl.pallas_call(
         functools.partial(reduce_kernel, (copies, groups)),
@@ -527,16 +571,17 @@
         + [
             jax.ShapeDtypeStruct((copies * groups,) + back.shape[1:], jnp.float32),
             jax.ShapeDtypeStruct(shared.shape, jnp.float32),
-            jax.ShapeDtypeStruct((copies * groups, back.shape[1], width), jnp.float32),
+            jax.ShapeDtypeStruct((features.shape[1], width), jnp.float32),
+            jax.ShapeDtypeStruct((width, width), jnp.float32),
         ],
         in_specs=[pl.BlockSpec(memory_space=pl.ANY)] * len(partials)
-        + [pl.BlockSpec(memory_space=pltpu.VMEM)] * 3,
-        out_specs=[pl.BlockSpec(memory_space=pltpu.VMEM)] * (len(partials) + 3),
+        + [pl.BlockSpec(memory_space=pltpu.VMEM)] * 7,
+        out_specs=[pl.BlockSpec(memory_space=pltpu.VMEM)] * (len(partials) + 4),
         scratch_shapes=scratch,
         compiler_params=pltpu.CompilerParams(
-            collective_id=collective_id, has_side_effects=True, vmem_limit_bytes=60 * 1024 * 1024
+            collective_id=collective_id, has_side_effects=True, vmem_limit_bytes=62 * 1024 * 1024
         ),
-    )(*shaped, back, low_weights, shared)
+    )(*shaped, *sides)
     sums = [result.reshape(copies * piece, width) for result in results[: len(partials)]]
     return sums, *results[len(partials) :]
 
@@ -1025,7 +1070,8 @@
         out_ref[rows, :] = jnp.where(upper, mixed[0], mixed[1]).astype(jnp.bfloat16)
 
 
-def attend_back_kernel(length_ref, q_ref, k_ref, v_ref, up_ref, down_ref):
+def attend_back_kernel(length_ref, q_ref, k_ref, v_ref, up_ref, mixed_ref, down_ref):
+    down_ref[3] = mixed_ref[...]
     patches = q_ref.shape[1]
     pair = 2 * HD
     live = lax.broadcasted_iota(jnp.int32, (patches, patches), 0) < length_ref[pl.program_id(0)]
@@ -1088,7 +1134,7 @@
     )(lengths, qkv, qkv, qkv)
 
 
-def attend_back(qkv, upstream, lengths, images):
+def attend_back(qkv, upstream, mixed, lengths, images):
     width, rows = upstream.shape
     patches = rows // images
     spec = _specs(width, patches)
@@ -1097,13 +1143,93 @@
         grid_spec=pltpu.PrefetchScalarGridSpec(
             num_scalar_prefetch=1,
             grid=(images,),
-            in_specs=[spec(0), spec(1), spec(2), spec(0)],
-            out_specs=pl.BlockSpec((3, width, patches), lambda image, lengths: (0, 0, image)),
+            in_specs=[spec(0), spec(1), spec(2), spec(0), spec(0)],
+            out_specs=pl.BlockSpec((4, width, patches), lambda image, lengths: (0, 0, image)),
         ),
-        out_shape=jax.ShapeDtypeStruct((3, width, rows), jnp.bfloat16),
+        out_shape=jax.ShapeDtypeStruct((4, width, rows), jnp.bfloat16),
         compiler_params=pltpu.CompilerParams(vmem_limit_bytes=48 * 1024 * 1024),
         cost_estimate=pl.CostEstimate(flops=10 * rows * patches * width, bytes_accessed=14 * rows * width, transcendentals=0),
-    )(lengths, qkv, qkv, qkv, upstream).reshape(3 * width, rows)
+    )(lengths, qkv, qkv, qkv, upstream, mixed)
+
+
+def mixer_weights_kernel(left_ref, input_ref, branch_ref, out_ref):
+    @pl.when(pl.program_id(0) < 3)
+    def _():
+        out_ref[...] = product(left_ref[0], input_ref[...]).astype(jnp.bfloat16)
+
+    @pl.when(pl.program_id(0) == 3)
+    def _():
+        out_ref[...] = product(left_ref[0], branch_ref[...]).astype(jnp.bfloat16)
+
+
+def mixer_weights(left, input_one, branch_one_grad):
+    _, width, rows = left.shape
+    whole = pl.BlockSpec((rows, width), lambda part: (0, 0))
+    return pl.pallas_call(
+        mixer_weights_kernel,
+        grid=(4,),
+        in_specs=[pl.BlockSpec((1, width, rows), lambda part: (part, 0, 0)), whole, whole],
+        out_specs=pl.BlockSpec((width, width), lambda part: (part, 0)),
+        out_shape=jax.ShapeDtypeStruct((4 * width, width), jnp.bfloat16),
+        compiler_params=pltpu.CompilerParams(vmem_limit_bytes=48 * 1024 * 1024),
+        cost_estimate=pl.CostEstimate(
+            flops=8 * rows * width * width, bytes_accessed=20 * rows * width, transcendentals=0
+        ),
+    )(left, input_one, branch_one_grad)
+
+
+def input_back_kernel(
+    left_ref, weight_ref, residual_ref, upstream_ref, scale_ref, noisy_ref, shift_out, scale_out, embed_out
+):
+    _, width, patches = left_ref.shape
+    grad = product_left(left_ref[...].reshape(3 * width, patches), weight_ref[...])
+    values = residual_ref[...]
+    normed = layer_norm(values)
+    shift_out[0] = jnp.sum(grad, axis=0, keepdims=True)
+    scale_out[0] = jnp.sum(grad * normed, axis=0, keepdims=True)
+    residual_grad = upstream_ref[...] + norm_back(values, grad * (1.0 + scale_ref[0]))
+
+    @pl.when(pl.program_id(0) == 0)
+    def _():
+        embed_out[...] = jnp.zeros_like(embed_out)
+
+    embed_out[...] += product_left(noisy_ref[...], residual_grad.astype(jnp.bfloat16))
+
+
+def input_back(left, weights, residual_zero, grad_residual, scale_one, noisy):
+    _, width, rows = left.shape
+    images, patches, _ = residual_zero.shape
+    by_image = pl.BlockSpec((patches, width), lambda image: (image, 0))
+    vector = pl.BlockSpec((1, 1, width), lambda image: (image, 0, 0))
+    return pl.pallas_call(
+        input_back_kernel,
+        grid=(images,),
+        in_specs=[
+            pl.BlockSpec((3, width, patches), lambda image: (0, 0, image)),
+            pl.BlockSpec((3 * width, width), lambda image: (0, 0)),
+            by_image,
+            by_image,
+            vector,
+            pl.BlockSpec((patches, noisy.shape[1]), lambda image: (image, 0)),
+        ],
+        out_specs=[vector, vector, pl.BlockSpec((noisy.shape[1], width), lambda image: (0, 0))],
+        out_shape=[
+            jax.ShapeDtypeStruct((images, 1, width), jnp.float32),
+            jax.ShapeDtypeStruct((images, 1, width), jnp.float32),
+            jax.ShapeDtypeStruct((noisy.shape[1], width), jnp.float32),
+        ],
+        compiler_params=pltpu.CompilerParams(vmem_limit_bytes=48 * 1024 * 1024),
+        cost_estimate=pl.CostEstimate(
+            flops=6 * rows * width * width, bytes_accessed=20 * rows * width, transcendentals=0
+        ),
+    )(
+        left,
+        weights,
+        residual_zero.reshape(rows, width),
+        grad_residual.reshape(rows, width),
+        scale_one.reshape(images, 1, width),
+        noisy,
+    )
 
 
 def across(values, axes):
@@ -1196,10 +1322,10 @@
     signal_all = jax.nn.silu(condition).astype(jnp.bfloat16)
     signal = lax.dynamic_slice_in_dim(signal_all, copy * group_images, group_images)
     mods_low = jnp.concatenate(
-        [modulator.astype(jnp.bfloat16), finisher.astype(jnp.bfloat16)], axis=1
+        [modulator.T.astype(jnp.bfloat16), finisher.T.astype(jnp.bfloat16)], axis=0
     )
     steer_here, final_here = modulator.shape[1], finisher.shape[1]
-    mods_part = product(signal, mods_low)
+    mods_part = product_right(signal, mods_low)
     mods_part = lax.reduce_precision(mods_part, 8, 7)
     mods_own = swap(mods_part.reshape(groups, -1, 128), "mp", 2)
     mods_own = mods_own.reshape(groups, images, steer_here + final_here).transpose(1, 0, 2)
@@ -1269,19 +1395,15 @@
     )
     gate_one_grad = jnp.sum(grad_residual * branch_one, axis=1)
     branch_one_grad = (steering[:, 2] * grad_residual).astype(jnp.bfloat16).reshape(rows, width)
-    outputs_part = product(mixed, branch_one_grad).astype(jnp.bfloat16)
     mixed_grad = product_right(outputs_use, branch_one_grad).astype(jnp.bfloat16)
-    qkv_grad = attend_back(qkv, mixed_grad, own_lengths, images)
-    inputs_part = product(qkv_grad, input_one).astype(jnp.bfloat16)
-    input_one_grad = product_left(qkv_grad, inputs_use).reshape(images, patches, width)
-    shift_one_grad = jnp.sum(input_one_grad, axis=1)
-    scale_one_grad = jnp.sum(input_one_grad * normed_one, axis=1)
-    grad_residual = grad_residual + norm_back(
-        residual_zero, input_one_grad * (1.0 + steering[:, 1])
-    )
-    embed_part = product_left(noisy, grad_residual.reshape(rows, width).astype(jnp.bfloat16))
-
-    mixer_part = jnp.concatenate([inputs_part, outputs_part], axis=0)
+    mixer_left = attend_back(qkv, mixed_grad, mixed, own_lengths, images)
+    shift_one_grad, scale_one_grad, embed_part = input_back(
+        mixer_left, mixer_all, residual_zero, grad_residual, steering[:, 1], noisy
+    )
+    shift_one_grad = shift_one_grad.reshape(images, width)
+    scale_one_grad = scale_one_grad.reshape(images, width)
+    mixer_part = mixer_weights(mixer_left, input_one, branch_one_grad)
+
     mixer_part = (
         mixer_part.reshape(4, groups, parts, piece_rows, width)
         .transpose(0, 2, 1, 3, 4)
@@ -1314,12 +1436,11 @@
         copies * groups,
     )
     contract_sum = reduce_weight(contract_part)
-    expand_piece = lax.psum_scatter(
-        expand_part, ("dp", "mp"), scatter_dimension=0, tiled=True
-    )
-    (mixer_sum,), cols_all, shared, signal_grad = reduce_weights(
-        [mixer_part], back, mods_low, shared, 3
-    )
+    sides = (back, mods_low, shared, features, hidden_pre, condition, time_second)
+    together = [expand_part, mixer_part] if piece_rows % 48 == 0 else [mixer_part]
+    sums, cols_all, shared, time_first_sum, time_second_sum = reduce_weights(together, sides, 3)
+    expand_sum = sums[0] if len(together) == 2 else reduce_weight(expand_part)
+    mixer_sum = sums[-1]
     held = heads_here * HD
     inputs_sum = (
         mixer_sum[: 3 * held]
@@ -1333,22 +1454,8 @@
     embed_sum = shared[: embedder.size].reshape(embedder.shape)
     readout_sum = shared[embedder.size : embedder.size + readout.size].reshape(-1, width)
     loss_sum = shared[embedder.size + readout.size]
-    signal_grad = signal_grad.reshape(copies * group_images, width)
-    expand_sum = across(jnp.where(loss_sum >= 0.0, expand_piece, 0.0), "dp")
     modulator_sum = product_left(cols_all[:, :steer_here], signal_all)
     finisher_sum = product_left(cols_all[:, steer_here:], signal_all)
-    hidden, hidden_pull = jax.vjp(jax.nn.silu, hidden_pre)
-    condition_grad = jax.vjp(jax.nn.silu, condition)[1](signal_grad)[0]
-    time_second_sum = lax.dot_general(
-        hidden, condition_grad, (((0,), (0,)), ((), ())), precision=highest
-    )
-    hidden_grad = hidden_pull(
-        lax.dot_general(condition_grad, time_second, (((1,), (1,)), ((), ())), precision=highest)
-    )[0]
-    time_first_sum = lax.dot_general(
-        features, hidden_grad, (((0,), (0,)), ((), ())), precision=highest
-    )
-
     gradients = (
         embed_sum,
         time_first_sum,

time: 750 us -> 706 us (0.941)
  matrix products: 234 us -> 176 us
  Pallas kernels: 362 us -> 412 us
  other arithmetic: 68.9 us -> 50.4 us
  local copies, waits for them, and re-layouts: 52 us -> 40.9 us
    pallas_call x0 -> x2, Pallas kernels: none -> 33.2 us  [the longest x1 17 us: input_back(): pl.pallas_call(input_back_kernel, grid=(images,), in_specs=[pl.BlockSpec(...]
    dot_general x8 -> x6, matrix products: 71.7 us -> 50.3 us  [product_left(): lax.dot_general(operand, other_operand, (((0,), (0,)), ((), ())), preferr...]
    dot_general x7 -> x4, matrix products: 65.4 us -> 47.2 us  [product(): return jnp.dot(operand, other_operand, preferred_element_type=jnp.float32)]
    dot_general x3 -> x0, matrix products: 17 us -> none  [the longest x1 7.62 us: body(): lax.dot_general(condition_grad, time_second, (((1,), (1,)), ((), ())), pr...]
    pallas_call x1, Pallas kernels: 82.6 us -> 96.2 us  [gather_pieces(): pl.pallas_call(functools.partial(gather_kernel, (copies, groups)), out_sh...]
    concatenate x2, other arithmetic: 15.1 us -> 4.16 us  [the longest x1 3.5 us: body(): jnp.concatenate([modulator.T.astype(jnp.bfloat16), finisher.T.astype(jnp....]
    dot_general x1 -> x0, local copies, waits for them, and re-layouts: 9.83 us -> none  [product_left(): lax.dot_general(operand, other_operand, (((0,), (0,)), ((), ())), preferr...]
    unnamed x134 -> x124, local copies, waits for them, and re-layouts: 16.8 us -> 18.7 us
  transfers between devices with their start and end apart: 6 -> 4, of which waited for: 1 -> 0; matrix products, arithmetic and copies ran while one was open for 36% -> 26% of each run, Pallas kernels for 41% -> 50%
where the time goes in v4:
time: 706 us; the launch traced here: 697 us
  Pallas kernels  412 us (58%)
  matrix products  176 us (25%)
  other arithmetic  50.4 us (7%)
  local copies, waits for them, and re-layouts  40.9 us (6%)
  between operations  17.4 us (2%)
    pallas_call x1, Pallas kernels, reduce_weights(): pl.pallas_call(functools.partial(reduce_kernel, (copies, groups)), out_sh...  149 us
    pallas_call x1, Pallas kernels, gather_pieces(): pl.pallas_call(functools.partial(gather_kernel, (copies, groups)), out_sh...  96.2 us
    dot_general x6, matrix products, product_right(): lax.dot_general(operand, other_operand, (((1,), (1,)), ((), ())), preferr...  70.9 us
    dot_general x6, matrix products, product_left(): lax.dot_general(operand, other_operand, (((0,), (0,)), ((), ())), preferr...  50.3 us
    dot_general x4, matrix products, product(): return jnp.dot(operand, other_operand, preferred_element_type=jnp.float32)  47.2 us
    pallas_call x1, Pallas kernels, scales(): pl.pallas_call(functools.partial(scale_kernel, layouts, flipped), out_sha...  35.2 us
    pallas_call x1, Pallas kernels, attend_back(): pl.pallas_call(attend_back_kernel, grid_spec=pltpu.PrefetchScalarGridSpec...  33.3 us
    pallas_call x1, Pallas kernels, attend(): pl.pallas_call(attend_kernel, grid_spec=pltpu.PrefetchScalarGridSpec(num_...  25.8 us
  transfers between devices with their start and end apart: 4, of which 0 were waited for; matrix products, arithmetic and copies ran while one was open for 26% of the time, Pallas kernels for 50%

profile of v4, /device:TPU:0, one launch (start us, length us, event | category | flops | bytes accessed | tf_op | source)
XLA Modules:
  0.0 696.9 jit_solution(12136515747562506260)
XLA Ops:
  7.3 1.9 fusion.24
  9.3 1.9 dynamic-slice_convert_fusion
  11.9 4.7 shard_map.378
  17.0 3.1 gather_fusion
  21.0 0.8 fusion.44.refs_6_
  21.9 7.1 %multiply_convert_fusion.3 = (bf16[128,1152]{1,0:T(8,128)(2,1)S(1)}, f32[128,1152]{1,0:T(8,128)}) fusion(bf16[128,1152]{1,0:T(8,128)(2,1)S(1)} %gather_fusion, pred[128]{0:T(512)(128)(4,1)S(1)} %compare_and_fusion, f32[1152,1152]{1,0:T(8,128)} %refs_12_.1, f32[128,1152]{1,0:T(8,128)S(1)} %fusion.44.refs_6_), kind=kOutput, calls=%fused_computation.57 | convolution fusion | flops 2040201216 | bytes 7078016 | tf_op jit(solution)/shard_map/dot_general | solution.py:1321
  30.6 0.9 convolution_reduce-precision_fusion
  31.6 8.5 %shard_map.379 = f32[8,36,128]{2,1,0:T(8,128)S(1)} custom-call(f32[8,36,128]{2,1,0:T(8,128)S(1)} %reshape.372.x_ref), custom_call_target="tpu_custom_call" | custom-call | tf_op jit(solution)/shard_map/pallas_call | solution.py:151
  43.6 0.9 fusion.25
  44.6 96.2 %shard_map.380 = bf16[2,2,4,2,3,48,1152]{6,5,4,3,2,1,0:T(8,128)(2,1)} custom-call(bf16[3,48,1152]{2,1,0:T(8,128)(2,1)} %bitcast.172), custom_call_target="tpu_custom_call" | custom-call | tf_op jit(solution)/shard_map/pallas_call | solution.py:731
  140.8 2.8 multiply_cosine_fusion
  143.6 0.9 concatenate.23
  144.5 1.0 fusion.52
  146.2 2.0 add_convert_fusion.2
  148.2 14.6 %fusion.9.q_ref.k_ref.v_ref = bf16[3456,1024]{1,0:T(8,128)(2,1)} fusion(bf16[1024,1152]{1,0:T(8,128)(2,1)S(1)} %bitcast.137, bf16[4608,1152]{1,0:T(8,128)(2,1)} %bitcast.152), kind=kOutput, calls=%fused_computation.15 | convolution fusion | flops 8157265920 | bytes 17399808 | tf_op jit(solution)/shard_map/dot_general | solution.py:32
  162.8 1.4 copy-done.3
  164.2 25.8 %shard_map.381.mixed_ref = bf16[1152,1024]{1,0:T(8,128)(2,1)S(1)} custom-call(s32[4]{0:T(128)S(1)} %dynamic_slice.48.length_ref, bf16[3456,1024]{1,0:T(8,128)(2,1)} %fusion.9.q_ref.k_ref.v_ref, bf16[3456,1024]{1,0:T(8,128)(2,1)} %fusion.9.q_ref.k_ref.v_ref, bf16[3456,1024]{1,0:T(8,128)(2,1)} %fusion.9.q_ref.k_ref.v_ref), custom_call_target="tpu_custom_call" | custom-call | flops 1207959552 | bytes 9437184 | tf_op jit(solution)/shard_map/pallas_call | solution.py:1123
  190.0 6.2 fusion.17
  196.9 1.5 copy-done.15
  199.0 1.5 copy-done.9
  200.5 2.0 add_convert_fusion.1
  202.6 19.7 %fusion.53 = f32[1024,4608]{1,0:T(8,128)} fusion(bf16[1024,1152]{1,0:T(8,128)(2,1)S(1)} %bitcast.168, bf16[4608,1152]{1,0:T(8,128)(2,1)} %all-gather.4.cloned.1.call-done), kind=kOutput, calls=%fused_computation.151 | convolution fusion | flops 10871635968 | bytes 31850496 | tf_op jit(solution)/shard_map/dot_general | solution.py:32
  222.3 22.8 %fusion.46 = f32[1024,1152]{1,0:T(8,128)S(1)} fusion(bf16[4608,1152]{1,0:T(8,128)(2,1)} %all-gather.6.cloned.1.call-done, f32[1024,4608]{1,0:T(8,128)} %fusion.53), kind=kOutput, calls=%fused_computation.144 | convolution fusion | flops 10914103296 | bytes 34209792 | tf_op jit(solution)/shard_map/dot_general | solution.py:28
  245.8 1.5 copy-done.16
  248.0 2.0 add_convert_fusion
  250.0 1.3 select_reduce_fusion
  251.4 2.9 fusion.13
  254.3 6.5 fusion.15
  260.9 1.2 copy-done.12
  262.1 3.5 multiply_reduce_fusion
  265.5 2.2 copy-done.13
  268.1 1.4 copy-done.29
  269.5 21.0 %convolution_convert_fusion = bf16[4608,1152]{1,0:T(8,128)(2,1)} fusion(bf16[1024,1152]{1,0:T(8,128)(2,1)S(1)} %bitcast.170, f32[1024,4608]{1,0:T(8,128)} %fusion.53), kind=kOutput, calls=%fused_computation.3 | convolution fusion | flops 10919411712 | bytes 31850496 | tf_op jit(solution)/shard_map/dot_general | solution.py:38
  292.6 1.3 stack.127.refs_11_
  293.9 1.3 concatenate.27.refs_10_
  295.9 3.5 pad_maximum_fusion.refs_3_
  300.1 27.4 %fusion.6 = bf16[1024,4608]{1,0:T(8,128)(2,1)S(1)} fusion(f32[1024,4608]{1,0:T(8,128)} %fusion.53, bf16[1024,1152]{1,0:T(8,128)(2,1)} %bitcast.171, bf16[4608,1152]{1,0:T(8,128)(2,1)} %all-gather.6.cloned.1.call-done), kind=kOutput, calls=%fused_computation.11 | convolution fusion | flops 10966007808 | bytes 41287680 | tf_op jit(solution)/shard_map/dot_general | solution.py:32
  327.6 22.0 %fusion.12 = (f32[1024]{0:T(1024)S(1)}, f32[1024,1152]{1,0:T(8,128)}) fusion(f32[4,1152]{1,0:T(4,128)S(1)} %bitcast.184, bf16[1024,4608]{1,0:T(8,128)(2,1)S(1)} %fusion.6, bf16[4608,1152]{1,0:T(8,128)(2,1)} %all-gather.4.cloned.1.call-done), kind=kOutput, calls=%fused_computation.18 | convolution fusion | flops 10873994240 | bytes 24795136 | tf_op jit(solution)/shard_map/dot_general | solution.py:28
  349.7 6.7 fusion.14
  356.4 6.7 multiply_reduce_fusion.1
  363.6 1.7 copy-done.17
  365.3 5.4 convolution_convert_fusion.2.up_ref
  370.7 1.4 copy-done.5
  372.1 33.3 %shard_map.382.left_ref = bf16[4,1152,1024]{2,1,0:T(8,128)(2,1)} custom-call(s32[4]{0:T(128)S(1)} %copy-done.8, bf16[3456,1024]{1,0:T(8,128)(2,1)} %fusion.9.q_ref.k_ref.v_ref, bf16[3456,1024]{1,0:T(8,128)(2,1)} %fusion.9.q_ref.k_ref.v_ref, bf16[3456,1024]{1,0:T(8,128)(2,1)} %fusion.9.q_ref.k_ref.v_ref, ...), custom_call_target="tpu_custom_call" | custom-call | flops 3019898880 | bytes 16515072 | tf_op jit(solution)/shard_map/pallas_call | solution.py:1141
  405.4 17.0 %shard_map.384 = (f32[4,1,1152]{2,1,0:T(1,128)S(1)}, f32[4,1,1152]{2,1,0:T(1,128)S(1)}, f32[16,1152]{1,0:T(8,128)S(1)}) custom-call(bf16[4,1152,1024]{2,1,0:T(8,128)(2,1)} %shard_map.382.left_ref, bf16[4608,1152]{1,0:T(8,128)(2,1)} %bitcast.155, f32[1024,1152]{1,0:T(8,128)S(1)} %bitcast.136, f32[1024,1152]{1,0:T(8,128)} %bitcast.150, ...), custom_call_target="tpu_custom_call" | custom-call | flops 8153726976 | bytes 23592960 | tf_op jit(solution)/shard_map/pallas_call | solution.py:1204
  422.9 1.4 select_maximum_fusion
  424.2 18.5 %convolution_convert_fusion.1 = bf16[4608,1152]{1,0:T(8,128)(2,1)} fusion(bf16[1024,4608]{1,0:T(8,128)(2,1)} %copy-done.54, bf16[1024,1152]{1,0:T(8,128)(2,1)} %bitcast.169), kind=kOutput, calls=%fused_computation.4 | convolution fusion | flops 10876944384 | bytes 22413312 | tf_op jit(solution)/shard_map/dot_general | solution.py:38
  442.8 0.8 maximum_bitcast_fusion.refs_2_
  443.5 1.7 copy-done.6
  445.2 16.2 %shard_map.383 = bf16[4608,1152]{1,0:T(8,128)(2,1)} custom-call(bf16[4,1152,1024]{2,1,0:T(8,128)(2,1)} %shard_map.382.left_ref, bf16[1024,1152]{1,0:T(8,128)(2,1)S(1)} %bitcast.138, bf16[1024,1152]{1,0:T(8,128)(2,1)S(1)} %bitcast.140), custom_call_target="tpu_custom_call" | custom-call | flops 10871635968 | bytes 23592960 | tf_op jit(solution)/shard_map/pallas_call | solution.py:1168
  461.4 149.3 %shard_map.385 = (bf16[2,2,3,48,1152]{4,3,2,1,0:T(8,128)(2,1)}, bf16[2,2,3,48,1152]{4,3,2,1,0:T(8,128)(2,1)}, f32[32,4,1152]{2,1,0:T(4,128)}, f32[32,16,128]{2,1...) custom-call(bf16[2,2,4,2,3,48,1152]{6,5,4,3,2,1,0:T(8,128)(2,1)} %bitcast.156, ...), custom_call_target="tpu_custom_call" | custom-call | tf_op jit(solution)/shard_map/pallas_call | solution.py:568
  610.7 1.8 slice.162.refs_5_
  612.5 1.3 slice.161
  613.8 1.2 slice.159
  615.0 1.2 convert_element_type.148
  616.2 0.9 fusion.49
  618.4 1.1 copy.56
  619.5 1.5 fusion.29.refs_8_
  621.1 2.6 fusion.27.refs_3_
  623.7 35.2 %shard_map.386 = (f32[1152,128]{1,0:T(8,128)}, f32[16,1152]{1,0:T(8,128)}, f32[16,1152]{1,0:T(8,128)}, f32[16,1152]{1,0:T(8,128)}, f32[8,8,1152]{2,1,0:T(8,128)}, /*index=5*/f32[8,128]{1,0:T(8,128)}) custom-call(f32[16,1152]{1,0:T(8,128)} %reshape.397.refs_0_, f32[256,1152]{1,0:T(8,128)} %get-tuple-element.66.refs_1_, ...), custom_call_target="tpu_custom_call" | custom-call | tf_op jit(solution)/shard_map/pallas_call | solution.py:911
  658.8 1.2 slice.144
  660.0 25.5 %shard_map.387 = (f32[16,1152]{1,0:T(8,128)}, f32[256,1152]{1,0:T(8,128)}, f32[1152,1152]{1,0:T(8,128)}, f32[864,1152]{1,0:T(8,128)}, f32[432,1152]{1,0:T(8,128)...) custom-call(f32[16,1152]{1,0:T(8,128)} %reshape.397.refs_0_, ...), custom_call_target="tpu_custom_call" | custom-call | flops 19906560 | bytes 79626240 | tf_op jit(solution)/shard_map/pallas_call | solution.py:1022
  685.5 1.6 reduce.5
  687.1 1.7 reduce.6
  (246 shorter events, 15.5 us)
Async XLA Ops:
  7.2 13.8 %copy-start.23 = (f32[256,1152]{1,0:T(8,128)S(1)}, f32[256,1152]{1,0:T(8,128)}, u32[]{:S(2)}) copy-start(f32[256,1152]{1,0:T(8,128)} %refs_11_.1) | copy-start | bytes 3538948
  7.2 195.4 %all-gather.4.cloned.1.call-start = ((), (), s32[]{:S(2)}) async-start(), calls=%async_computation.1 | async-start | bytes 10948608 | tf_op jit(solution)/shard_map/all_gather | solution.py:1236
  9.2 213.1 %all-gather.6.cloned.1.call-start = ((), (), s32[]{:S(2)}) async-start(), calls=%async_computation.2 | async-start | bytes 10948608 | tf_op jit(solution)/shard_map/all_gather | solution.py:1236
  11.2 431.6 %reduce-scatter.2.cloned.1.call-start = ((), (), s32[]{:S(2)}) async-start(), calls=%async_computation.3 | async-start | bytes 10948608 | tf_op jit(solution)/shard_map/reduce_scatter | solution.py:1244
  20.0 8.9 %copy-start.21 = (f32[1152,288]{0,1:T(8,128)S(1)}, f32[1152,288]{0,1:T(8,128)}, u32[]{:S(2)}) copy-start(f32[1152,288]{0,1:T(8,128)} %param.34) | copy-start | bytes 3981316
  20.4 0.6 copy-start.31
  20.4 0.6 copy-start.33
  21.9 7.1 %copy-start.22 = (f32[128,1152]{1,0:T(8,128)}, f32[128,1152]{1,0:T(8,128)S(1)}, u32[]{:S(2)}) copy-start(f32[128,1152]{1,0:T(8,128)S(1)} %fusion.44.refs_6_) | copy-start | bytes 1769476
  21.9 7.2 %copy-start.18 = (f32[1152,864]{0,1:T(8,128)S(1)}, f32[1152,864]{0,1:T(8,128)}, u32[]{:S(2)}) copy-start(f32[1152,864]{0,1:T(8,128)} %param.29) | copy-start | bytes 11943940
  29.0 0.7 copy-start.25
  29.1 0.8 copy-start.27
  29.1 11.8 %copy-start.53 = (s32[128]{0:T(128)S(1)}, s32[128]{0:T(128)}, u32[]{:S(2)}) copy-start(s32[128]{0:T(128)} %param.24) | copy-start | bytes 1540
  29.1 13.3 %copy-start.52 = (f32[32]{0:T(128)S(1)}, f32[32]{0:T(128)}, u32[]{:S(2)}) copy-start(f32[32]{0:T(128)} %param.21) | copy-start | bytes 388
  29.1 13.4 %copy-start.46 = (f32[4,256,16]{1,2,0:T(8,128)S(1)}, f32[4,256,16]{1,2,0:T(8,128)}, u32[]{:S(2)}) copy-start(f32[4,256,16]{1,2,0:T(8,128)} %param.19) | copy-start | bytes 196612
  29.1 13.3 %copy-start.47 = (f32[4,256,16]{1,2,0:T(8,128)S(1)}, f32[4,256,16]{1,2,0:T(8,128)}, u32[]{:S(2)}) copy-start(f32[4,256,16]{1,2,0:T(8,128)} %param.20) | copy-start | bytes 196612
  29.1 13.5 %copy-start.24 = (f32[144,1152]{1,0:T(8,128)S(1)}, f32[144,1152]{1,0:T(8,128)}, u32[]{:S(2)}) copy-start(f32[144,1152]{1,0:T(8,128)} %refs_15_.1) | copy-start | bytes 1990660
  29.3 1.3 copy-start.20
  29.4 13.3 %copy-start.19 = (f32[1152,432]{0,1:T(8,128)S(1)}, f32[1152,432]{0,1:T(8,128)}, u32[]{:S(2)}) copy-start(f32[1152,432]{0,1:T(8,128)} %param.30) | copy-start | bytes 5971972
  42.3 120.5 %copy-start.7 = (s32[4]{0:T(128)}, s32[4]{0:T(128)S(1)}, u32[]{:S(2)}) copy-start(s32[4]{0:T(128)S(1)} %dynamic_slice.48.length_ref) | copy-start | bytes 52
  42.4 0.8 copy-start.40
  42.5 102.0 %copy-start.35 = (bf16[4,256,16]{1,2,0:T(8,128)(2,1)}, bf16[4,256,16]{1,2,0:T(8,128)(2,1)S(1)}, u32[]{:S(2)}) copy-start(bf16[4,256,16]{1,2,0:T(8,128)(2,1)S(1)} %get-tuple-element.123) | copy-start | bytes 98308
  43.6 155.4 %copy-start.38 = (f32[4,1,1,1152]{3,0,2,1:T(4,128)}, f32[4,1,1,1152]{3,0,2,1:T(4,128)S(1)}, u32[]{:S(2)}) copy-start(f32[4,1,1,1152]{3,0,2,1:T(4,128)S(1)} %copy.76) | copy-start | bytes 55300
  44.6 100.0 %copy-start.37 = (f32[16,1152]{1,0:T(8,128)S(1)}, f32[16,1152]{1,0:T(8,128)}, u32[]{:S(2)}) copy-start(f32[16,1152]{1,0:T(8,128)} %refs_10_.1) | copy-start | bytes 221188
  145.5 50.7 %copy-start = (f32[4,256,1152]{2,1,0:T(8,128)}, f32[4,256,1152]{2,1,0:T(8,128)S(1)}, u32[]{:S(2)}) copy-start(f32[4,256,1152]{2,1,0:T(8,128)S(1)} %get-tuple-element.154) | copy-start | bytes 14155780
  146.2 50.1 %copy-start.41 = (f32[4,1152]{1,0:T(4,128)}, f32[4,1152]{1,0:T(4,128)S(1)}, u32[]{:S(2)}) copy-start(f32[4,1152]{1,0:T(4,128)S(1)} %get-tuple-element.166) | copy-start | bytes 55300
  162.8 1.4 copy-start.3
  189.9 6.3 copy-start.1
  196.2 2.1 copy-start.15
  198.3 2.2 copy-start.9
  198.4 4.2 copy-start.44
  199.0 23.3 %copy-start.48 = (f32[4,256]{1,0:T(4,128)}, f32[4,256]{1,0:T(4,128)S(1)}, u32[]{:S(2)}) copy-start(f32[4,256]{1,0:T(4,128)S(1)} %add_rsqrt_fusion.1) | copy-start | bytes 12292
  202.6 19.7 %copy-start.28 = (bf16[4,256,1152]{2,1,0:T(8,128)(2,1)}, bf16[4,256,1152]{2,1,0:T(8,128)(2,1)S(1)}, u32[]{:S(2)}) copy-start(bf16[4,256,1152]{2,1,0:T(8,128)(2,1)S(1)} %add_convert_fusion.1) | copy-start | bytes 7077892
  222.3 22.9 %copy-start.10 = (f32[4,256,1152]{2,1,0:T(8,128)S(1)}, f32[4,256,1152]{2,1,0:T(8,128)}, u32[]{:S(2)}) copy-start(f32[4,256,1152]{2,1,0:T(8,128)} %copy-done.9) | copy-start | bytes 14155780
  245.2 2.2 copy-start.16
  247.4 2.7 copy-start.11
  248.0 2.0 copy-start.30
  251.4 9.5 %slice-start.2 = ((s8[4718592]{0:T(1024)(128)(4,1)}), s8[524288]{0:T(1024)(128)(4,1)S(1)}, s32[]{:S(2)}) async-start(s8[4718592]{0:T(1024)(128)(4,1)} %bitcast.142), calls=%async_computation.7 | async-start | bytes 1048576
  254.3 6.5 slice-start.3
  254.3 7.7 %copy-start.12 = (f32[1024,1152]{1,0:T(8,128)S(1)}, f32[1024,1152]{1,0:T(8,128)}, u32[]{:S(2)}) copy-start(f32[1024,1152]{1,0:T(8,128)} %get-tuple-element.156) | copy-start | bytes 14155780
  265.5 2.2 copy-start.13
  268.1 1.4 copy-start.29
  290.5 0.8 copy-start.43
  290.5 1.0 copy-start.36
  290.5 1.2 copy-start.50
  290.5 1.9 copy-start.51
  290.6 4.7 copy-start.32
  290.6 4.7 copy-start.34
  290.6 333.1 %all-gather.8.cloned.1.call-start = ((), (), s32[]{:S(2)}) async-start(), calls=%async_computation.4 | async-start | bytes 1658880 | tf_op jit(solution)/shard_map/all_gather | solution.py:1236
  300.1 27.4 %copy-start.39 = (f32[4,1,1,1152]{3,0,2,1:T(4,128)S(1)}, f32[4,1,1,1152]{3,0,2,1:T(4,128)}, u32[]{:S(2)}) copy-start(f32[4,1,1,1152]{3,0,2,1:T(4,128)} %copy-done.38) | copy-start | bytes 55300
  327.5 22.1 %copy-start.54 = (bf16[1024,4608]{1,0:T(8,128)(2,1)}, bf16[1024,4608]{1,0:T(8,128)(2,1)S(1)}, u32[]{:S(2)}) copy-start(bf16[1024,4608]{1,0:T(8,128)(2,1)S(1)} %fusion.6) | copy-start | bytes 28311556
  327.5 22.1 %copy-start.45 = (f32[4,256]{1,0:T(4,128)S(1)}, f32[4,256]{1,0:T(4,128)}, u32[]{:S(2)}) copy-start(f32[4,256]{1,0:T(4,128)} %copy-done.44) | copy-start | bytes 12292
  327.6 22.1 %copy-start.49 = (f32[4,256]{1,0:T(4,128)S(1)}, f32[4,256]{1,0:T(4,128)}, u32[]{:S(2)}) copy-start(f32[4,256]{1,0:T(4,128)} %copy-done.48) | copy-start | bytes 12292
  349.6 6.7 copy-start.14
  356.4 6.8 copy-start.42
  363.1 2.2 copy-start.17
  365.3 6.8 copy-start.2
  365.3 6.8 copy-start.8
  365.3 40.1 %slice-start = ((s8[4718592]{0:T(1024)(128)(4,1)}), s8[4194304]{0:T(1024)(128)(4,1)S(1)}, s32[]{:S(2)}) async-start(s8[4718592]{0:T(1024)(128)(4,1)} %bitcast.134), calls=%async_computation.5 | async-start | bytes 8388608
  370.7 1.4 copy-start.5
  372.1 33.3 %slice-start.1 = ((s8[4718592]{0:T(1024)(128)(4,1)}), s8[524288]{0:T(1024)(128)(4,1)S(1)}, s32[]{:S(2)}) async-start(s8[4718592]{0:T(1024)(128)(4,1)} %bitcast.134), calls=%async_computation.6 | async-start | bytes 1048576
  424.2 19.3 %copy-start.4 = (bf16[4,256,1152]{2,1,0:T(8,128)(2,1)S(1)}, bf16[4,256,1152]{2,1,0:T(8,128)(2,1)}, u32[]{:S(2)}) copy-start(bf16[4,256,1152]{2,1,0:T(8,128)(2,1)} %copy-done.3) | copy-start | bytes 7077892
  443.5 1.7 copy-start.6
  610.7 8.8 %copy-start.26 = (bf16[128,1152]{1,0:T(8,128)(2,1)S(1)}, bf16[128,1152]{1,0:T(8,128)(2,1)}, u32[]{:S(2)}) copy-start(bf16[128,1152]{1,0:T(8,128)(2,1)} %copy-done.25) | copy-start | bytes 884740
Sparse Core Ops, SparseCore 0:
  11.6 114.7 all-gather.3
  130.0 86.6 all-gather.5
  290.7 141.9 reduce-scatter.1
  442.9 18.7 all-gather.7

commit v5 on v4

--- a/solution.py
+++ b/solution.py
@@ -1057,7 +1057,7 @@
     live = lax.broadcasted_iota(jnp.int32, (patches, patches), 0) < length_ref[pl.program_id(0)]
     upper = lax.broadcasted_iota(jnp.int32, (pair, patches), 0) < HD
 
-    @pl.loop(0, q_ref.shape[0] // pair, unroll=4)
+    @pl.loop(0, q_ref.shape[0] // pair, unroll=8)
     def _(index):
         rows = pl.ds(pl.multiple_of(index * pair, 16), pair)
         queries, keys, values = q_ref[rows, :], k_ref[rows, :], v_ref[rows, :]
@@ -1077,7 +1077,7 @@
     live = lax.broadcasted_iota(jnp.int32, (patches, patches), 0) < length_ref[pl.program_id(0)]
     upper = lax.broadcasted_iota(jnp.int32, (pair, patches), 0) < HD
 
-    @pl.loop(0, q_ref.shape[0] // pair, unroll=4)
+    @pl.loop(0, q_ref.shape[0] // pair, unroll=8)
     def _(index):
         rows = pl.ds(pl.multiple_of(index * pair, 16), pair)
         queries, keys, values, upstream = (

time: 706 us -> 704 us (level)
  no operation moved by 1% of the time
where the time goes in v5:
time: 704 us; the launch traced here: 695 us
  Pallas kernels  409 us (58%)
  matrix products  176 us (25%)
  other arithmetic  50.4 us (7%)
  local copies, waits for them, and re-layouts  40.9 us (6%)
  between operations  17.4 us (2%)
    pallas_call x1, Pallas kernels, reduce_weights(): pl.pallas_call(functools.partial(reduce_kernel, (copies, groups)), out_sh...  149 us
    pallas_call x1, Pallas kernels, gather_pieces(): pl.pallas_call(functools.partial(gather_kernel, (copies, groups)), out_sh...  96.2 us
    dot_general x6, matrix products, product_right(): lax.dot_general(operand, other_operand, (((1,), (1,)), ((), ())), preferr...  71 us
    dot_general x6, matrix products, product_left(): lax.dot_general(operand, other_operand, (((0,), (0,)), ((), ())), preferr...  50.3 us
    dot_general x4, matrix products, product(): return jnp.dot(operand, other_operand, preferred_element_type=jnp.float32)  47.2 us
    pallas_call x1, Pallas kernels, scales(): pl.pallas_call(functools.partial(scale_kernel, layouts, flipped), out_sha...  35.3 us
    pallas_call x1, Pallas kernels, attend_back(): pl.pallas_call(attend_back_kernel, grid_spec=pltpu.PrefetchScalarGridSpec...  32 us
    pallas_call x1, Pallas kernels, apply_scales(): pl.pallas_call(functools.partial(apply_kernel, layouts, flipped, groups),...  25.5 us
  transfers between devices with their start and end apart: 4, of which 0 were waited for; matrix products, arithmetic and copies ran while one was open for 26% of the time, Pallas kernels for 50%

profile of v5, /device:TPU:0, one launch (start us, length us, event | category | flops | bytes accessed | tf_op | source)
XLA Modules:
  0.0 694.7 jit_solution(11674062036695697538)
XLA Ops:
  7.3 1.9 fusion.24
  9.3 1.9 dynamic-slice_convert_fusion
  11.9 4.7 shard_map.378
  17.0 3.1 gather_fusion
  21.0 0.8 fusion.44.refs_6_
  21.9 7.1 %multiply_convert_fusion.3 = (bf16[128,1152]{1,0:T(8,128)(2,1)S(1)}, f32[128,1152]{1,0:T(8,128)}) fusion(bf16[128,1152]{1,0:T(8,128)(2,1)S(1)} %gather_fusion, pred[128]{0:T(512)(128)(4,1)S(1)} %compare_and_fusion, f32[1152,1152]{1,0:T(8,128)} %refs_12_.1, f32[128,1152]{1,0:T(8,128)S(1)} %fusion.44.refs_6_), kind=kOutput, calls=%fused_computation.57 | convolution fusion | flops 2040201216 | bytes 7078016 | tf_op jit(solution)/shard_map/dot_general | solution.py:1321
  30.6 0.9 convolution_reduce-precision_fusion
  31.6 8.5 %shard_map.379 = f32[8,36,128]{2,1,0:T(8,128)S(1)} custom-call(f32[8,36,128]{2,1,0:T(8,128)S(1)} %reshape.372.x_ref), custom_call_target="tpu_custom_call" | custom-call | tf_op jit(solution)/shard_map/pallas_call | solution.py:151
  43.6 0.9 fusion.25
  44.6 96.2 %shard_map.380 = bf16[2,2,4,2,3,48,1152]{6,5,4,3,2,1,0:T(8,128)(2,1)} custom-call(bf16[3,48,1152]{2,1,0:T(8,128)(2,1)} %bitcast.172), custom_call_target="tpu_custom_call" | custom-call | tf_op jit(solution)/shard_map/pallas_call | solution.py:731
  140.8 2.8 multiply_cosine_fusion
  143.6 0.9 concatenate.23
  144.5 1.0 fusion.52
  146.2 2.0 add_convert_fusion.2
  148.2 14.6 %fusion.9.q_ref.k_ref.v_ref = bf16[3456,1024]{1,0:T(8,128)(2,1)} fusion(bf16[1024,1152]{1,0:T(8,128)(2,1)S(1)} %bitcast.137, bf16[4608,1152]{1,0:T(8,128)(2,1)} %bitcast.152), kind=kOutput, calls=%fused_computation.15 | convolution fusion | flops 8157265920 | bytes 17399808 | tf_op jit(solution)/shard_map/dot_general | solution.py:32
  162.8 1.4 copy-done.3
  164.2 24.5 %shard_map.381.mixed_ref = bf16[1152,1024]{1,0:T(8,128)(2,1)S(1)} custom-call(s32[4]{0:T(128)S(1)} %dynamic_slice.48.length_ref, bf16[3456,1024]{1,0:T(8,128)(2,1)} %fusion.9.q_ref.k_ref.v_ref, bf16[3456,1024]{1,0:T(8,128)(2,1)} %fusion.9.q_ref.k_ref.v_ref, bf16[3456,1024]{1,0:T(8,128)(2,1)} %fusion.9.q_ref.k_ref.v_ref), custom_call_target="tpu_custom_call" | custom-call | flops 1207959552 | bytes 9437184 | tf_op jit(solution)/shard_map/pallas_call | solution.py:1123
  188.7 6.2 fusion.17
  195.6 1.5 copy-done.15
  197.8 1.5 copy-done.9
  199.3 2.0 add_convert_fusion.1
  201.4 19.8 %fusion.53 = f32[1024,4608]{1,0:T(8,128)} fusion(bf16[1024,1152]{1,0:T(8,128)(2,1)S(1)} %bitcast.168, bf16[4608,1152]{1,0:T(8,128)(2,1)} %all-gather.4.cloned.1.call-done), kind=kOutput, calls=%fused_computation.151 | convolution fusion | flops 10871635968 | bytes 31850496 | tf_op jit(solution)/shard_map/dot_general | solution.py:32
  221.3 22.8 %fusion.46 = f32[1024,1152]{1,0:T(8,128)S(1)} fusion(bf16[4608,1152]{1,0:T(8,128)(2,1)} %all-gather.6.cloned.1.call-done, f32[1024,4608]{1,0:T(8,128)} %fusion.53), kind=kOutput, calls=%fused_computation.144 | convolution fusion | flops 10914103296 | bytes 34209792 | tf_op jit(solution)/shard_map/dot_general | solution.py:28
  244.8 1.5 copy-done.16
  246.9 2.0 add_convert_fusion
  249.0 1.3 select_reduce_fusion
  250.3 2.9 fusion.13
  253.3 6.5 fusion.15
  259.8 1.2 copy-done.12
  261.0 3.5 multiply_reduce_fusion
  264.5 2.2 copy-done.13
  267.0 1.4 copy-done.29
  268.4 21.0 %convolution_convert_fusion = bf16[4608,1152]{1,0:T(8,128)(2,1)} fusion(bf16[1024,1152]{1,0:T(8,128)(2,1)S(1)} %bitcast.170, f32[1024,4608]{1,0:T(8,128)} %fusion.53), kind=kOutput, calls=%fused_computation.3 | convolution fusion | flops 10919411712 | bytes 31850496 | tf_op jit(solution)/shard_map/dot_general | solution.py:38
  291.6 1.3 stack.127.refs_11_
  292.9 1.3 concatenate.27.refs_10_
  294.9 3.5 pad_maximum_fusion.refs_3_
  299.1 27.4 %fusion.6 = bf16[1024,4608]{1,0:T(8,128)(2,1)S(1)} fusion(f32[1024,4608]{1,0:T(8,128)} %fusion.53, bf16[1024,1152]{1,0:T(8,128)(2,1)} %bitcast.171, bf16[4608,1152]{1,0:T(8,128)(2,1)} %all-gather.6.cloned.1.call-done), kind=kOutput, calls=%fused_computation.11 | convolution fusion | flops 10966007808 | bytes 41287680 | tf_op jit(solution)/shard_map/dot_general | solution.py:32
  326.5 22.0 %fusion.12 = (f32[1024]{0:T(1024)S(1)}, f32[1024,1152]{1,0:T(8,128)}) fusion(f32[4,1152]{1,0:T(4,128)S(1)} %bitcast.184, bf16[1024,4608]{1,0:T(8,128)(2,1)S(1)} %fusion.6, bf16[4608,1152]{1,0:T(8,128)(2,1)} %all-gather.4.cloned.1.call-done), kind=kOutput, calls=%fused_computation.18 | convolution fusion | flops 10873994240 | bytes 24795136 | tf_op jit(solution)/shard_map/dot_general | solution.py:28
  348.6 6.7 fusion.14
  355.3 6.7 multiply_reduce_fusion.1
  362.5 1.7 copy-done.17
  364.2 5.4 convolution_convert_fusion.2.up_ref
  369.6 1.4 copy-done.5
  371.1 32.0 %shard_map.382.left_ref = bf16[4,1152,1024]{2,1,0:T(8,128)(2,1)} custom-call(s32[4]{0:T(128)S(1)} %copy-done.8, bf16[3456,1024]{1,0:T(8,128)(2,1)} %fusion.9.q_ref.k_ref.v_ref, bf16[3456,1024]{1,0:T(8,128)(2,1)} %fusion.9.q_ref.k_ref.v_ref, bf16[3456,1024]{1,0:T(8,128)(2,1)} %fusion.9.q_ref.k_ref.v_ref, ...), custom_call_target="tpu_custom_call" | custom-call | flops 3019898880 | bytes 16515072 | tf_op jit(solution)/shard_map/pallas_call | solution.py:1141
  403.0 17.2 %shard_map.384 = (f32[4,1,1152]{2,1,0:T(1,128)S(1)}, f32[4,1,1152]{2,1,0:T(1,128)S(1)}, f32[16,1152]{1,0:T(8,128)S(1)}) custom-call(bf16[4,1152,1024]{2,1,0:T(8,128)(2,1)} %shard_map.382.left_ref, bf16[4608,1152]{1,0:T(8,128)(2,1)} %bitcast.155, f32[1024,1152]{1,0:T(8,128)S(1)} %bitcast.136, f32[1024,1152]{1,0:T(8,128)} %bitcast.150, ...), custom_call_target="tpu_custom_call" | custom-call | flops 8153726976 | bytes 23592960 | tf_op jit(solution)/shard_map/pallas_call | solution.py:1204
  420.6 1.4 select_maximum_fusion
  422.0 18.5 %convolution_convert_fusion.1 = bf16[4608,1152]{1,0:T(8,128)(2,1)} fusion(bf16[1024,4608]{1,0:T(8,128)(2,1)} %copy-done.54, bf16[1024,1152]{1,0:T(8,128)(2,1)} %bitcast.169), kind=kOutput, calls=%fused_computation.4 | convolution fusion | flops 10876944384 | bytes 22413312 | tf_op jit(solution)/shard_map/dot_general | solution.py:38
  440.5 0.8 maximum_bitcast_fusion.refs_2_
  441.3 1.7 copy-done.6
  442.9 16.2 %shard_map.383 = bf16[4608,1152]{1,0:T(8,128)(2,1)} custom-call(bf16[4,1152,1024]{2,1,0:T(8,128)(2,1)} %shard_map.382.left_ref, bf16[1024,1152]{1,0:T(8,128)(2,1)S(1)} %bitcast.138, bf16[1024,1152]{1,0:T(8,128)(2,1)S(1)} %bitcast.140), custom_call_target="tpu_custom_call" | custom-call | flops 10871635968 | bytes 23592960 | tf_op jit(solution)/shard_map/pallas_call | solution.py:1168
  459.1 149.1 %shard_map.385 = (bf16[2,2,3,48,1152]{4,3,2,1,0:T(8,128)(2,1)}, bf16[2,2,3,48,1152]{4,3,2,1,0:T(8,128)(2,1)}, f32[32,4,1152]{2,1,0:T(4,128)}, f32[32,16,128]{2,1...) custom-call(bf16[2,2,4,2,3,48,1152]{6,5,4,3,2,1,0:T(8,128)(2,1)} %bitcast.156, ...), custom_call_target="tpu_custom_call" | custom-call | tf_op jit(solution)/shard_map/pallas_call | solution.py:568
  608.3 1.8 slice.162.refs_5_
  610.0 1.3 slice.161
  611.3 1.2 slice.159
  612.5 1.2 convert_element_type.148
  613.8 0.9 fusion.49
  616.0 1.1 copy.56
  617.1 1.5 fusion.29.refs_8_
  618.6 2.6 fusion.27.refs_3_
  621.2 35.3 %shard_map.386 = (f32[1152,128]{1,0:T(8,128)}, f32[16,1152]{1,0:T(8,128)}, f32[16,1152]{1,0:T(8,128)}, f32[16,1152]{1,0:T(8,128)}, f32[8,8,1152]{2,1,0:T(8,128)}, /*index=5*/f32[8,128]{1,0:T(8,128)}) custom-call(f32[16,1152]{1,0:T(8,128)} %reshape.397.refs_0_, f32[256,1152]{1,0:T(8,128)} %get-tuple-element.66.refs_1_, ...), custom_call_target="tpu_custom_call" | custom-call | tf_op jit(solution)/shard_map/pallas_call | solution.py:911
  656.6 1.2 slice.144
  657.8 25.5 %shard_map.387 = (f32[16,1152]{1,0:T(8,128)}, f32[256,1152]{1,0:T(8,128)}, f32[1152,1152]{1,0:T(8,128)}, f32[864,1152]{1,0:T(8,128)}, f32[432,1152]{1,0:T(8,128)...) custom-call(f32[16,1152]{1,0:T(8,128)} %reshape.397.refs_0_, ...), custom_call_target="tpu_custom_call" | custom-call | flops 19906560 | bytes 79626240 | tf_op jit(solution)/shard_map/pallas_call | solution.py:1022
  683.3 1.6 reduce.5
  684.8 1.7 reduce.6
  (246 shorter events, 15.5 us)
Async XLA Ops:
  7.2 13.8 %copy-start.23 = (f32[256,1152]{1,0:T(8,128)S(1)}, f32[256,1152]{1,0:T(8,128)}, u32[]{:S(2)}) copy-start(f32[256,1152]{1,0:T(8,128)} %refs_11_.1) | copy-start | bytes 3538948
  7.2 194.2 %all-gather.4.cloned.1.call-start = ((), (), s32[]{:S(2)}) async-start(), calls=%async_computation.1 | async-start | bytes 10948608 | tf_op jit(solution)/shard_map/all_gather | solution.py:1236
  9.2 212.0 %all-gather.6.cloned.1.call-start = ((), (), s32[]{:S(2)}) async-start(), calls=%async_computation.2 | async-start | bytes 10948608 | tf_op jit(solution)/shard_map/all_gather | solution.py:1236
  11.2 429.3 %reduce-scatter.2.cloned.1.call-start = ((), (), s32[]{:S(2)}) async-start(), calls=%async_computation.3 | async-start | bytes 10948608 | tf_op jit(solution)/shard_map/reduce_scatter | solution.py:1244
  20.0 8.9 %copy-start.21 = (f32[1152,288]{0,1:T(8,128)S(1)}, f32[1152,288]{0,1:T(8,128)}, u32[]{:S(2)}) copy-start(f32[1152,288]{0,1:T(8,128)} %param.34) | copy-start | bytes 3981316
  20.4 0.6 copy-start.31
  20.4 0.6 copy-start.33
  21.9 7.1 %copy-start.22 = (f32[128,1152]{1,0:T(8,128)}, f32[128,1152]{1,0:T(8,128)S(1)}, u32[]{:S(2)}) copy-start(f32[128,1152]{1,0:T(8,128)S(1)} %fusion.44.refs_6_) | copy-start | bytes 1769476
  21.9 7.2 %copy-start.18 = (f32[1152,864]{0,1:T(8,128)S(1)}, f32[1152,864]{0,1:T(8,128)}, u32[]{:S(2)}) copy-start(f32[1152,864]{0,1:T(8,128)} %param.29) | copy-start | bytes 11943940
  29.0 0.7 copy-start.25
  29.1 0.8 copy-start.27
  29.1 11.8 %copy-start.53 = (s32[128]{0:T(128)S(1)}, s32[128]{0:T(128)}, u32[]{:S(2)}) copy-start(s32[128]{0:T(128)} %param.24) | copy-start | bytes 1540
  29.1 13.3 %copy-start.52 = (f32[32]{0:T(128)S(1)}, f32[32]{0:T(128)}, u32[]{:S(2)}) copy-start(f32[32]{0:T(128)} %param.21) | copy-start | bytes 388
  29.1 13.4 %copy-start.46 = (f32[4,256,16]{1,2,0:T(8,128)S(1)}, f32[4,256,16]{1,2,0:T(8,128)}, u32[]{:S(2)}) copy-start(f32[4,256,16]{1,2,0:T(8,128)} %param.19) | copy-start | bytes 196612
  29.1 13.3 %copy-start.47 = (f32[4,256,16]{1,2,0:T(8,128)S(1)}, f32[4,256,16]{1,2,0:T(8,128)}, u32[]{:S(2)}) copy-start(f32[4,256,16]{1,2,0:T(8,128)} %param.20) | copy-start | bytes 196612
  29.1 13.5 %copy-start.24 = (f32[144,1152]{1,0:T(8,128)S(1)}, f32[144,1152]{1,0:T(8,128)}, u32[]{:S(2)}) copy-start(f32[144,1152]{1,0:T(8,128)} %refs_15_.1) | copy-start | bytes 1990660
  29.3 1.3 copy-start.20
  29.4 13.3 %copy-start.19 = (f32[1152,432]{0,1:T(8,128)S(1)}, f32[1152,432]{0,1:T(8,128)}, u32[]{:S(2)}) copy-start(f32[1152,432]{0,1:T(8,128)} %param.30) | copy-start | bytes 5971972
  42.3 120.5 %copy-start.7 = (s32[4]{0:T(128)}, s32[4]{0:T(128)S(1)}, u32[]{:S(2)}) copy-start(s32[4]{0:T(128)S(1)} %dynamic_slice.48.length_ref) | copy-start | bytes 52
  42.4 0.8 copy-start.40
  42.5 102.0 %copy-start.35 = (bf16[4,256,16]{1,2,0:T(8,128)(2,1)}, bf16[4,256,16]{1,2,0:T(8,128)(2,1)S(1)}, u32[]{:S(2)}) copy-start(bf16[4,256,16]{1,2,0:T(8,128)(2,1)S(1)} %get-tuple-element.123) | copy-start | bytes 98308
  43.6 154.2 %copy-start.38 = (f32[4,1,1,1152]{3,0,2,1:T(4,128)}, f32[4,1,1,1152]{3,0,2,1:T(4,128)S(1)}, u32[]{:S(2)}) copy-start(f32[4,1,1,1152]{3,0,2,1:T(4,128)S(1)} %copy.76) | copy-start | bytes 55300
  44.6 100.0 %copy-start.37 = (f32[16,1152]{1,0:T(8,128)S(1)}, f32[16,1152]{1,0:T(8,128)}, u32[]{:S(2)}) copy-start(f32[16,1152]{1,0:T(8,128)} %refs_10_.1) | copy-start | bytes 221188
  145.5 49.5 %copy-start = (f32[4,256,1152]{2,1,0:T(8,128)}, f32[4,256,1152]{2,1,0:T(8,128)S(1)}, u32[]{:S(2)}) copy-start(f32[4,256,1152]{2,1,0:T(8,128)S(1)} %get-tuple-element.154) | copy-start | bytes 14155780
  146.2 48.8 %copy-start.41 = (f32[4,1152]{1,0:T(4,128)}, f32[4,1152]{1,0:T(4,128)S(1)}, u32[]{:S(2)}) copy-start(f32[4,1152]{1,0:T(4,128)S(1)} %get-tuple-element.166) | copy-start | bytes 55300
  162.8 1.4 copy-start.3
  188.7 6.3 copy-start.1
  195.0 2.1 copy-start.15
  197.1 2.2 copy-start.9
  197.1 4.2 copy-start.44
  197.7 23.5 %copy-start.48 = (f32[4,256]{1,0:T(4,128)}, f32[4,256]{1,0:T(4,128)S(1)}, u32[]{:S(2)}) copy-start(f32[4,256]{1,0:T(4,128)S(1)} %add_rsqrt_fusion.1) | copy-start | bytes 12292
  201.3 19.9 %copy-start.28 = (bf16[4,256,1152]{2,1,0:T(8,128)(2,1)}, bf16[4,256,1152]{2,1,0:T(8,128)(2,1)S(1)}, u32[]{:S(2)}) copy-start(bf16[4,256,1152]{2,1,0:T(8,128)(2,1)S(1)} %add_convert_fusion.1) | copy-start | bytes 7077892
  221.2 22.9 %copy-start.10 = (f32[4,256,1152]{2,1,0:T(8,128)S(1)}, f32[4,256,1152]{2,1,0:T(8,128)}, u32[]{:S(2)}) copy-start(f32[4,256,1152]{2,1,0:T(8,128)} %copy-done.9) | copy-start | bytes 14155780
  244.1 2.2 copy-start.16
  246.3 2.7 copy-start.11
  246.9 2.0 copy-start.30
  250.3 9.5 %slice-start.2 = ((s8[4718592]{0:T(1024)(128)(4,1)}), s8[524288]{0:T(1024)(128)(4,1)S(1)}, s32[]{:S(2)}) async-start(s8[4718592]{0:T(1024)(128)(4,1)} %bitcast.142), calls=%async_computation.7 | async-start | bytes 1048576
  253.3 6.5 slice-start.3
  253.3 7.7 %copy-start.12 = (f32[1024,1152]{1,0:T(8,128)S(1)}, f32[1024,1152]{1,0:T(8,128)}, u32[]{:S(2)}) copy-start(f32[1024,1152]{1,0:T(8,128)} %get-tuple-element.156) | copy-start | bytes 14155780
  264.4 2.2 copy-start.13
  267.0 1.4 copy-start.29
  289.5 0.8 copy-start.43
  289.5 1.0 copy-start.36
  289.5 1.2 copy-start.50
  289.5 1.9 copy-start.51
  289.5 4.7 copy-start.32
  289.5 4.7 copy-start.34
  289.5 331.7 %all-gather.8.cloned.1.call-start = ((), (), s32[]{:S(2)}) async-start(), calls=%async_computation.4 | async-start | bytes 1658880 | tf_op jit(solution)/shard_map/all_gather | solution.py:1236
  299.0 27.4 %copy-start.39 = (f32[4,1,1,1152]{3,0,2,1:T(4,128)S(1)}, f32[4,1,1,1152]{3,0,2,1:T(4,128)}, u32[]{:S(2)}) copy-start(f32[4,1,1,1152]{3,0,2,1:T(4,128)} %copy-done.38) | copy-start | bytes 55300
  326.5 22.1 %copy-start.54 = (bf16[1024,4608]{1,0:T(8,128)(2,1)}, bf16[1024,4608]{1,0:T(8,128)(2,1)S(1)}, u32[]{:S(2)}) copy-start(bf16[1024,4608]{1,0:T(8,128)(2,1)S(1)} %fusion.6) | copy-start | bytes 28311556
  326.5 22.1 %copy-start.45 = (f32[4,256]{1,0:T(4,128)S(1)}, f32[4,256]{1,0:T(4,128)}, u32[]{:S(2)}) copy-start(f32[4,256]{1,0:T(4,128)} %copy-done.44) | copy-start | bytes 12292
  326.5 22.1 %copy-start.49 = (f32[4,256]{1,0:T(4,128)S(1)}, f32[4,256]{1,0:T(4,128)}, u32[]{:S(2)}) copy-start(f32[4,256]{1,0:T(4,128)} %copy-done.48) | copy-start | bytes 12292
  348.6 6.7 copy-start.14
  355.3 6.8 copy-start.42
  362.0 2.2 copy-start.17
  364.2 6.8 copy-start.2
  364.2 6.8 copy-start.8
  364.2 38.8 %slice-start = ((s8[4718592]{0:T(1024)(128)(4,1)}), s8[4194304]{0:T(1024)(128)(4,1)S(1)}, s32[]{:S(2)}) async-start(s8[4718592]{0:T(1024)(128)(4,1)} %bitcast.134), calls=%async_computation.5 | async-start | bytes 8388608
  369.6 1.4 copy-start.5
  371.0 32.0 %slice-start.1 = ((s8[4718592]{0:T(1024)(128)(4,1)}), s8[524288]{0:T(1024)(128)(4,1)S(1)}, s32[]{:S(2)}) async-start(s8[4718592]{0:T(1024)(128)(4,1)} %bitcast.134), calls=%async_computation.6 | async-start | bytes 1048576
  422.0 19.3 %copy-start.4 = (bf16[4,256,1152]{2,1,0:T(8,128)(2,1)S(1)}, bf16[4,256,1152]{2,1,0:T(8,128)(2,1)}, u32[]{:S(2)}) copy-start(bf16[4,256,1152]{2,1,0:T(8,128)(2,1)} %copy-done.3) | copy-start | bytes 7077892
  441.3 1.7 copy-start.6
  608.3 8.8 %copy-start.26 = (bf16[128,1152]{1,0:T(8,128)(2,1)S(1)}, bf16[128,1152]{1,0:T(8,128)(2,1)}, u32[]{:S(2)}) copy-start(bf16[128,1152]{1,0:T(8,128)(2,1)} %copy-done.25) | copy-start | bytes 884740
Sparse Core Ops, SparseCore 0:
  11.6 114.7 all-gather.3
  130.0 86.5 all-gather.5
  289.7 141.8 reduce-scatter.1
  440.6 18.6 all-gather.7
